TPU v7x, 256 devices: a whole 4x4x8 slice. The times are simulated.
256 devices in a mesh: tile: 64 (over x, z, core), depth: 4 (over y).
Axes of the slice: x: 4, y: 4, z: 8, core: 2. Of those that a mesh axis runs over, the one named last changes fastest.
Arguments:
- reference_image: float32 [32, 2048, 128], P('depth', 'tile'), may hold values from -120 to 120, as said below
- deformed_image: float32 [32, 2048, 128], P('depth', 'tile'), may hold values from -120 to 120, as said below
- offsets: int32 [3, 32, 2048, 128], P(None, 'depth', 'tile'), may hold values from -2 to 1, as said below
- node_ids: int32 [2, 128, 8], P(None, 'tile'), may hold values from 0 to 2047, as said below
- start_motion: float32 [3, 2048], P(None, 'tile'), may hold values from -0.6 to 0.6
Outputs:
- displacement: float32 [3, 2048], P(None, 'tile')
- misfit: float32 [3], replicated
- residual_field: float32 [32, 2048, 128], P('depth', 'tile')
Inputs may be any that keep to these rules, and one draw needn't show every extreme that they name: `node_ids`: every number from 0 to 2047 stands once; the nodes at first in-plane layers k with k // 2 = t carry the numbers t * 32 to (t + 1) * 32 - 1. `offsets`: each component is constant over each element, the blocks of 16 x 16 x 16 voxels between node layers. `reference_image`: gray values. `deformed_image`: gray values.
All inputs are finite; a program needn't handle non-finite values.
Results may differ from a plain program's by a relative error of at most 0.0055.
Values sent between devices are 32-bit elements; how exact they have to be, the bound alone decides.
No kernel may reach another device: no remote copies, remote signals or barrier semaphores. Data moves between devices by JAX's collectives and lax.ppermute only.
A program may use at most 64 MiB of HBM per device.

v0:
```python
import jax
import jax.numpy as jnp
from jax import lax
from jax.sharding import PartitionSpec as P

ELEM = 16
ITERS = 3


highest = lax.Precision.HIGHEST


def from_behind(block, axis, distance):
    devices = range(lax.axis_size(axis))
    route = [(i - distance, i) for i in devices if i - distance in devices]
    return lax.ppermute(block, axis, route)


def padded_2(shard, sides, width):
    for axis, dim in sides:
        peers, length = (lax.axis_size(axis), shard.shape[dim])
        up = [(i, (i + 1) % peers) for i in range(peers - 1)]
        down = [(j, i) for i, j in up]
        last = lax.slice_in_dim(shard, length - width, length, axis=dim)
        leading = lax.slice_in_dim(shard, 0, width, axis=dim)
        before = lax.ppermute(last, axis, up)
        after = lax.ppermute(leading, axis, down)
        shard = jnp.concatenate([before, shard, after], axis=dim)
    return shard


def hat_matrix(voxel_start, voxel_count, node_start, node_count):
    centers = (jnp.arange(voxel_count, dtype=jnp.int32) + voxel_start).astype(jnp.float32) + 0.5
    places = ((jnp.arange(node_count, dtype=jnp.int32) + node_start) * ELEM).astype(jnp.float32)
    return jnp.maximum(1.0 - jnp.abs(centers[:, None] - places[None, :]) / ELEM, 0.0)


def interpolate(node_values, weight_z, weight_x, weight_y):
    along_x = jnp.einsum("cakb,xk->caxb", node_values, weight_x, precision=highest)
    along_y = jnp.einsum("caxb,yb->caxy", along_x, weight_y, precision=highest)
    return jnp.einsum("caxy,za->czxy", along_y, weight_z, precision=highest)


def restrict(voxel_field, weight_z, weight_x, weight_y):
    over_z = jnp.einsum("czxy,za->caxy", voxel_field, weight_z, precision=highest)
    over_y = jnp.einsum("caxy,yb->caxb", over_z, weight_y, precision=highest)
    return jnp.einsum("caxb,xk->cakb", over_y, weight_x, precision=highest)


def shift_weights(offset, fraction):
    return [
        jnp.where(offset == step, 1.0 - fraction, 0.0)
        + jnp.where(offset == step - 1, fraction, 0.0)
        for step in range(-2, 3)
    ]


def warp_image(padded, off_z, off_x, off_y, motion):
    depth_len, rows_len, cols_len = motion.shape[1:]
    weights_z = shift_weights(off_z, motion[0])
    weights_x = shift_weights(off_x, motion[1])
    weights_y = shift_weights(off_y, motion[2])
    warped = jnp.zeros(motion.shape[1:], jnp.float32)
    for step_z in range(5):
        plane_sum = jnp.zeros(motion.shape[1:], jnp.float32)
        for step_x in range(5):
            line_sum = jnp.zeros(motion.shape[1:], jnp.float32)
            for step_y in range(5):
                window = padded[
                    step_z : step_z + depth_len,
                    step_x : step_x + rows_len,
                    step_y : step_y + cols_len,
                ]
                line_sum = line_sum + weights_y[step_y] * window
            plane_sum = plane_sum + weights_x[step_x] * line_sum
        warped = warped + weights_z[step_z] * plane_sum
    return warped


def gradient(padded):
    slope_z = (
        padded[:-4, 2:-2, 2:-2]
        - padded[4:, 2:-2, 2:-2]
        + 8.0 * (padded[3:-1, 2:-2, 2:-2] - padded[1:-3, 2:-2, 2:-2])
    ) / 12.0
    slope_x = (
        padded[2:-2, :-4, 2:-2]
        - padded[2:-2, 4:, 2:-2]
        + 8.0 * (padded[2:-2, 3:-1, 2:-2] - padded[2:-2, 1:-3, 2:-2])
    ) / 12.0
    slope_y = (
        padded[2:-2, 2:-2, :-4]
        - padded[2:-2, 2:-2, 4:]
        + 8.0 * (padded[2:-2, 2:-2, 3:-1] - padded[2:-2, 2:-2, 1:-3])
    ) / 12.0
    return jnp.stack([slope_z, slope_x, slope_y])


def with_upper(node_values):
    upper_nodes = from_behind(node_values[:, :, :1], "tile", -1)
    return jnp.concatenate([node_values, upper_nodes], axis=2)


def local(reference_image, deformed_image, offsets, node_ids, start_motion):
    tile_count = lax.axis_size("tile")
    depth_count = lax.axis_size("depth")
    tile_index = lax.axis_index("tile")
    depth_index = lax.axis_index("depth")
    slices, row_count, columns = reference_image.shape
    z_layers = slices * depth_count // ELEM
    x_layers = row_count // ELEM
    y_layers = columns // ELEM
    node_count = z_layers * x_layers * y_layers
    levenberg = 0.1 * ELEM**3
    full_count = float(slices * depth_count * row_count * tile_count * columns)
    slab_start = depth_index * slices
    row_start = tile_index * row_count
    weight_z = hat_matrix(slab_start, slices, 0, z_layers)
    weight_x = hat_matrix(row_start, row_count, tile_index * x_layers, x_layers + 1)
    weight_y = hat_matrix(0, columns, 0, y_layers)
    padded = padded_2(deformed_image, (("tile", 1), ("depth", 0)), 2)
    padded = jnp.pad(padded, ((0, 0), (0, 0), (2, 2)))
    local_ids = node_ids % node_count
    chooser = (
        local_ids.reshape(-1)[:, None] == jnp.arange(node_count, dtype=jnp.int32)[None, :]
    ).astype(jnp.float32)
    node_motion = jnp.einsum("ci,si->cs", start_motion, chooser, precision=highest).reshape(
        3, z_layers, x_layers, y_layers
    )
    misfits = []
    residual = jnp.zeros(reference_image.shape, jnp.float32)
    for iteration in range(ITERS):
        motion = interpolate(with_upper(node_motion), weight_z, weight_x, weight_y)
        warped = warp_image(padded, offsets[0], offsets[1], offsets[2], motion)
        extended = padded_2(warped, (("tile", 1), ("depth", 0)), 2)
        residual = warped - reference_image
        misfit_local = jnp.sum(residual * residual)
        misfit_total = lax.psum(misfit_local, ("tile", "depth"))
        slopes = gradient(jnp.pad(extended, ((0, 0), (0, 0), (2, 2))))
        node_force = restrict(slopes * residual[None], weight_z, weight_x, weight_y)
        node_stiffness = restrict(
            slopes * slopes, weight_z * weight_z, weight_x * weight_x, weight_y * weight_y
        )
        partials = lax.psum(jnp.concatenate([node_force, node_stiffness], axis=0), "depth")
        carried = from_behind(partials[:, :, -1:], "tile", 1)
        owned_partials = partials[:, :, :-1].at[:, :, :1].add(carried)
        node_force = owned_partials[:3]
        node_stiffness = owned_partials[3:]
        direction = node_force / (node_stiffness + levenberg)
        descent_local = jnp.sum(node_force * direction)
        length_local = jnp.sum(direction * direction)
        projected = jnp.sum(
            slopes * interpolate(with_upper(direction), weight_z, weight_x, weight_y), axis=0
        )
        curvature_local = jnp.sum(projected * projected)
        descent, length = lax.psum((descent_local, length_local), "tile")
        curvature = lax.psum(curvature_local, ("tile", "depth"))
        step_size = descent / (curvature + levenberg * length)
        node_motion = node_motion - step_size * direction
        misfits.append(misfit_total / full_count)
    displacement = jnp.einsum("cs,si->ci", node_motion.reshape(3, -1), chooser, precision=highest)
    return (displacement, jnp.stack(misfits), residual)


def solution(mesh):
    in_specs = (
        P("depth", "tile", None),
        P("depth", "tile", None),
        P(None, "depth", "tile", None),
        P(None, "tile", None),
        P(None, "tile"),
    )
    out_specs = (P(None, "tile"), P(), P("depth", "tile", None))
    return jax.shard_map(local, mesh=mesh, in_specs=in_specs, out_specs=out_specs, check_vma=False)
```

profile of v0, /device:TPU:1, one launch (start us, length us, event | category | flops | bytes accessed | tf_op | source)
XLA Modules:
  0.0 795.8 jit_solution(1403973607150013336)
XLA Ops:
  0.6 0.8 fusion.362
  1.4 4.9 collective-permute-start.1
  6.4 1.9 collective-permute-start.2
  8.7 1.9 collective-permute-start
  10.7 1.1 fusion.357
  11.8 1.8 collective-permute-done
  15.1 1.3 collective-permute-start.4
  16.4 4.0 collective-permute-start.3
  21.9 4.0 multiply_reduce_fusion.2
  25.9 1.9 collective-permute-start.6
  27.8 3.6 collective-permute-start.5
  31.5 0.8 collective-permute-done.5
  32.3 1.3 collective-permute-start.8
  33.6 4.2 collective-permute-start.7
  37.9 1.0 collective-permute-done.7
  42.8 14.4 %psum.105 = f32[6,2,3,8]{3,2,1,0:T(4,128)S(1)} all-reduce(f32[6,2,3,8]{3,2,1,0:T(4,128)S(1)} %pad_maximum_fusion.44), channel_id=1, replica_groups=mesh['tile'=64,'depth'=4] {'depth'}, use_global_device_ids=true, to_apply=%region_0.1 | all-reduce | flops 288 | bytes 2304 | tf_op jit(solution)/shard_map/psum | solution.py:144
  57.3 9.4 %collective-permute-start.9 = (f32[6,2,1,8]{3,2,1,0:T(1,128)S(1)}, f32[6,2,1,8]{3,2,1,0:T(1,128)S(1)}, u32[]{:S(2)}, u32[]{:S(2)}) collective-permute-start(f32[6,2,1,8]{3,2,1,0:T(1,128)S(1)} %slice.1448), channel_id=1, source_target_pairs={{0,4},{4,8},{8,12},{12,16},{16,20},{20,24},{24,28},{28,32},{32,36}... | collective-permute-start | bytes 1160 | tf_op jit(solution)/shard_map/ppermute | solution.py:16
  68.1 1.9 collective-permute-start.10
  70.0 128.4 %all-reduce.7 = (f32[]{:T(128)}, f32[]{:T(128)}) all-reduce(f32[]{:T(128)} %get-tuple-element.50, f32[]{:T(128)} %get-tuple-element.49), channel_id=1, replica_groups=mesh['tile'=64,'depth'=4] {'tile'}, use_global_device_ids=true, to_apply=%region_2.3 | all-reduce | flops 2 | bytes 16 | tf_op jit(solution)/shard_map/psum | solution.py:156
  201.2 76.2 %psum.107 = f32[]{:T(128)} all-reduce(f32[]{:T(128)} %multiply_reduce_fusion.5), channel_id=1, replica_groups=mesh['tile'=64,'depth'=4] {'tile','depth'}, use_global_device_ids=true, to_apply=%region_5.6 | all-reduce | flops 1 | bytes 8 | tf_op jit(solution)/shard_map/psum | solution.py:157
  278.7 2.5 collective-permute-start.11
  281.2 2.9 collective-permute-done.11
  285.5 3.9 multiply_reduce_fusion.1
  289.3 1.9 collective-permute-start.13
  291.3 3.6 collective-permute-start.12
  294.9 0.8 collective-permute-done.12
  295.7 1.3 collective-permute-start.15
  297.0 4.2 collective-permute-start.14
  301.2 0.8 collective-permute-done.14
  306.0 13.0 %psum.109 = f32[6,2,3,8]{3,2,1,0:T(4,128)S(1)} all-reduce(f32[6,2,3,8]{3,2,1,0:T(4,128)S(1)} %pad_maximum_fusion.45), channel_id=1, replica_groups=mesh['tile'=64,'depth'=4] {'depth'}, use_global_device_ids=true, to_apply=%region_8.9 | all-reduce | flops 288 | bytes 2304 | tf_op jit(solution)/shard_map/psum | solution.py:144
  319.0 9.1 %collective-permute-start.16 = (f32[6,2,1,8]{3,2,1,0:T(1,128)S(1)}, f32[6,2,1,8]{3,2,1,0:T(1,128)S(1)}, u32[]{:S(2)}, u32[]{:S(2)}) collective-permute-start(f32[6,2,1,8]{3,2,1,0:T(1,128)S(1)} %slice.1468), channel_id=1, source_target_pairs={{0,4},{4,8},{8,12},{12,16},{16,20},{20,24},{24,28},{28,32},{32,36}... | collective-permute-start | bytes 1160 | tf_op jit(solution)/shard_map/ppermute | solution.py:16
  329.5 1.9 collective-permute-start.17
  331.5 123.9 %all-reduce.6 = (f32[]{:T(128)}, f32[]{:T(128)}) all-reduce(f32[]{:T(128)} %get-tuple-element.48, f32[]{:T(128)} %get-tuple-element.47), channel_id=1, replica_groups=mesh['tile'=64,'depth'=4] {'tile'}, use_global_device_ids=true, to_apply=%region_10.11 | all-reduce | flops 2 | bytes 16 | tf_op jit(solution)/shard_map/psum | solution.py:156
  458.0 76.2 %psum.111 = f32[]{:T(128)} all-reduce(f32[]{:T(128)} %multiply_reduce_fusion.4), channel_id=1, replica_groups=mesh['tile'=64,'depth'=4] {'tile','depth'}, use_global_device_ids=true, to_apply=%region_13.14 | all-reduce | flops 1 | bytes 8 | tf_op jit(solution)/shard_map/psum | solution.py:157
  535.6 2.5 collective-permute-start.18
  538.1 2.9 collective-permute-done.18
  542.4 4.0 multiply_reduce_fusion
  546.3 1.9 collective-permute-start.20
  548.3 3.6 collective-permute-start.19
  552.7 1.3 collective-permute-start.22
  554.0 4.0 collective-permute-start.21
  558.0 1.0 collective-permute-done.21
  563.0 13.0 %psum.113 = f32[6,2,3,8]{3,2,1,0:T(4,128)S(1)} all-reduce(f32[6,2,3,8]{3,2,1,0:T(4,128)S(1)} %pad_maximum_fusion.46), channel_id=1, replica_groups=mesh['tile'=64,'depth'=4] {'depth'}, use_global_device_ids=true, to_apply=%region_16.17 | all-reduce | flops 288 | bytes 2304 | tf_op jit(solution)/shard_map/psum | solution.py:144
  576.0 9.1 %collective-permute-start.23 = (f32[6,2,1,8]{3,2,1,0:T(1,128)S(1)}, f32[6,2,1,8]{3,2,1,0:T(1,128)S(1)}, u32[]{:S(2)}, u32[]{:S(2)}) collective-permute-start(f32[6,2,1,8]{3,2,1,0:T(1,128)S(1)} %slice.1488), channel_id=1, source_target_pairs={{0,4},{4,8},{8,12},{12,16},{16,20},{20,24},{24,28},{28,32},{32,36}... | collective-permute-start | bytes 1160 | tf_op jit(solution)/shard_map/ppermute | solution.py:16
  586.6 1.9 collective-permute-start.24
  588.5 123.8 %all-reduce.5 = (f32[]{:T(128)}, f32[]{:T(128)}) all-reduce(f32[]{:T(128)} %get-tuple-element.46, f32[]{:T(128)} %get-tuple-element.45), channel_id=1, replica_groups=mesh['tile'=64,'depth'=4] {'tile'}, use_global_device_ids=true, to_apply=%region_18.19 | all-reduce | flops 2 | bytes 16 | tf_op jit(solution)/shard_map/psum | solution.py:156
  714.9 76.3 %all-reduce.4 = (f32[]{:T(128)}, f32[]{:T(128)}, f32[]{:T(128)}, f32[]{:T(128)}) all-reduce(f32[]{:T(128)} %multiply_reduce_fusion.3, f32[]{:T(128)} %get-tuple-element.85, f32[]{:T(128)} %get-tuple-element.82, f32[]{:T(128)} %get-tuple-element.61), channel_id=1, replica_groups=mesh['tile'=64,'depth'=4] {'tile','depth'}, use_global_device_ids=true, to_apply=%region_21.22 | all-reduce | flops 4 | bytes 32 | tf_op jit(solution)/shard_map/psum | solution.py:157
  792.6 0.8 fusion.245
  (135 shorter events, 29.6 us)
Async XLA Ops:
  0.6 7.8 copy-start
  1.4 12.9 %collective-permute-start.1 = (f32[8,2,128]{2,0,1:T(8,128)S(1)}, f32[8,2,128]{2,0,1:T(8,128)S(1)}, u32[]{:S(2)}, u32[]{:S(2)}) collective-permute-start(f32[8,2,128]{2,0,1:T(8,128)S(1)} %copy.158), channel_id=1, source_target_pairs={{0,4},{4,8},{8,12},{12,16},{16,20},{20,24},{24,28},{28,32},{32,36}... | collective-permute-start | bytes 24584 | tf_op jit(solution)/shard_map/ppermute | solution.py:26
  6.4 2.0 copy-start.3
  6.4 8.6 %collective-permute-start.2 = (f32[8,2,128]{2,0,1:T(8,128)S(1)}, f32[8,2,128]{2,0,1:T(8,128)S(1)}, u32[]{:S(2)}, u32[]{:S(2)}) collective-permute-start(f32[8,2,128]{2,0,1:T(8,128)S(1)} %copy.159), channel_id=1, source_target_pairs={{4,0},{8,4},{12,8},{16,12},{20,16},{24,20},{28,24},{32,28},{36,32}... | collective-permute-start | bytes 24584 | tf_op jit(solution)/shard_map/ppermute | solution.py:27
  8.7 4.9 collective-permute-start
  14.0 0.9 copy-start.1
  15.1 5.9 collective-permute-start.4
  16.4 5.0 collective-permute-start.3
  21.0 0.9 copy-start.2
  25.9 5.6 collective-permute-start.6
  27.8 4.4 collective-permute-start.5
  32.3 5.6 collective-permute-start.8
  33.6 5.3 collective-permute-start.7
  57.3 10.1 %collective-permute-start.9 = (f32[6,2,1,8]{3,2,1,0:T(1,128)S(1)}, f32[6,2,1,8]{3,2,1,0:T(1,128)S(1)}, u32[]{:S(2)}, u32[]{:S(2)}) collective-permute-start(f32[6,2,1,8]{3,2,1,0:T(1,128)S(1)} %slice.1448), channel_id=1, source_target_pairs={{0,4},{4,8},{8,12},{12,16},{16,20},{20,24},{24,28},{28,32},{32,36}... | collective-permute-start | bytes 1160 | tf_op jit(solution)/shard_map/ppermute | solution.py:16
  68.1 130.4 %collective-permute-start.10 = (f32[3,2,1,8]{3,2,1,0:T(1,128)S(1)}, f32[3,2,1,8]{3,2,1,0:T(1,128)S(1)}, u32[]{:S(2)}, u32[]{:S(2)}) collective-permute-start(f32[3,2,1,8]{3,2,1,0:T(1,128)S(1)} %slice.1451), channel_id=1, source_target_pairs={{4,0},{8,4},{12,8},{16,12},{20,16},{24,20},{28,24},{32,28},{36,32}... | collective-permute-start | bytes 584 | tf_op jit(solution)/shard_map/ppermute | solution.py:16
  278.7 5.5 collective-permute-start.11
  289.3 5.6 collective-permute-start.13
  291.3 4.4 collective-permute-start.12
  295.7 5.5 collective-permute-start.15
  297.0 5.0 collective-permute-start.14
  319.0 9.9 %collective-permute-start.16 = (f32[6,2,1,8]{3,2,1,0:T(1,128)S(1)}, f32[6,2,1,8]{3,2,1,0:T(1,128)S(1)}, u32[]{:S(2)}, u32[]{:S(2)}) collective-permute-start(f32[6,2,1,8]{3,2,1,0:T(1,128)S(1)} %slice.1468), channel_id=1, source_target_pairs={{0,4},{4,8},{8,12},{12,16},{16,20},{20,24},{24,28},{28,32},{32,36}... | collective-permute-start | bytes 1160 | tf_op jit(solution)/shard_map/ppermute | solution.py:16
  329.5 125.9 %collective-permute-start.17 = (f32[3,2,1,8]{3,2,1,0:T(1,128)S(1)}, f32[3,2,1,8]{3,2,1,0:T(1,128)S(1)}, u32[]{:S(2)}, u32[]{:S(2)}) collective-permute-start(f32[3,2,1,8]{3,2,1,0:T(1,128)S(1)} %slice.1471), channel_id=1, source_target_pairs={{4,0},{8,4},{12,8},{16,12},{20,16},{24,20},{28,24},{32,28},{36,32}... | collective-permute-start | bytes 584 | tf_op jit(solution)/shard_map/ppermute | solution.py:16
  535.6 5.5 collective-permute-start.18
  546.3 5.6 collective-permute-start.20
  548.3 4.4 collective-permute-start.19
  552.7 5.3 collective-permute-start.22
  554.0 5.0 collective-permute-start.21
  576.0 9.9 %collective-permute-start.23 = (f32[6,2,1,8]{3,2,1,0:T(1,128)S(1)}, f32[6,2,1,8]{3,2,1,0:T(1,128)S(1)}, u32[]{:S(2)}, u32[]{:S(2)}) collective-permute-start(f32[6,2,1,8]{3,2,1,0:T(1,128)S(1)} %slice.1488), channel_id=1, source_target_pairs={{0,4},{4,8},{8,12},{12,16},{16,20},{20,24},{24,28},{28,32},{32,36}... | collective-permute-start | bytes 1160 | tf_op jit(solution)/shard_map/ppermute | solution.py:16
  586.6 126.3 %collective-permute-start.24 = (f32[3,2,1,8]{3,2,1,0:T(1,128)S(1)}, f32[3,2,1,8]{3,2,1,0:T(1,128)S(1)}, u32[]{:S(2)}, u32[]{:S(2)}) collective-permute-start(f32[3,2,1,8]{3,2,1,0:T(1,128)S(1)} %slice.1491), channel_id=1, source_target_pairs={{4,0},{8,4},{12,8},{16,12},{20,16},{24,20},{28,24},{32,28},{36,32}... | collective-permute-start | bytes 584 | tf_op jit(solution)/shard_map/ppermute | solution.py:16
where the time goes:
time: 797 us; the launch traced here: 796 us
  blocking collectives  645 us (81%)
  starting transfers between devices  85.3 us (11%)
  other arithmetic  19.1 us (2%)
  matrix products  17.7 us (2%)
  waiting for transfers between devices  14.7 us (2%)
  between operations  9.13 us (1%)
    psum x3, blocking collectives, local(): descent, length = lax.psum((descent_local, length_local), 'tile')  376 us
    psum x3, blocking collectives, local(): curvature = lax.psum(curvature_local, ('tile', 'depth'))  229 us
    psum x3, blocking collectives, local(): lax.psum(jnp.concatenate([node_force, node_stiffness], axis=0), 'depth')  40.5 us
    ppermute x9, starting transfers between devices, from_behind(): return lax.ppermute(block, axis, route)  40.3 us
    ppermute x8, starting transfers between devices, padded_2(): before = lax.ppermute(last, axis, up)  32.3 us
  transfers between devices with their start and end apart: 25, of which 13 were waited for; matrix products, arithmetic and copies ran while one was open for 0% of the time, Pallas kernels for 0%

commit v1 on v0

v1 whole, which is shorter than its diff:
```python
import functools

import jax
import jax.numpy as jnp
import numpy as np
from jax import lax
from jax.experimental import pallas as pl
from jax.experimental.pallas import tpu as pltpu
from jax.sharding import PartitionSpec as P

ELEM = 16
ITERS = 3
SLAB = 32
ROWS = 32
LANES = 128
HALO = 24
FRAME = ROWS + 2 * HALO
GROUPS = FRAME // 8
LEVENBERG = 0.1 * ELEM**3
VOXELS = 8388608.0
F32 = jnp.float32

highest = lax.Precision.HIGHEST


def hat(centers, places):
    return np.maximum(1.0 - np.abs(centers[:, None] - places[None, :]) / ELEM, 0.0)


def constants():
    frame = np.arange(FRAME) - HALO + 0.5
    along_x = np.zeros((6, FRAME, 4, 16), np.float32)
    for tile in range(4):
        for k in range(2):
            column = hat(frame, np.array([(2 * (tile - 1) + k) * ELEM]))[:, 0]
            for ca in range(6):
                along_x[ca, :, tile, k * 6 + ca] = column
    along_y = hat(np.arange(LANES) + 0.5, (np.arange(LANES) % 8) * ELEM).astype(np.float32)
    return (
        along_x.reshape(6 * FRAME, 64),
        np.ascontiguousarray(along_y.T),
        along_y,
        along_y * along_y,
    )


def dot(left, right):
    return jnp.dot(left, right, precision=highest, preferred_element_type=F32)


def lane_ids(shape):
    return lax.broadcasted_iota(jnp.int32, shape, 1)


def row_ids(shape):
    return lax.broadcasted_iota(jnp.int32, shape, 0)


def pack_body(with_extra, halo, place, own, one, two, three, *refs):
    if with_extra:
        extra, full, low, high = refs
    else:
        full, low, high = refs
    depth = place[1]
    for step, piece in enumerate((own, one, two, three)):
        start = lax.rem(depth + step, 4) * 8
        block = piece[...]
        full[pl.ds(start, 8)] = block
        low[pl.ds(start, 8)] = block[:, :halo]
        high[pl.ds(start, 8)] = block[:, ROWS - halo :]
    if with_extra:
        low[SLAB] = extra[...]
        high[SLAB] = extra[...]


def pack(place, pieces, halo, extra=None):
    planes = SLAB + (extra is not None)
    shapes = [
        jax.ShapeDtypeStruct((SLAB, ROWS, LANES), F32),
        jax.ShapeDtypeStruct((planes, halo, LANES), F32),
        jax.ShapeDtypeStruct((planes, halo, LANES), F32),
    ]
    vmem = pl.BlockSpec(memory_space=pltpu.VMEM)
    args = [place, *pieces] + ([extra] if extra is not None else [])
    return pl.pallas_call(
        functools.partial(pack_body, extra is not None, halo),
        out_shape=shapes,
        in_specs=[pl.BlockSpec(memory_space=pltpu.SMEM)] + [vmem] * (len(args) - 1),
        out_specs=[vmem] * 3,
        cost_estimate=pl.CostEstimate(flops=0, bytes_accessed=2000000, transcendentals=0),
        name="pack",
    )(*args)


def corner_body(tiles, place, full, left, right, extra, cor, source, shifted, table, chunk, sems):
    tile = place[0]
    zero = jnp.zeros((2, FRAME + 16, LANES), F32)
    source[0:2] = zero
    source[SLAB + 2 : SLAB + 4] = zero
    edge = jnp.zeros((SLAB, 8, LANES), F32)
    source[2 : SLAB + 2, 0:8] = edge
    source[2 : SLAB + 2, 8 + FRAME : 16 + FRAME] = edge
    source[2 : SLAB + 2, 8 : 8 + HALO] = left[0:SLAB]
    source[2 : SLAB + 2, 8 + HALO : 8 + HALO + ROWS] = full[...]
    source[2 : SLAB + 2, 8 + HALO + ROWS : 8 + FRAME] = right[0:SLAB]
    sides = ((left, 0), (left, 1), (extra, 0), (extra, 1), (right, 0), (right, 1))
    for ex, (side, which) in enumerate(sides):
        for e in range(2):
            for c in range(3):
                at = e * 6 + c * 2 + which
                row = side[at : at + 1] if side is extra else side[SLAB, at : at + 1]
                place_at = (e * 6 + ex) * 3 + c
                table[place_at : place_at + 1] = row

    shape = (8, LANES)
    lanes = lane_ids(shape)

    def group(v, carry):
        ex = (v + 1) // 2
        outside = ((tile == 0) & (v < 3)) | ((tile == tiles - 1) & (v >= 7))
        inside = jnp.where(outside, 0.0, 1.0).astype(F32)
        for e in range(2):
            offs = [
                jnp.broadcast_to(table[pl.ds((e * 6 + ex) * 3 + c, 1)], shape) for c in range(3)
            ]
            base = lanes + offs[2].astype(jnp.int32)
            picks = []
            for s in range(2):
                at = base + s
                good = jnp.where((at >= 0) & (at < LANES), inside, 0.0)
                picks.append((jnp.clip(at, 0, LANES - 1), good))
            for p in range(20):
                for half in range(2):
                    block = source[16 * e + p, pl.ds(8 * v + 6 + 4 * half, 8)]
                    for s in range(2):
                        index, good = picks[s]
                        taken = jnp.take_along_axis(block, index, axis=1, mode="promise_in_bounds")
                        shifted[s, p, 4 * half : 4 * half + 8] = taken * good
            is_x = [offs[1] == float(o) for o in (-2, -1, 0)]
            is_z = [offs[0] == float(o) for o in (-2, -1, 0)]
            window = []
            for p in range(20):
                corners = []
                for sx in range(2):
                    for sy in range(2):
                        rows = [shifted[sy, p, sx + o : sx + o + 8] for o in range(4)]
                        corners.append(
                            jnp.where(
                                is_x[0],
                                rows[0],
                                jnp.where(is_x[1], rows[1], jnp.where(is_x[2], rows[2], rows[3])),
                            )
                        )
                window.append(corners)
                if p >= 3:
                    c00, c01, c10, c11 = [
                        jnp.where(
                            is_z[0],
                            window[p - 3][n],
                            jnp.where(
                                is_z[1],
                                window[p - 2][n],
                                jnp.where(is_z[2], window[p - 1][n], window[p][n]),
                            ),
                        )
                        for n in range(4)
                    ]
                    chunk[v, e, p - 3, 0] = c00
                    chunk[v, e, p - 3, 1] = c01 - c00
                    chunk[v, e, p - 3, 2] = c10 - c00
                    chunk[v, e, p - 3, 3] = (c11 - c10) - (c01 - c00)
        pltpu.make_async_copy(chunk.at[v], cor.at[v], sems.at[v]).start()
        return carry

    lax.fori_loop(0, GROUPS, group, 0)
    for v in range(GROUPS):
        pltpu.make_async_copy(chunk.at[v], cor.at[v], sems.at[v]).wait()


def corner_images(tiles, place, full, left, right, extra):
    vmem = pl.BlockSpec(memory_space=pltpu.VMEM)
    shape = (GROUPS, 2, 17, 4, 8, LANES)
    return pl.pallas_call(
        functools.partial(corner_body, tiles),
        out_shape=jax.ShapeDtypeStruct(shape, F32),
        in_specs=[pl.BlockSpec(memory_space=pltpu.SMEM)] + [vmem] * 4,
        out_specs=pl.BlockSpec(memory_space=pl.ANY),
        scratch_shapes=[
            pltpu.VMEM((SLAB + 4, FRAME + 16, LANES), F32),
            pltpu.VMEM((2, 20, 16, LANES), F32),
            pltpu.VMEM((40, LANES), F32),
            pltpu.VMEM(shape, F32),
            pltpu.SemaphoreType.DMA((GROUPS,)),
        ],
        cost_estimate=pl.CostEstimate(flops=10000000, bytes_accessed=9000000, transcendentals=0),
        name="corners",
        compiler_params=pltpu.CompilerParams(vmem_limit_bytes=48 * 2**20),
    )(place, full, left, right, extra)


def updated_motion(motion, received, tile, tiles, padded):
    padded[...] = jnp.zeros_like(padded)
    padded[8 : 8 + tiles] = received[...]
    total = jnp.sum(received[...], axis=0, keepdims=True)
    descent = total[:, 96:97]
    length = total[:, 97:98]
    curvature = total[:, 98:99]
    step = descent / (curvature + LEVENBERG * length)
    near = padded[pl.ds(7 + tile, 8)]
    return motion[...] - step * near


def iteration_body(tiles, first, last, place, *refs):
    refs = list(refs)
    motion = refs.pop(0)
    received = None if first else refs.pop(0)
    ref_left, ref_own, ref_right, cor, along_x, along_y, over_y, over_y2 = refs[:8]
    refs = refs[8:]
    block_out, motion_out = refs[:2]
    refs = refs[2:]
    residual_out = refs.pop(0) if last else None
    cors, wide, warped, slopes, layers, rows_f, rows_s, padded = refs[:8]
    refs = refs[8:]
    residuals = refs.pop(0) if last else None
    sems = refs.pop(0)

    for v in range(GROUPS):
        pltpu.make_async_copy(cor.at[v], cors.at[v], sems.at[v]).start()

    tile = place[0]
    low_flag = jnp.where(tile > 0, 1.0, 0.0).astype(F32)
    high_flag = jnp.where(tile < tiles - 1, 1.0, 0.0).astype(F32)
    now = motion[...] if first else updated_motion(motion, received, tile, tiles, padded)
    motion_out[...] = now
    shape16 = (16, LANES)
    pick = (lane_ids(shape16) // 8 == row_ids(shape16)) & (row_ids(shape16) < 12)
    spread = jnp.concatenate(
        [jnp.where(pick, jnp.broadcast_to(now[n : n + 1], shape16), 0.0) for n in range(4)], axis=0
    )
    wide[...] = dot(along_x[...], dot(spread, along_y[...]))

    zero = jnp.zeros((2, FRAME, LANES), F32)
    warped[0:2] = zero
    warped[SLAB + 2 : SLAB + 4] = zero

    def warp(v, carry):
        pltpu.make_async_copy(cor.at[v], cors.at[v], sems.at[v]).wait()
        at = pl.ds(pl.multiple_of(8 * v, 8), 8)
        near = [wide[pl.ds(pl.multiple_of(2 * c * FRAME + 8 * v, 8), 8)] for c in range(3)]
        far = [wide[pl.ds(pl.multiple_of((2 * c + 1) * FRAME + 8 * v, 8), 8)] for c in range(3)]
        for e in range(2):
            if e == 0:
                move = [n + (f - n) * (1.0 / 32) for n, f in zip(near, far)]
                gain = [(f - n) * (1.0 / 16) for n, f in zip(near, far)]
            else:
                move = [f * (31.0 / 32) for f in far]
                gain = [f * (-1.0 / 16) for f in far]
            plane = [cors[v, e, 0, n] for n in range(4)]
            for j in range(16):
                above = [cors[v, e, j + 1, n] for n in range(4)]
                mz, mx, my = move
                here = (plane[0] + my * plane[1]) + mx * (plane[2] + my * plane[3])
                there = (above[0] + my * above[1]) + mx * (above[2] + my * above[3])
                warped[2 + 16 * e + j, at] = here + mz * (there - here)
                plane = above
                if j < 15:
                    move = [m + g for m, g in zip(move, gain)]
        return carry

    lax.fori_loop(0, GROUPS, warp, 0)

    shape = (8, LANES)
    lanes = lane_ids(shape)
    ahead_1 = jnp.where(lanes < LANES - 1, 8.0, 0.0)
    behind_1 = jnp.where(lanes > 0, 8.0, 0.0)
    ahead_2 = jnp.where(lanes < LANES - 2, 1.0, 0.0)
    behind_2 = jnp.where(lanes > 1, 1.0, 0.0)
    zeros = jnp.zeros(shape, F32)

    def slope_group(v, target, target_start, own, misfit):
        at = pl.ds(pl.multiple_of(8 * v, 8), 8)
        row = pl.multiple_of(8 * (v - target_start), 8)
        planes = [warped[n, at] for n in range(4)]
        for e in range(2):
            first_sum = [zeros] * 3
            second_sum = [zeros] * 3
            squares_0 = [zeros] * 3
            squares_1 = [zeros] * 3
            for j in range(16):
                z = 16 * e + j
                planes.append(warped[z + 4, at])
                mid = planes[2]
                slope_z = 8.0 * (planes[3] - planes[1]) - (planes[4] - planes[0])
                planes = planes[1:]
                up_1 = warped[z + 2, pl.ds(8 * v + 1, 8)]
                up_2 = warped[z + 2, pl.ds(8 * v + 2, 8)]
                down_1 = warped[z + 2, pl.ds(8 * v - 1, 8)]
                down_2 = warped[z + 2, pl.ds(8 * v - 2, 8)]
                slope_x = 8.0 * (up_1 - down_1) - (up_2 - down_2)
                slope_y = (
                    ahead_1 * pltpu.roll(mid, LANES - 1, 1) - behind_1 * pltpu.roll(mid, 1, 1)
                ) - (ahead_2 * pltpu.roll(mid, LANES - 2, 1) - behind_2 * pltpu.roll(mid, 2, 1))
                residual = mid - target[z, pl.ds(row, 8)]
                three = (slope_z, slope_x, slope_y)
                if own:
                    misfit = misfit + residual * residual
                    for c in range(3):
                        slopes[c, z, pl.ds(row, 8)] = three[c]
                    if last:
                        residuals[z, pl.ds(row, 8)] = residual
                weight = 1.0 - (j + 0.5) / 16.0
                for c in range(3):
                    first_sum[c] = first_sum[c] + three[c] * residual
                    second_sum[c] = second_sum[c] + first_sum[c]
                    square = three[c] * three[c]
                    squares_0[c] = squares_0[c] + (weight * weight) * square
                    if e == 0:
                        squares_1[c] = squares_1[c] + ((1.0 - weight) ** 2) * square
            for c in range(3):
                falling = (second_sum[c] - 0.5 * first_sum[c]) * (1.0 / 16)
                if e == 0:
                    layers[v - 1, 2 * c] = falling
                    layers[v - 1, 2 * c + 1] = first_sum[c] - falling
                    layers[v - 1, 6 + 2 * c] = squares_0[c]
                    layers[v - 1, 6 + 2 * c + 1] = squares_1[c]
                else:
                    layers[v - 1, 2 * c + 1] += falling
                    layers[v - 1, 6 + 2 * c + 1] += squares_0[c]
        return misfit

    lax.fori_loop(1, 3, lambda v, m: slope_group(v, ref_left, 1, False, m), zeros)
    misfit = lax.fori_loop(3, 7, lambda v, m: slope_group(v, ref_own, 3, True, m), zeros)
    lax.fori_loop(7, 9, lambda v, m: slope_group(v, ref_right, 7, False, m), zeros)

    rows_f[...] = jnp.zeros_like(rows_f)
    rows_s[...] = jnp.zeros_like(rows_s)
    rows8 = row_ids((8, 1)).astype(F32)
    for k in range(3):
        sums = [zeros] * 12
        for v in range(1 + 2 * k, 5 + 2 * k):
            weight = 1.0 - jnp.abs((8 * v - HALO - ELEM * k) + 0.5 + rows8) * (1.0 / ELEM)
            square = weight * weight
            if v < 3:
                weight, square = weight * low_flag, square * low_flag
            if v >= 7:
                weight, square = weight * high_flag, square * high_flag
            for n in range(12):
                sums[n] = sums[n] + (weight if n < 6 else square) * layers[v - 1, n]
        for n in range(6):
            at = k * 6 + n
            rows_f[at : at + 1] = jnp.sum(sums[n], axis=0, keepdims=True)
            rows_s[at : at + 1] = jnp.sum(sums[6 + n], axis=0, keepdims=True)
    force = dot(rows_f[...], over_y[...]) * (1.0 / 12)
    stiffness = dot(rows_s[...], over_y2[...]) * (1.0 / 144)
    shape24 = (24, LANES)
    rows24 = row_ids(shape24)
    lanes24 = lane_ids(shape24)
    direction = force / (stiffness + LEVENBERG)
    direction = jnp.where(rows24 < 12, direction, direction * high_flag)
    held = jnp.where(lanes24 < 8, direction, 0.0)
    owned = jnp.where(rows24 < 12, held, 0.0)
    descent = jnp.sum(force * owned)
    length = jnp.sum(owned * owned)
    rows_f[...] = dot(held, along_y[...])
    curved = zeros
    for v in range(3, 7):
        k = (v - 3) // 2
        share = (8.0 * ((v - 3) % 2) + 0.5 + rows8) * (1.0 / ELEM)
        field = []
        for n in range(6):
            near = rows_f[k * 6 + n : k * 6 + n + 1]
            far = rows_f[k * 6 + 6 + n : k * 6 + 7 + n]
            field.append(near + share * (far - near))
        row = 8 * (v - 3)
        for e in range(2):
            if e == 0:
                move = [field[2 * c] + (field[2 * c + 1] - field[2 * c]) * (1.0 / 32) for c in range(3)]
                gain = [(field[2 * c + 1] - field[2 * c]) * (1.0 / 16) for c in range(3)]
            else:
                move = [field[2 * c + 1] * (31.0 / 32) for c in range(3)]
                gain = [field[2 * c + 1] * (-1.0 / 16) for c in range(3)]
            for j in range(16):
                three = [slopes[c, 16 * e + j, row : row + 8] for c in range(3)]
                projected = (three[0] * move[0] + three[1] * move[1]) + three[2] * move[2]
                curved = curved + projected * projected
                if j < 15:
                    move = [m + g for m, g in zip(move, gain)]
    curvature = jnp.sum(curved) * (1.0 / 144)
    misfit = jnp.sum(misfit)
    line = jnp.sum(jnp.where(pick, direction[0:16], 0.0), axis=0, keepdims=True)
    line_lanes = lane_ids((1, LANES))
    for at, value in ((96, descent), (97, length), (98, curvature), (99, misfit)):
        line = jnp.where(line_lanes == at, value, line)
    block_out[...] = jnp.broadcast_to(line, (tiles, LANES))
    if last:
        residual_out[...] = residuals[pl.ds(place[1] * 8, 8)]


def iteration(tiles, first, last, place, motion, received, targets, cor, tables):
    vmem = pl.BlockSpec(memory_space=pltpu.VMEM)
    args = [place, motion] + ([] if first else [received]) + [*targets, cor, *tables]
    in_specs = [pl.BlockSpec(memory_space=pltpu.SMEM)] + [vmem] * (len(args) - 1)
    in_specs[-5] = pl.BlockSpec(memory_space=pl.ANY)
    shapes = [
        jax.ShapeDtypeStruct((tiles, LANES), F32),
        jax.ShapeDtypeStruct((8, LANES), F32),
    ]
    scratch = [
        pltpu.VMEM((GROUPS, 2, 17, 4, 8, LANES), F32),
        pltpu.VMEM((6 * FRAME, LANES), F32),
        pltpu.VMEM((SLAB + 4, FRAME, LANES), F32),
        pltpu.VMEM((3, SLAB, ROWS, LANES), F32),
        pltpu.VMEM((8, 12, 8, LANES), F32),
        pltpu.VMEM((24, LANES), F32),
        pltpu.VMEM((24, LANES), F32),
        pltpu.VMEM((tiles + 24, LANES), F32),
    ]
    if last:
        shapes.append(jax.ShapeDtypeStruct((8, ROWS, LANES), F32))
        scratch.append(pltpu.VMEM((SLAB, ROWS, LANES), F32))
    scratch.append(pltpu.SemaphoreType.DMA((GROUPS,)))
    return pl.pallas_call(
        functools.partial(iteration_body, tiles, first, last),
        out_shape=shapes,
        in_specs=in_specs,
        out_specs=[vmem] * len(shapes),
        scratch_shapes=scratch,
        cost_estimate=pl.CostEstimate(flops=20000000, bytes_accessed=9000000, transcendentals=0),
        name="iteration",
        compiler_params=pltpu.CompilerParams(vmem_limit_bytes=48 * 2**20),
    )(*args)


def finish_body(tiles, place, motion, got_1, got_2, got_3, ids, displacement, misfits, padded):
    now = updated_motion(motion, got_3, place[0], tiles, padded)
    shape = (8, LANES)
    component = (lane_ids(shape) // 16) % 3
    mine = jnp.where(component == row_ids(shape), jnp.broadcast_to(now[1:2], shape), 0.0)
    mine = jnp.where(lane_ids(shape) < 96, mine, 0.0)
    chooser = jnp.where(ids[...] == lane_ids((LANES, LANES)), 1.0, 0.0)
    placed = dot(mine, chooser)
    displacement[...] = placed[0:3, 0:32]
    for n, got in enumerate((got_1, got_2, got_3)):
        total = jnp.sum(got[...], axis=0, keepdims=True)
        misfits[:, n : n + 1] = total[:, 99:100] * (1.0 / VOXELS)


def finish(tiles, place, motion, got, ids):
    vmem = pl.BlockSpec(memory_space=pltpu.VMEM)
    return pl.pallas_call(
        functools.partial(finish_body, tiles),
        out_shape=[jax.ShapeDtypeStruct((3, 32), F32), jax.ShapeDtypeStruct((1, 3), F32)],
        in_specs=[pl.BlockSpec(memory_space=pltpu.SMEM)] + [vmem] * 5,
        out_specs=[vmem] * 2,
        scratch_shapes=[pltpu.VMEM((tiles + 24, LANES), F32)],
        name="finish",
    )(place, motion, *got, ids)


def from_behind(block, axis, distance):
    devices = range(lax.axis_size(axis))
    return lax.ppermute(block, axis, [(i - distance, i) for i in devices if i - distance in devices])


def ring(block, distance):
    peers = lax.axis_size("depth")
    return lax.ppermute(block, "depth", [((i + distance) % peers, i) for i in range(peers)])


def local(reference_image, deformed_image, offsets, node_ids, start_motion):
    tiles = lax.axis_size("tile")
    tile = lax.axis_index("tile")
    depth = lax.axis_index("depth")
    place = jnp.stack([tile, depth]).astype(jnp.int32)
    tables = [jnp.asarray(table) for table in constants()]

    deformed = [deformed_image] + [ring(deformed_image, n) for n in (1, 2, 3)]
    targets = [reference_image] + [ring(reference_image, n) for n in (1, 2, 3)]

    mine = offsets[:, 0, ::ELEM, :].astype(F32).reshape(6, LANES)
    other = ring(mine, 2)
    upper = depth >= 2
    shifts = jnp.concatenate([jnp.where(upper, other, mine), jnp.where(upper, mine, other)], axis=0)

    local_ids = jnp.transpose(node_ids % 32, (1, 0, 2))
    id_line = jnp.broadcast_to(local_ids[:, None], (2, 3, 2, 8)).reshape(96)
    id_line = jnp.concatenate([id_line, jnp.full((32,), -1, jnp.int32)])
    chooser = (id_line[:, None] == jnp.arange(32, dtype=jnp.int32)[None, :]).astype(F32)
    part = (jnp.arange(LANES, dtype=jnp.int32) // 16) % 3
    line = jnp.sum(chooser * jnp.take(start_motion, part, axis=0), axis=1)[None]
    beyond = from_behind(line, "tile", -2)

    extra = jnp.concatenate([shifts, line, jnp.zeros((HALO - 13, LANES), F32)], axis=0)
    full, low, high = pack(place, deformed, HALO, extra)
    left = from_behind(high, "tile", 1)
    right = from_behind(low, "tile", -1)
    motion = jnp.concatenate(
        [left[SLAB, 12:13], line, right[SLAB, 12:13], beyond, jnp.zeros((4, LANES), F32)], axis=0
    )
    cor = corner_images(tiles, place, full, left, right, extra)

    target_own, target_low, target_high = pack(place, targets, ELEM)
    target_left = from_behind(target_high, "tile", 1)
    target_right = from_behind(target_low, "tile", -1)
    targets = (target_left, target_own, target_right)

    received = None
    got = []
    for number in range(ITERS):
        last = number == ITERS - 1
        outs = iteration(tiles, number == 0, last, place, motion, received, targets, cor, tables)
        block, motion = outs[:2]
        received = lax.all_to_all(block, "tile", 0, 0, tiled=True)
        got.append(received)
    displacement, misfits = finish(tiles, place, motion, got, id_line[:, None])
    return displacement, misfits.reshape(3), outs[2]


def solution(mesh):
    in_specs = (
        P("depth", "tile", None),
        P("depth", "tile", None),
        P(None, "depth", "tile", None),
        P(None, "tile", None),
        P(None, "tile"),
    )
    out_specs = (P(None, "tile"), P(), P("depth", "tile", None))
    return jax.shard_map(local, mesh=mesh, in_specs=in_specs, out_specs=out_specs, check_vma=False)
```

time: 797 us -> 124 us (0.16)
  blocking collectives: 645 us -> 34.7 us
  starting transfers between devices: 85.3 us -> 27.9 us
  Pallas kernels: 0 us -> 31.6 us
  matrix products: 17.7 us -> 0 us
  other arithmetic: 19.1 us -> 2.2 us
  between operations: 9.13 us -> 0.94 us
    psum x9 -> x0, blocking collectives: 645 us -> none  [the longest x3 376 us: local(): descent, length = lax.psum((descent_local, length_local), 'tile')]
    ppermute x25 -> x12, starting transfers between devices: 85.3 us -> 23.2 us  [the longest x5 14.3 us: from_behind(): lax.ppermute(block, axis, [(i - distance, i) for i in devices if i - dist...]
    all_to_all x0 -> x2, blocking collectives: none -> 34.7 us  [local(): received = lax.all_to_all(block, 'tile', 0, 0, tiled=True)]
    pallas_call x0 -> x7, Pallas kernels: none -> 31.6 us  [the longest x3 19.5 us: iteration(): pl.pallas_call(functools.partial(iteration_body, tiles, first, last), out...]
    dot_general x38 -> x0, matrix products: 17.7 us -> none  [the longest x6 3.83 us: interpolate(): return jnp.einsum('caxy,za->czxy', along_y, weight_z, precision=highest)]
    reduce_sum x9 -> x1, other arithmetic: 15.7 us -> 0.18 us  [local(): line = jnp.sum(chooser * jnp.take(start_motion, part, axis=0), axis=1)[None]]
    all_to_all x0 -> x1, waiting for transfers between devices: none -> 8.66 us  [local(): received = lax.all_to_all(block, 'tile', 0, 0, tiled=True)]
  transfers between devices with their start and end apart: 25 -> 13, of which waited for: 13 -> 6; matrix products, arithmetic and copies ran while one was open for 0% -> 4% of each run, Pallas kernels for 0% -> 6%
where the time goes in v1:
time: 124 us
  blocking collectives  34.7 us (28%)
  Pallas kernels  31.6 us (25%)
  starting transfers between devices  27.9 us (22%)
  waiting for transfers between devices  18 us (15%)
  local copies, waits for them, and re-layouts  8.16 us (7%)
  other arithmetic  2.2 us (2%)
    all_to_all x2, blocking collectives, local(): received = lax.all_to_all(block, 'tile', 0, 0, tiled=True)  34.7 us
    pallas_call x3, Pallas kernels, iteration(): pl.pallas_call(functools.partial(iteration_body, tiles, first, last), out...  19.5 us
    ppermute x5, starting transfers between devices, from_behind(): lax.ppermute(block, axis, [(i - distance, i) for i in devices if i - dist...  14.3 us
    ppermute x7, waiting for transfers between devices, ring(): lax.ppermute(block, 'depth', [((i + distance) % peers, i) for i in range(...  9.34 us
    ppermute x7, starting transfers between devices, ring(): lax.ppermute(block, 'depth', [((i + distance) % peers, i) for i in range(...  8.86 us
    all_to_all x1, waiting for transfers between devices, local(): received = lax.all_to_all(block, 'tile', 0, 0, tiled=True)  8.66 us
    pallas_call x1, Pallas kernels, corner_images(): pl.pallas_call(functools.partial(corner_body, tiles), out_shape=jax.Shape...  5.77 us
    unnamed x38, local copies, waits for them, and re-layouts  5.09 us
  transfers between devices with their start and end apart: 13, of which 6 were waited for; matrix products, arithmetic and copies ran while one was open for 4% of the time, Pallas kernels for 6%

profile of v1, /device:TPU:1, one launch (start us, length us, event | category | flops | bytes accessed | tf_op | source)
XLA Modules:
  0.0 123.5 jit_solution(5335986243824641760)
XLA Ops:
  0.6 0.0 copy-start
  0.7 0.0 copy-start.3
  0.7 0.0 copy-start.4
  0.7 3.6 %collective-permute-start = (f32[8,32,128]{2,1,0:T(8,128)}, f32[8,32,128]{2,1,0:T(8,128)S(1)}, u32[]{:S(2)}, u32[]{:S(2)}) collective-permute-start(f32[8,32,128]{2,1,0:T(8,128)} %own.2), channel_id=1, source_target_pairs={{1,0},{2,1},{3,2},{0,3},{5,4},{6,5},{7,6},{4,7},{9,8},{10,9},{11,1... | collective-permute-start | bytes 393224 | tf_op jit(solution)/shard_map/ppermute | solution.py:467
  4.3 0.3 collective-permute-start.1
  4.7 0.7 collective-permute-start.2
  5.4 1.5 %slice.9 = s32[3,1,2,128]{3,2,1,0:T(2,128)S(1)} slice(s32[3,8,32,128]{3,2,1,0:T(8,128)} %param.11), slice={[0:3:1], [0:1:1], [0:32:16], [0:128:1]} | slice | bytes 6144 | tf_op jit(solution)/shard_map/slice | solution.py:480
  6.9 2.0 %collective-permute-start.3 = (f32[6,128]{1,0:T(8,128)S(1)}, f32[6,128]{1,0:T(8,128)S(1)}, u32[]{:S(2)}, u32[]{:S(2)}) collective-permute-start(f32[6,128]{1,0:T(8,128)S(1)} %convert_element_type.9), channel_id=1, source_target_pairs={{2,0},{3,1},{0,2},{1,3},{6,4},{7,5},{4,6},{5,7},{10,8},{11,9},{8,1... | collective-permute-start | bytes 9224 | tf_op jit(solution)/shard_map/ppermute | solution.py:467
  8.9 0.7 fusion
  9.6 0.1 reshape.89
  9.7 0.6 gather_fusion
  10.4 0.2 select_reduce_fusion
  10.6 0.6 pad_add_fusion.place
  11.2 0.1 pad.4.clone
  11.2 1.7 %collective-permute-done.3 = f32[6,128]{1,0:T(8,128)S(1)} collective-permute-done((f32[6,128]{1,0:T(8,128)S(1)}, f32[6,128]{1,0:T(8,128)S(1)}, u32[]{:S(2)}, u32[]{:S(2)}) %collective-permute-start.3) | collective-permute-done | bytes 3104 | tf_op jit(solution)/shard_map/ppermute | solution.py:467
  13.0 0.7 maximum_maximum_fusion.refs_0_.extra
  13.7 0.5 collective-permute-done.2.three
  14.2 0.1 copy-done.12
  14.3 0.0 copy-done.13
  14.4 0.7 copy-done.14
  15.0 2.3 %pack.2 = (f32[32,32,128]{2,1,0:T(8,128)}, f32[33,24,128]{2,1,0:T(8,128)}, f32[33,24,128]{2,1,0:T(8,128)}) custom-call(s32[2]{0:T(128)} %pad_add_fusion.place, f32[8,32,128]{2,1,0:T(8,128)} %own.2, f32[8,32,128]{2,1,0:T(8,128)} %copy-done.12, f32[8,32,128]{2,1,0:T(8,128)} %copy-done.13, f32[8,32,128]{2,1,0:T(8,128)} %copy-done.14, ...), custom_call_target="tpu_custom_call" | custom-call | bytes 2000000 | tf_op jit(solution)/shard_map/pack/pallas_call | solution.py:85
  17.3 3.8 %collective-permute-start.5 = (f32[33,24,128]{2,1,0:T(8,128)}, f32[33,24,128]{2,1,0:T(8,128)S(1)}, u32[]{:S(2)}, u32[]{:S(2)}) collective-permute-start(f32[33,24,128]{2,1,0:T(8,128)} %get-tuple-element.19), channel_id=1, source_target_pairs={{4,0},{8,4},{12,8},{16,12},{20,16},{24,20},{28,24},{32,28},{36,32}... | collective-permute-start | bytes 1216520 | tf_op jit(solution)/shard_map/ppermute | solution.py:462
  21.1 3.4 %collective-permute-start.4 = (f32[33,24,128]{2,1,0:T(8,128)}, f32[33,24,128]{2,1,0:T(8,128)S(1)}, u32[]{:S(2)}, u32[]{:S(2)}) collective-permute-start(f32[33,24,128]{2,1,0:T(8,128)} %get-tuple-element.18), channel_id=1, source_target_pairs={{0,4},{4,8},{8,12},{12,16},{16,20},{20,24},{24,28},{28,32},{32,36}... | collective-permute-start | bytes 1216520 | tf_op jit(solution)/shard_map/ppermute | solution.py:462
  24.5 0.8 collective-permute-start.7
  25.3 1.4 %collective-permute-start.8 = (f32[8,32,128]{2,1,0:T(8,128)}, f32[8,32,128]{2,1,0:T(8,128)S(1)}, u32[]{:S(2)}, u32[]{:S(2)}) collective-permute-start(f32[8,32,128]{2,1,0:T(8,128)} %own.3), channel_id=1, source_target_pairs={{2,0},{3,1},{0,2},{1,3},{6,4},{7,5},{4,6},{5,7},{10,8},{11,9},{8,1... | collective-permute-start | bytes 393224 | tf_op jit(solution)/shard_map/ppermute | solution.py:467
  26.7 3.6 %collective-permute-done.7.one = f32[8,32,128]{2,1,0:T(8,128)S(1)} collective-permute-done((f32[8,32,128]{2,1,0:T(8,128)}, f32[8,32,128]{2,1,0:T(8,128)S(1)}, u32[]{:S(2)}, u32[]{:S(2)}) %collective-permute-start.7) | collective-permute-done | bytes 131104 | tf_op jit(solution)/shard_map/ppermute | solution.py:467
  30.3 1.3 %collective-permute-start.6 = (f32[1,128]{1,0:T(1,128)S(1)}, f32[1,128]{1,0:T(1,128)S(1)}, u32[]{:S(2)}, u32[]{:S(2)}) collective-permute-start(f32[1,128]{1,0:T(1,128)S(1)} %bitcast.34), channel_id=1, source_target_pairs={{8,0},{12,4},{16,8},{20,12},{24,16},{28,20},{32,24},{36,28},{40,32... | collective-permute-start | bytes 1544 | tf_op jit(solution)/shard_map/ppermute | solution.py:462
  31.6 0.7 collective-permute-done.8.two
  32.2 2.8 %collective-permute-done.9.three = f32[8,32,128]{2,1,0:T(8,128)S(1)} collective-permute-done((f32[8,32,128]{2,1,0:T(8,128)}, f32[8,32,128]{2,1,0:T(8,128)S(1)}, u32[]{:S(2)}, u32[]{:S(2)}) %collective-permute-start.9) | collective-permute-done | bytes 131104 | tf_op jit(solution)/shard_map/ppermute | solution.py:467
  35.1 0.7 copy-done.17
  35.7 2.2 %pack.3 = (f32[32,32,128]{2,1,0:T(8,128)}, f32[32,16,128]{2,1,0:T(8,128)}, f32[32,16,128]{2,1,0:T(8,128)}) custom-call(s32[2]{0:T(128)} %pad_add_fusion.place, f32[8,32,128]{2,1,0:T(8,128)} %own.3, f32[8,32,128]{2,1,0:T(8,128)} %copy-done.15, f32[8,32,128]{2,1,0:T(8,128)} %copy-done.16, f32[8,32,128]{2,1,0:T(8,128)} %copy-done.17), custom_call_target="tpu_custom_call" | custom-call | bytes 2000000 | tf_op jit(solution)/shard_map/pack/pallas_call | solution.py:85
  37.9 3.9 %collective-permute-start.10 = (f32[32,16,128]{2,1,0:T(8,128)}, f32[32,16,128]{2,1,0:T(8,128)S(1)}, u32[]{:S(2)}, u32[]{:S(2)}) collective-permute-start(f32[32,16,128]{2,1,0:T(8,128)} %get-tuple-element.20), channel_id=1, source_target_pairs={{0,4},{4,8},{8,12},{12,16},{16,20},{20,24},{24,28},{28,32},{32,36}... | collective-permute-start | bytes 786440 | tf_op jit(solution)/shard_map/ppermute | solution.py:462
  41.8 1.9 %collective-permute-start.11 = (f32[32,16,128]{2,1,0:T(8,128)}, f32[32,16,128]{2,1,0:T(8,128)S(1)}, u32[]{:S(2)}, u32[]{:S(2)}) collective-permute-start(f32[32,16,128]{2,1,0:T(8,128)} %get-tuple-element.22), channel_id=1, source_target_pairs={{4,0},{8,4},{12,8},{16,12},{20,16},{24,20},{28,24},{32,28},{36,32}... | collective-permute-start | bytes 786440 | tf_op jit(solution)/shard_map/ppermute | solution.py:462
  43.9 1.0 copy-done.6
  44.9 0.7 copy-done.9
  45.6 0.6 copy-done.10
  46.2 5.8 %corners.1.refs_4_.refs_5_ = f32[10,2,17,4,8,128]{5,4,3,2,1,0:T(8,128)} custom-call(s32[2]{0:T(128)S(1)} %copy-done.10, f32[32,32,128]{2,1,0:T(8,128)S(1)} %copy-done.6, f32[33,24,128]{2,1,0:T(8,128)S(1)} %collective-permute-done.4.left, f32[33,24,128]{2,1,0:T(8,128)S(1)} %collective-permute-done.5.right, f32[24,128]{1,0:T(8,128)S(1)} %copy-done.9), custom_call_target="tpu_custom_call" | custom-call | flops 10000000 | bytes 9000000 | tf_op jit(solution)/shard_map/corners/pallas_call | solution.py:183
  52.1 6.1 %iteration.3 = (f32[64,128]{1,0:T(8,128)S(1)}, f32[8,128]{1,0:T(8,128)S(1)}) custom-call(s32[2]{0:T(128)S(1)} %copy-done.10, f32[8,128]{1,0:T(8,128)S(1)} %concatenate.11.refs_0_, f32[32,16,128]{2,1,0:T(8,128)S(1)} %collective-permute-done.10.refs_1_.refs_2_, f32[32,32,128]{2,1,0:T(8,128)S(1)} %copy-done.1, ...), custom_call_target="tpu_custom_call" | custom-call | flops 20000000 | bytes 9000000 | tf_op jit(solution)/shard_map/iteration/pallas_call | solution.py:422
  58.2 21.4 %all_to_all.33 = f32[64,1,128]{2,1,0:T(1,128)S(1)} all-to-all(f32[64,1,128]{2,1,0:T(1,128)S(1)} %bitcast.30), channel_id=1, replica_groups=mesh['tile'=64,'depth'=4] {'tile'}, dimensions={0} | all-to-all | bytes 65536 | tf_op jit(solution)/shard_map/all_to_all | solution.py:513
  79.6 6.4 %iteration.4 = (f32[64,128]{1,0:T(8,128)S(1)}, f32[8,128]{1,0:T(8,128)S(1)}) custom-call(s32[2]{0:T(128)S(1)} %copy-done.10, f32[8,128]{1,0:T(8,128)S(1)} %get-tuple-element.24.refs_0_, f32[64,128]{1,0:T(8,128)S(1)} %bitcast.26, f32[32,16,128]{2,1,0:T(8,128)S(1)} %collective-permute-done.10.refs_1_.refs_2_, f32[32,32,128]{2,1,0:T(8,128)S(1)} %copy-done.1, ...), custom_call_target="tpu_custom_call" | custom-call | flops 20000000 | bytes 9000000 | tf_op jit(solution)/shard_map/iteration/pallas_call | solution.py:422
  86.0 13.3 %all_to_all.34 = f32[64,1,128]{2,1,0:T(1,128)S(1)} all-to-all(f32[64,1,128]{2,1,0:T(1,128)S(1)} %bitcast.31), channel_id=1, replica_groups=mesh['tile'=64,'depth'=4] {'tile'}, dimensions={0} | all-to-all | bytes 65536 | tf_op jit(solution)/shard_map/all_to_all | solution.py:513
  99.3 7.0 %iteration.5 = (f32[64,128]{1,0:T(8,128)}, f32[8,128]{1,0:T(8,128)S(1)}, f32[8,32,128]{2,1,0:T(8,128)}) custom-call(s32[2]{0:T(128)S(1)} %copy-done.10, f32[8,128]{1,0:T(8,128)S(1)} %get-tuple-element.26.refs_0_, f32[64,128]{1,0:T(8,128)S(1)} %bitcast.28, f32[32,16,128]{2,1,0:T(8,128)S(1)} %collective-permute-done.10.refs_1_.refs_2_, ...), custom_call_target="tpu_custom_call" | custom-call | flops 20000000 | bytes 9000000 | tf_op jit(solution)/shard_map/iteration/pallas_call | solution.py:422
  106.3 0.6 copy-done.11
  106.9 4.7 %all-to-all-start.2 = ((f32[64,1,128]{2,1,0:T(1,128)}), f32[64,1,128]{2,1,0:T(1,128)S(1)}, u32[]{:S(2)}, u32[]{:S(2)}) async-start(f32[64,1,128]{2,1,0:T(1,128)} %bitcast.14), calls=%async_computation.2 | async-start | bytes 65536 | tf_op jit(solution)/shard_map/all_to_all | solution.py:513
  111.6 0.7 copy.20.ids
  112.4 8.7 %all-to-all-done.2 = f32[64,1,128]{2,1,0:T(1,128)S(1)} async-done(((f32[64,1,128]{2,1,0:T(1,128)}), f32[64,1,128]{2,1,0:T(1,128)S(1)}, u32[]{:S(2)}, u32[]{:S(2)}) %all-to-all-start.2) | async-done | bytes 32800 | tf_op jit(solution)/shard_map/all_to_all | solution.py:513
  121.0 0.6 copy-done.18
  121.6 1.9 %finish.1 = (f32[3,32]{1,0:T(4,128)}, f32[1,3]{1,0:T(1,128)}) custom-call(s32[2]{0:T(128)} %pad_add_fusion.place, f32[8,128]{1,0:T(8,128)} %copy-done.11, f32[64,128]{1,0:T(8,128)} %bitcast.27, f32[64,128]{1,0:T(8,128)} %bitcast.29, f32[64,128]{1,0:T(8,128)} %bitcast.32, s32[128,1]{1,0:T(8,128)} %copy.20.ids), custom_call_target="tpu_custom_call" | custom-call | tf_op jit(solution)/shard_map/finish/pallas_call | solution.py:450
  (48 shorter events, 0.2 us)
Async XLA Ops:
  0.6 9.1 %copy-start = (f32[3,32]{1,0:T(4,128)S(1)}, f32[3,32]{1,0:T(4,128)}, u32[]{:S(2)}) copy-start(f32[3,32]{1,0:T(4,128)} %param.13) | copy-start | bytes 1156
  0.6 51.4 %copy-start.2 = (f32[480,64]{1,0:T(8,128)S(1)}, f32[480,64]{1,0:T(8,128)}, u32[]{:S(2)}) copy-start(f32[480,64]{1,0:T(8,128)} %constant.83.clone.refs_5_.refs_6_) | copy-start | bytes 368644
  0.7 51.4 %copy-start.3 = (f32[128,128]{1,0:T(8,128)S(1)}, f32[128,128]{1,0:T(8,128)}, u32[]{:S(2)}) copy-start(f32[128,128]{1,0:T(8,128)} %constant.84.clone.refs_6_.refs_7_) | copy-start | bytes 196612
  0.7 51.4 %copy-start.4 = (f32[128,128]{1,0:T(8,128)S(1)}, f32[128,128]{1,0:T(8,128)}, u32[]{:S(2)}) copy-start(f32[128,128]{1,0:T(8,128)} %constant.85.clone.refs_7_.refs_8_) | copy-start | bytes 196612
  0.7 51.4 %copy-start.5 = (f32[128,128]{1,0:T(8,128)S(1)}, f32[128,128]{1,0:T(8,128)}, u32[]{:S(2)}) copy-start(f32[128,128]{1,0:T(8,128)} %constant.86.clone.refs_8_.refs_9_) | copy-start | bytes 196612
  0.7 13.0 %collective-permute-start = (f32[8,32,128]{2,1,0:T(8,128)}, f32[8,32,128]{2,1,0:T(8,128)S(1)}, u32[]{:S(2)}, u32[]{:S(2)}) collective-permute-start(f32[8,32,128]{2,1,0:T(8,128)} %own.2), channel_id=1, source_target_pairs={{1,0},{2,1},{3,2},{0,3},{5,4},{6,5},{7,6},{4,7},{9,8},{10,9},{11,1... | collective-permute-start | bytes 393224 | tf_op jit(solution)/shard_map/ppermute | solution.py:467
  4.3 9.3 %collective-permute-start.1 = (f32[8,32,128]{2,1,0:T(8,128)}, f32[8,32,128]{2,1,0:T(8,128)S(1)}, u32[]{:S(2)}, u32[]{:S(2)}) collective-permute-start(f32[8,32,128]{2,1,0:T(8,128)} %own.2), channel_id=1, source_target_pairs={{2,0},{3,1},{0,2},{1,3},{6,4},{7,5},{4,6},{5,7},{10,8},{11,9},{8,1... | collective-permute-start | bytes 393224 | tf_op jit(solution)/shard_map/ppermute | solution.py:467
  4.7 9.5 %collective-permute-start.2 = (f32[8,32,128]{2,1,0:T(8,128)}, f32[8,32,128]{2,1,0:T(8,128)S(1)}, u32[]{:S(2)}, u32[]{:S(2)}) collective-permute-start(f32[8,32,128]{2,1,0:T(8,128)} %own.2), channel_id=1, source_target_pairs={{3,0},{0,1},{1,2},{2,3},{7,4},{4,5},{5,6},{6,7},{11,8},{8,9},{9,10... | collective-permute-start | bytes 393224 | tf_op jit(solution)/shard_map/ppermute | solution.py:467
  6.9 6.1 %collective-permute-start.3 = (f32[6,128]{1,0:T(8,128)S(1)}, f32[6,128]{1,0:T(8,128)S(1)}, u32[]{:S(2)}, u32[]{:S(2)}) collective-permute-start(f32[6,128]{1,0:T(8,128)S(1)} %convert_element_type.9), channel_id=1, source_target_pairs={{2,0},{3,1},{0,2},{1,3},{6,4},{7,5},{4,6},{5,7},{10,8},{11,9},{8,1... | collective-permute-start | bytes 9224 | tf_op jit(solution)/shard_map/ppermute | solution.py:467
  13.7 0.7 copy-start.12
  13.7 0.7 copy-start.13
  14.4 0.7 copy-start.14
  17.3 26.5 %collective-permute-start.5 = (f32[33,24,128]{2,1,0:T(8,128)}, f32[33,24,128]{2,1,0:T(8,128)S(1)}, u32[]{:S(2)}, u32[]{:S(2)}) collective-permute-start(f32[33,24,128]{2,1,0:T(8,128)} %get-tuple-element.19), channel_id=1, source_target_pairs={{4,0},{8,4},{12,8},{16,12},{20,16},{24,20},{28,24},{32,28},{36,32}... | collective-permute-start | bytes 1216520 | tf_op jit(solution)/shard_map/ppermute | solution.py:462
  21.1 22.7 %collective-permute-start.4 = (f32[33,24,128]{2,1,0:T(8,128)}, f32[33,24,128]{2,1,0:T(8,128)S(1)}, u32[]{:S(2)}, u32[]{:S(2)}) collective-permute-start(f32[33,24,128]{2,1,0:T(8,128)} %get-tuple-element.18), channel_id=1, source_target_pairs={{0,4},{4,8},{8,12},{12,16},{16,20},{20,24},{24,28},{28,32},{32,36}... | collective-permute-start | bytes 1216520 | tf_op jit(solution)/shard_map/ppermute | solution.py:462
  24.5 5.7 %collective-permute-start.7 = (f32[8,32,128]{2,1,0:T(8,128)}, f32[8,32,128]{2,1,0:T(8,128)S(1)}, u32[]{:S(2)}, u32[]{:S(2)}) collective-permute-start(f32[8,32,128]{2,1,0:T(8,128)} %own.3), channel_id=1, source_target_pairs={{1,0},{2,1},{3,2},{0,3},{5,4},{6,5},{7,6},{4,7},{9,8},{10,9},{11,1... | collective-permute-start | bytes 393224 | tf_op jit(solution)/shard_map/ppermute | solution.py:467
  25.3 6.9 %collective-permute-start.8 = (f32[8,32,128]{2,1,0:T(8,128)}, f32[8,32,128]{2,1,0:T(8,128)S(1)}, u32[]{:S(2)}, u32[]{:S(2)}) collective-permute-start(f32[8,32,128]{2,1,0:T(8,128)} %own.3), channel_id=1, source_target_pairs={{2,0},{3,1},{0,2},{1,3},{6,4},{7,5},{4,6},{5,7},{10,8},{11,9},{8,1... | collective-permute-start | bytes 393224 | tf_op jit(solution)/shard_map/ppermute | solution.py:467
  26.7 8.4 %collective-permute-start.9 = (f32[8,32,128]{2,1,0:T(8,128)}, f32[8,32,128]{2,1,0:T(8,128)S(1)}, u32[]{:S(2)}, u32[]{:S(2)}) collective-permute-start(f32[8,32,128]{2,1,0:T(8,128)} %own.3), channel_id=1, source_target_pairs={{3,0},{0,1},{1,2},{2,3},{7,4},{4,5},{5,6},{6,7},{11,8},{8,9},{9,10... | collective-permute-start | bytes 393224 | tf_op jit(solution)/shard_map/ppermute | solution.py:467
  30.3 4.8 %copy-start.15 = (f32[8,32,128]{2,1,0:T(8,128)}, f32[8,32,128]{2,1,0:T(8,128)S(1)}, u32[]{:S(2)}) copy-start(f32[8,32,128]{2,1,0:T(8,128)S(1)} %collective-permute-done.7.one) | copy-start | bytes 393220
  30.3 13.5 %collective-permute-start.6 = (f32[1,128]{1,0:T(1,128)S(1)}, f32[1,128]{1,0:T(1,128)S(1)}, u32[]{:S(2)}, u32[]{:S(2)}) collective-permute-start(f32[1,128]{1,0:T(1,128)S(1)} %bitcast.34), channel_id=1, source_target_pairs={{8,0},{12,4},{16,8},{20,12},{24,16},{28,20},{32,24},{36,28},{40,32... | collective-permute-start | bytes 1544 | tf_op jit(solution)/shard_map/ppermute | solution.py:462
  32.2 2.8 %copy-start.16 = (f32[8,32,128]{2,1,0:T(8,128)}, f32[8,32,128]{2,1,0:T(8,128)S(1)}, u32[]{:S(2)}) copy-start(f32[8,32,128]{2,1,0:T(8,128)S(1)} %collective-permute-done.8.two) | copy-start | bytes 393220
  35.1 0.7 copy-start.17
  37.9 14.2 %copy-start.1 = (f32[32,32,128]{2,1,0:T(8,128)S(1)}, f32[32,32,128]{2,1,0:T(8,128)}, u32[]{:S(2)}) copy-start(f32[32,32,128]{2,1,0:T(8,128)} %get-tuple-element.21.refs_2_.refs_3_) | copy-start | bytes 1572868
  37.9 14.1 %collective-permute-start.10 = (f32[32,16,128]{2,1,0:T(8,128)}, f32[32,16,128]{2,1,0:T(8,128)S(1)}, u32[]{:S(2)}, u32[]{:S(2)}) collective-permute-start(f32[32,16,128]{2,1,0:T(8,128)} %get-tuple-element.20), channel_id=1, source_target_pairs={{0,4},{4,8},{8,12},{12,16},{16,20},{20,24},{24,28},{28,32},{32,36}... | collective-permute-start | bytes 786440 | tf_op jit(solution)/shard_map/ppermute | solution.py:462
  41.8 10.2 %collective-permute-start.11 = (f32[32,16,128]{2,1,0:T(8,128)}, f32[32,16,128]{2,1,0:T(8,128)S(1)}, u32[]{:S(2)}, u32[]{:S(2)}) collective-permute-start(f32[32,16,128]{2,1,0:T(8,128)} %get-tuple-element.22), channel_id=1, source_target_pairs={{4,0},{8,4},{12,8},{16,12},{20,16},{24,20},{28,24},{32,28},{36,32}... | collective-permute-start | bytes 786440 | tf_op jit(solution)/shard_map/ppermute | solution.py:462
  43.9 1.0 copy-start.6
  44.9 0.7 copy-start.9
  45.6 0.6 copy-start.10
  79.6 26.7 %copy-start.7 = (f32[64,1,128]{2,1,0:T(1,128)}, f32[64,1,128]{2,1,0:T(1,128)S(1)}, u32[]{:S(2)}) copy-start(f32[64,1,128]{2,1,0:T(1,128)S(1)} %all_to_all.33) | copy-start | bytes 98308
  99.3 21.7 %copy-start.8 = (f32[64,1,128]{2,1,0:T(1,128)}, f32[64,1,128]{2,1,0:T(1,128)S(1)}, u32[]{:S(2)}) copy-start(f32[64,1,128]{2,1,0:T(1,128)S(1)} %all_to_all.34) | copy-start | bytes 98308
  106.3 0.6 copy-start.11
  106.9 14.1 %all-to-all-start.2 = ((f32[64,1,128]{2,1,0:T(1,128)}), f32[64,1,128]{2,1,0:T(1,128)S(1)}, u32[]{:S(2)}, u32[]{:S(2)}) async-start(f32[64,1,128]{2,1,0:T(1,128)} %bitcast.14), calls=%async_computation.2 | async-start | bytes 65536 | tf_op jit(solution)/shard_map/all_to_all | solution.py:513
  121.0 0.6 copy-start.18

commit v2 on v1

--- a/solution.py
+++ b/solution.py
@@ -2,7 +2,6 @@
 
 import jax
 import jax.numpy as jnp
-import numpy as np
 from jax import lax
 from jax.experimental import pallas as pl
 from jax.experimental.pallas import tpu as pltpu
@@ -23,27 +22,6 @@
 highest = lax.Precision.HIGHEST
 
 
-def hat(centers, places):
-    return np.maximum(1.0 - np.abs(centers[:, None] - places[None, :]) / ELEM, 0.0)
-
-
-def constants():
-    frame = np.arange(FRAME) - HALO + 0.5
-    along_x = np.zeros((6, FRAME, 4, 16), np.float32)
-    for tile in range(4):
-        for k in range(2):
-            column = hat(frame, np.array([(2 * (tile - 1) + k) * ELEM]))[:, 0]
-            for ca in range(6):
-                along_x[ca, :, tile, k * 6 + ca] = column
-    along_y = hat(np.arange(LANES) + 0.5, (np.arange(LANES) % 8) * ELEM).astype(np.float32)
-    return (
-        along_x.reshape(6 * FRAME, 64),
-        np.ascontiguousarray(along_y.T),
-        along_y,
-        along_y * along_y,
-    )
-
-
 def dot(left, right):
     return jnp.dot(left, right, precision=highest, preferred_element_type=F32)
 
@@ -56,61 +34,160 @@
     return lax.broadcasted_iota(jnp.int32, shape, 0)
 
 
-def pack_body(with_extra, halo, place, own, one, two, three, *refs):
-    if with_extra:
-        extra, full, low, high = refs
-    else:
-        full, low, high = refs
-    depth = place[1]
-    for step, piece in enumerate((own, one, two, three)):
-        start = lax.rem(depth + step, 4) * 8
-        block = piece[...]
-        full[pl.ds(start, 8)] = block
-        low[pl.ds(start, 8)] = block[:, :halo]
-        high[pl.ds(start, 8)] = block[:, ROWS - halo :]
-    if with_extra:
-        low[SLAB] = extra[...]
-        high[SLAB] = extra[...]
-
-
-def pack(place, pieces, halo, extra=None):
-    planes = SLAB + (extra is not None)
-    shapes = [
-        jax.ShapeDtypeStruct((SLAB, ROWS, LANES), F32),
-        jax.ShapeDtypeStruct((planes, halo, LANES), F32),
-        jax.ShapeDtypeStruct((planes, halo, LANES), F32),
+def along_y_table(shape, lane_axis):
+    y = lax.broadcasted_iota(jnp.int32, shape, 1 - lane_axis).astype(F32) + 0.5
+    places = (lax.broadcasted_iota(jnp.int32, shape, lane_axis) % 8 * ELEM).astype(F32)
+    return jnp.maximum(1.0 - jnp.abs(y - places) * (1.0 / ELEM), 0.0)
+
+
+def along_x_table():
+    shape = (FRAME, 64)
+    row = row_ids(shape).astype(F32) + (0.5 - HALO)
+    column = lane_ids(shape)
+    node = 2 * (column // 16 - 1) + column % 16 // 6
+    hats = jnp.maximum(1.0 - jnp.abs(row - (node * ELEM).astype(F32)) * (1.0 / ELEM), 0.0)
+    return [jnp.where((column % 16 < 12) & (column % 16 % 6 == n), hats, 0.0) for n in range(6)]
+
+
+def prepare_body(offsets, far_ids, far_motion, *refs):
+    lines, chooser, along_x, along_y, over_y, over_y2 = refs[:6]
+    held, node_ids, start_motion, sem = refs[6:]
+    nodes = [
+        pltpu.make_async_copy(far_ids, node_ids, sem.at[6]),
+        pltpu.make_async_copy(far_motion, start_motion, sem.at[7]),
     ]
+    picked = [
+        pltpu.make_async_copy(
+            offsets.at[c, 0, pl.ds(ELEM * ex, 8)], held.at[2 * c + ex], sem.at[2 * c + ex]
+        )
+        for c in range(3)
+        for ex in range(2)
+    ]
+    for copy in nodes + picked:
+        copy.start()
+    for copy in nodes:
+        copy.wait()
+    shape = (8, LANES)
+    lanes = lane_ids(shape)
+    eight = jnp.where(lanes % 8 == row_ids(shape), 1.0, 0.0)
+    ids = jnp.zeros((1, LANES), F32)
+    lanes1 = lane_ids((1, LANES))
+    group = lanes1 // 8
+    for k in range(2):
+        for a in range(2):
+            wide = dot((node_ids[a, k : k + 1] % 32).astype(F32), eight)
+            ids = jnp.where((group // 6 == k) & (group % 2 == a), wide, ids)
+    ids = jnp.where(lanes1 < 96, ids, -1.0)
+    chosen = jnp.where(row_ids((32, LANES)).astype(F32) == ids, 1.0, 0.0)
+    chooser[...] = chosen
+    taken = dot(start_motion[...], chosen)
+    component = (lane_ids((3, LANES)) // 16) % 3
+    line = jnp.sum(
+        jnp.where(component == row_ids((3, LANES)), taken, 0.0), axis=0, keepdims=True
+    )
+    square = (LANES, LANES)
+    along_y[...] = along_y_table(square, 0)
+    table = along_y_table(square, 1)
+    over_y[...] = table
+    over_y2[...] = table * table
+    for n, hats in enumerate(along_x_table()):
+        along_x[n * FRAME : (n + 1) * FRAME] = hats
+    lines[...] = jnp.broadcast_to(line, shape)
+    for n, copy in enumerate(picked):
+        copy.wait()
+        lines[n : n + 1] = held[n, 0:1].astype(F32)
+
+
+def prepare(offsets, node_ids, start_motion):
     vmem = pl.BlockSpec(memory_space=pltpu.VMEM)
-    args = [place, *pieces] + ([extra] if extra is not None else [])
+    outside = pl.BlockSpec(memory_space=pltpu.HBM)
+    shapes = ((8, LANES), (32, LANES), (6 * FRAME, 64)) + ((LANES, LANES),) * 3
     return pl.pallas_call(
-        functools.partial(pack_body, extra is not None, halo),
-        out_shape=shapes,
-        in_specs=[pl.BlockSpec(memory_space=pltpu.SMEM)] + [vmem] * (len(args) - 1),
-        out_specs=[vmem] * 3,
+        prepare_body,
+        out_shape=[jax.ShapeDtypeStruct(shape, F32) for shape in shapes],
+        in_specs=[outside] * 3,
+        out_specs=[vmem] * len(shapes),
+        scratch_shapes=[
+            pltpu.VMEM((6, 8, LANES), jnp.int32),
+            pltpu.VMEM(node_ids.shape, jnp.int32),
+            pltpu.VMEM(start_motion.shape, F32),
+            pltpu.SemaphoreType.DMA((8,)),
+        ],
+        name="prepare",
+        compiler_params=pltpu.CompilerParams(vmem_limit_bytes=2 * 2**20),
+    )(offsets, node_ids, start_motion)
+
+
+def pack_body(*refs):
+    both = refs[:4]
+    lines, other, beyond, far, far_target, near, near_target, extra = refs[4:]
+    depth = lax.axis_index("depth")
+    odd = lax.rem(lax.axis_index("tile"), 2)
+    for step in range(4):
+        planes = pl.ds(lax.rem(depth + step, 4) * 8, 8)
+        for part, odds in ((far, odd), (near, 1 - odd)):
+            rows = pl.ds(pl.multiple_of(8 * odds, 8), HALO)
+            part[planes] = both[step][0:8, rows]
+        for part, odds in ((far_target, odd), (near_target, 1 - odd)):
+            rows = pl.ds(pl.multiple_of(16 * odds, 8), ELEM)
+            part[planes] = both[step][8:16, rows]
+    upper = depth >= 2
+    mine, given = lines[0:6], other[0:6]
+    extra[...] = jnp.zeros_like(extra)
+    extra[0:6] = jnp.where(upper, given, mine)
+    extra[6:12] = jnp.where(upper, mine, given)
+    extra[12:13] = lines[6:7]
+    extra[13:14] = beyond[6:7]
+    far[SLAB] = extra[...]
+    near[SLAB] = extra[...]
+
+
+def pack(*args):
+    sides = (SLAB + 1, HALO, LANES)
+    target_sides = (SLAB, ELEM, LANES)
+    shapes = (sides, target_sides, sides, target_sides, (HALO, LANES))
+    vmem = pl.BlockSpec(memory_space=pltpu.VMEM)
+    return pl.pallas_call(
+        pack_body,
+        out_shape=[jax.ShapeDtypeStruct(shape, F32) for shape in shapes],
+        in_specs=[vmem] * len(args),
+        out_specs=[vmem] * len(shapes),
         cost_estimate=pl.CostEstimate(flops=0, bytes_accessed=2000000, transcendentals=0),
         name="pack",
+        compiler_params=pltpu.CompilerParams(vmem_limit_bytes=4 * 2**20),
     )(*args)
 
 
-def corner_body(tiles, place, full, left, right, extra, cor, source, shifted, table, chunk, sems):
-    tile = place[0]
+def corner_body(tiles, own, one, two, three, far, near, extra, *refs):
+    chunk, motion, source, shifted, table = refs
+    tile = lax.axis_index("tile")
+    depth = lax.axis_index("depth")
+    odd = lax.rem(tile, 2)
+    motion[...] = jnp.zeros_like(motion)
+    motion[1:2] = extra[12:13]
+    motion[3:4] = extra[13:14]
+    motion[pl.ds(2 * odd, 1)] = far[SLAB, 12:13]
+    motion[pl.ds(2 - 2 * odd, 1)] = near[SLAB, 12:13]
     zero = jnp.zeros((2, FRAME + 16, LANES), F32)
     source[0:2] = zero
     source[SLAB + 2 : SLAB + 4] = zero
     edge = jnp.zeros((SLAB, 8, LANES), F32)
     source[2 : SLAB + 2, 0:8] = edge
     source[2 : SLAB + 2, 8 + FRAME : 16 + FRAME] = edge
-    source[2 : SLAB + 2, 8 : 8 + HALO] = left[0:SLAB]
-    source[2 : SLAB + 2, 8 + HALO : 8 + HALO + ROWS] = full[...]
-    source[2 : SLAB + 2, 8 + HALO + ROWS : 8 + FRAME] = right[0:SLAB]
-    sides = ((left, 0), (left, 1), (extra, 0), (extra, 1), (right, 0), (right, 1))
-    for ex, (side, which) in enumerate(sides):
-        for e in range(2):
-            for c in range(3):
+    for part, right in ((far, odd), (near, 1 - odd)):
+        rows = pl.ds(pl.multiple_of(8 + (HALO + ROWS) * right, 8), HALO)
+        source[2 : SLAB + 2, rows] = part[0:SLAB]
+    for step, piece in enumerate((own, one, two, three)):
+        start = lax.rem(depth + step, 4) * 8
+        source[pl.ds(start + 2, 8), 8 + HALO : 8 + HALO + ROWS] = piece[0:8]
+    for e in range(2):
+        for c in range(3):
+            for which in range(2):
                 at = e * 6 + c * 2 + which
-                row = side[at : at + 1] if side is extra else side[SLAB, at : at + 1]
-                place_at = (e * 6 + ex) * 3 + c
-                table[place_at : place_at + 1] = row
+                row = (e * 6 + which) * 3 + c
+                table[row + 6 : row + 7] = extra[at : at + 1]
+                table[pl.ds(row + 12 * odd, 1)] = far[SLAB, at : at + 1]
+                table[pl.ds(row + 12 - 12 * odd, 1)] = near[SLAB, at : at + 1]
 
     shape = (8, LANES)
     lanes = lane_ids(shape)
@@ -169,33 +246,31 @@
                     chunk[v, e, p - 3, 1] = c01 - c00
                     chunk[v, e, p - 3, 2] = c10 - c00
                     chunk[v, e, p - 3, 3] = (c11 - c10) - (c01 - c00)
-        pltpu.make_async_copy(chunk.at[v], cor.at[v], sems.at[v]).start()
         return carry
 
     lax.fori_loop(0, GROUPS, group, 0)
-    for v in range(GROUPS):
-        pltpu.make_async_copy(chunk.at[v], cor.at[v], sems.at[v]).wait()
-
-
-def corner_images(tiles, place, full, left, right, extra):
+
+
+def corner_images(tiles, *args):
     vmem = pl.BlockSpec(memory_space=pltpu.VMEM)
     shape = (GROUPS, 2, 17, 4, 8, LANES)
     return pl.pallas_call(
         functools.partial(corner_body, tiles),
-        out_shape=jax.ShapeDtypeStruct(shape, F32),
-        in_specs=[pl.BlockSpec(memory_space=pltpu.SMEM)] + [vmem] * 4,
-        out_specs=pl.BlockSpec(memory_space=pl.ANY),
+        out_shape=[
+            jax.ShapeDtypeStruct(size, F32)
+            for size in (shape, (8, LANES))
+        ],
+        in_specs=[vmem] * len(args),
+        out_specs=[vmem] * 2,
         scratch_shapes=[
             pltpu.VMEM((SLAB + 4, FRAME + 16, LANES), F32),
             pltpu.VMEM((2, 20, 16, LANES), F32),
             pltpu.VMEM((40, LANES), F32),
-            pltpu.VMEM(shape, F32),
-            pltpu.SemaphoreType.DMA((GROUPS,)),
         ],
         cost_estimate=pl.CostEstimate(flops=10000000, bytes_accessed=9000000, transcendentals=0),
         name="corners",
-        compiler_params=pltpu.CompilerParams(vmem_limit_bytes=48 * 2**20),
-    )(place, full, left, right, extra)
+        compiler_params=pltpu.CompilerParams(vmem_limit_bytes=12 * 2**20),
+    )(*args)
 
 
 def updated_motion(motion, received, tile, tiles, padded):
@@ -210,24 +285,31 @@
     return motion[...] - step * near
 
 
-def iteration_body(tiles, first, last, place, *refs):
+def iteration_body(tiles, first, last, *refs):
     refs = list(refs)
     motion = refs.pop(0)
     received = None if first else refs.pop(0)
-    ref_left, ref_own, ref_right, cor, along_x, along_y, over_y, over_y2 = refs[:8]
-    refs = refs[8:]
-    block_out, motion_out = refs[:2]
-    refs = refs[2:]
+    if first:
+        pieces, refs = refs[:6], refs[6:]
+    else:
+        target = refs.pop(0)
+    cors, along_x, along_y, over_y, over_y2, block_out, motion_out = refs[:7]
+    refs = refs[7:]
+    if first:
+        target = refs.pop(0)
     residual_out = refs.pop(0) if last else None
-    cors, wide, warped, slopes, layers, rows_f, rows_s, padded = refs[:8]
-    refs = refs[8:]
-    residuals = refs.pop(0) if last else None
-    sems = refs.pop(0)
-
-    for v in range(GROUPS):
-        pltpu.make_async_copy(cor.at[v], cors.at[v], sems.at[v]).start()
-
-    tile = place[0]
+    wide, warped, slopes, layers, rows_f, rows_s, padded = refs[:7]
+    residuals = refs[7] if last else None
+
+    tile = lax.axis_index("tile")
+    if first:
+        depth = lax.axis_index("depth")
+        odd = lax.rem(tile, 2)
+        for step, piece in enumerate(pieces[:4]):
+            start = lax.rem(depth + step, 4) * 8
+            target[pl.ds(start, 8), ELEM : ELEM + ROWS] = piece[8:16]
+        for part, right in ((pieces[4], odd), (pieces[5], 1 - odd)):
+            target[:, pl.ds(pl.multiple_of((ELEM + ROWS) * right, 8), ELEM)] = part[...]
     low_flag = jnp.where(tile > 0, 1.0, 0.0).astype(F32)
     high_flag = jnp.where(tile < tiles - 1, 1.0, 0.0).astype(F32)
     now = motion[...] if first else updated_motion(motion, received, tile, tiles, padded)
@@ -244,7 +326,6 @@
     warped[SLAB + 2 : SLAB + 4] = zero
 
     def warp(v, carry):
-        pltpu.make_async_copy(cor.at[v], cors.at[v], sems.at[v]).wait()
         at = pl.ds(pl.multiple_of(8 * v, 8), 8)
         near = [wide[pl.ds(pl.multiple_of(2 * c * FRAME + 8 * v, 8), 8)] for c in range(3)]
         far = [wide[pl.ds(pl.multiple_of((2 * c + 1) * FRAME + 8 * v, 8), 8)] for c in range(3)]
@@ -277,9 +358,10 @@
     behind_2 = jnp.where(lanes > 1, 1.0, 0.0)
     zeros = jnp.zeros(shape, F32)
 
-    def slope_group(v, target, target_start, own, misfit):
+    def slope_group(v, own, misfit):
         at = pl.ds(pl.multiple_of(8 * v, 8), 8)
-        row = pl.multiple_of(8 * (v - target_start), 8)
+        row = pl.multiple_of(8 * (v - 3), 8)
+        goal = pl.ds(pl.multiple_of(8 * (v - 1), 8), 8)
         planes = [warped[n, at] for n in range(4)]
         for e in range(2):
             first_sum = [zeros] * 3
@@ -300,7 +382,7 @@
                 slope_y = (
                     ahead_1 * pltpu.roll(mid, LANES - 1, 1) - behind_1 * pltpu.roll(mid, 1, 1)
                 ) - (ahead_2 * pltpu.roll(mid, LANES - 2, 1) - behind_2 * pltpu.roll(mid, 2, 1))
-                residual = mid - target[z, pl.ds(row, 8)]
+                residual = mid - target[z, goal]
                 three = (slope_z, slope_x, slope_y)
                 if own:
                     misfit = misfit + residual * residual
@@ -328,9 +410,9 @@
                     layers[v - 1, 6 + 2 * c + 1] += squares_0[c]
         return misfit
 
-    lax.fori_loop(1, 3, lambda v, m: slope_group(v, ref_left, 1, False, m), zeros)
-    misfit = lax.fori_loop(3, 7, lambda v, m: slope_group(v, ref_own, 3, True, m), zeros)
-    lax.fori_loop(7, 9, lambda v, m: slope_group(v, ref_right, 7, False, m), zeros)
+    lax.fori_loop(1, 3, lambda v, m: slope_group(v, False, m), zeros)
+    misfit = lax.fori_loop(3, 7, lambda v, m: slope_group(v, True, m), zeros)
+    lax.fori_loop(7, 9, lambda v, m: slope_group(v, False, m), zeros)
 
     rows_f[...] = jnp.zeros_like(rows_f)
     rows_s[...] = jnp.zeros_like(rows_s)
@@ -393,20 +475,17 @@
         line = jnp.where(line_lanes == at, value, line)
     block_out[...] = jnp.broadcast_to(line, (tiles, LANES))
     if last:
-        residual_out[...] = residuals[pl.ds(place[1] * 8, 8)]
-
-
-def iteration(tiles, first, last, place, motion, received, targets, cor, tables):
+        residual_out[...] = residuals[pl.ds(lax.axis_index("depth") * 8, 8)]
+
+
+def iteration(tiles, first, last, motion, received, target, cor, tables):
     vmem = pl.BlockSpec(memory_space=pltpu.VMEM)
-    args = [place, motion] + ([] if first else [received]) + [*targets, cor, *tables]
-    in_specs = [pl.BlockSpec(memory_space=pltpu.SMEM)] + [vmem] * (len(args) - 1)
-    in_specs[-5] = pl.BlockSpec(memory_space=pl.ANY)
+    args = [motion] + ([] if first else [received]) + [*target, cor, *tables]
     shapes = [
         jax.ShapeDtypeStruct((tiles, LANES), F32),
         jax.ShapeDtypeStruct((8, LANES), F32),
     ]
     scratch = [
-        pltpu.VMEM((GROUPS, 2, 17, 4, 8, LANES), F32),
         pltpu.VMEM((6 * FRAME, LANES), F32),
         pltpu.VMEM((SLAB + 4, FRAME, LANES), F32),
         pltpu.VMEM((3, SLAB, ROWS, LANES), F32),
@@ -415,46 +494,49 @@
         pltpu.VMEM((24, LANES), F32),
         pltpu.VMEM((tiles + 24, LANES), F32),
     ]
+    if first:
+        shapes.append(jax.ShapeDtypeStruct((SLAB, ROWS + 2 * ELEM, LANES), F32))
     if last:
         shapes.append(jax.ShapeDtypeStruct((8, ROWS, LANES), F32))
         scratch.append(pltpu.VMEM((SLAB, ROWS, LANES), F32))
-    scratch.append(pltpu.SemaphoreType.DMA((GROUPS,)))
     return pl.pallas_call(
         functools.partial(iteration_body, tiles, first, last),
         out_shape=shapes,
-        in_specs=in_specs,
+        in_specs=[vmem] * len(args),
         out_specs=[vmem] * len(shapes),
         scratch_shapes=scratch,
         cost_estimate=pl.CostEstimate(flops=20000000, bytes_accessed=9000000, transcendentals=0),
         name="iteration",
-        compiler_params=pltpu.CompilerParams(vmem_limit_bytes=48 * 2**20),
+        compiler_params=pltpu.CompilerParams(vmem_limit_bytes=16 * 2**20),
     )(*args)
 
 
-def finish_body(tiles, place, motion, got_1, got_2, got_3, ids, displacement, misfits, padded):
-    now = updated_motion(motion, got_3, place[0], tiles, padded)
+def finish_body(tiles, motion, got_1, got_2, got_3, chooser, displacement, misfits, padded):
+    now = updated_motion(motion, got_3, lax.axis_index("tile"), tiles, padded)
     shape = (8, LANES)
     component = (lane_ids(shape) // 16) % 3
     mine = jnp.where(component == row_ids(shape), jnp.broadcast_to(now[1:2], shape), 0.0)
     mine = jnp.where(lane_ids(shape) < 96, mine, 0.0)
-    chooser = jnp.where(ids[...] == lane_ids((LANES, LANES)), 1.0, 0.0)
-    placed = dot(mine, chooser)
-    displacement[...] = placed[0:3, 0:32]
+    placed = lax.dot_general(
+        mine, chooser[...], (((1,), (1,)), ((), ())), precision=highest, preferred_element_type=F32
+    )
+    displacement[...] = placed[0:3]
     for n, got in enumerate((got_1, got_2, got_3)):
         total = jnp.sum(got[...], axis=0, keepdims=True)
         misfits[:, n : n + 1] = total[:, 99:100] * (1.0 / VOXELS)
 
 
-def finish(tiles, place, motion, got, ids):
+def finish(tiles, motion, got, chooser):
     vmem = pl.BlockSpec(memory_space=pltpu.VMEM)
     return pl.pallas_call(
         functools.partial(finish_body, tiles),
         out_shape=[jax.ShapeDtypeStruct((3, 32), F32), jax.ShapeDtypeStruct((1, 3), F32)],
-        in_specs=[pl.BlockSpec(memory_space=pltpu.SMEM)] + [vmem] * 5,
+        in_specs=[vmem] * 5,
         out_specs=[vmem] * 2,
         scratch_shapes=[pltpu.VMEM((tiles + 24, LANES), F32)],
         name="finish",
-    )(place, motion, *got, ids)
+        compiler_params=pltpu.CompilerParams(vmem_limit_bytes=2**20),
+    )(motion, *got, chooser)
 
 
 def from_behind(block, axis, distance):
@@ -462,6 +544,11 @@
     return lax.ppermute(block, axis, [(i - distance, i) for i in devices if i - distance in devices])
 
 
+def swap(block, first):
+    pairs = [(i, i + 1) for i in range(first, lax.axis_size("tile") - 1, 2)]
+    return lax.ppermute(block, "tile", pairs + [(j, i) for i, j in pairs])
+
+
 def ring(block, distance):
     peers = lax.axis_size("depth")
     return lax.ppermute(block, "depth", [((i + distance) % peers, i) for i in range(peers)])
@@ -469,50 +556,29 @@
 
 def local(reference_image, deformed_image, offsets, node_ids, start_motion):
     tiles = lax.axis_size("tile")
-    tile = lax.axis_index("tile")
-    depth = lax.axis_index("depth")
-    place = jnp.stack([tile, depth]).astype(jnp.int32)
-    tables = [jnp.asarray(table) for table in constants()]
-
-    deformed = [deformed_image] + [ring(deformed_image, n) for n in (1, 2, 3)]
-    targets = [reference_image] + [ring(reference_image, n) for n in (1, 2, 3)]
-
-    mine = offsets[:, 0, ::ELEM, :].astype(F32).reshape(6, LANES)
-    other = ring(mine, 2)
-    upper = depth >= 2
-    shifts = jnp.concatenate([jnp.where(upper, other, mine), jnp.where(upper, mine, other)], axis=0)
-
-    local_ids = jnp.transpose(node_ids % 32, (1, 0, 2))
-    id_line = jnp.broadcast_to(local_ids[:, None], (2, 3, 2, 8)).reshape(96)
-    id_line = jnp.concatenate([id_line, jnp.full((32,), -1, jnp.int32)])
-    chooser = (id_line[:, None] == jnp.arange(32, dtype=jnp.int32)[None, :]).astype(F32)
-    part = (jnp.arange(LANES, dtype=jnp.int32) // 16) % 3
-    line = jnp.sum(chooser * jnp.take(start_motion, part, axis=0), axis=1)[None]
-    beyond = from_behind(line, "tile", -2)
-
-    extra = jnp.concatenate([shifts, line, jnp.zeros((HALO - 13, LANES), F32)], axis=0)
-    full, low, high = pack(place, deformed, HALO, extra)
-    left = from_behind(high, "tile", 1)
-    right = from_behind(low, "tile", -1)
-    motion = jnp.concatenate(
-        [left[SLAB, 12:13], line, right[SLAB, 12:13], beyond, jnp.zeros((4, LANES), F32)], axis=0
-    )
-    cor = corner_images(tiles, place, full, left, right, extra)
-
-    target_own, target_low, target_high = pack(place, targets, ELEM)
-    target_left = from_behind(target_high, "tile", 1)
-    target_right = from_behind(target_low, "tile", -1)
-    targets = (target_left, target_own, target_right)
-
+    both = jnp.concatenate([deformed_image, reference_image], axis=0)
+    both = [both] + [ring(both, n) for n in (1, 2, 3)]
+    lines, chooser, *tables = prepare(offsets, node_ids, start_motion)
+    other = ring(lines, 2)
+    beyond = from_behind(lines, "tile", -2)
+    far, far_target, near, near_target, extra = pack(*both, lines, other, beyond)
+    far = swap(far, 1)
+    near = swap(near, 0)
+    far_target = swap(far_target, 1)
+    near_target = swap(near_target, 0)
+    cor, motion = corner_images(tiles, *both, far, near, extra)
+    target = (*both, far_target, near_target)
     received = None
     got = []
     for number in range(ITERS):
-        last = number == ITERS - 1
-        outs = iteration(tiles, number == 0, last, place, motion, received, targets, cor, tables)
+        first, last = number == 0, number == ITERS - 1
+        outs = iteration(tiles, first, last, motion, received, target, cor, tables)
         block, motion = outs[:2]
+        if first:
+            target = (outs[2],)
         received = lax.all_to_all(block, "tile", 0, 0, tiled=True)
         got.append(received)
-    displacement, misfits = finish(tiles, place, motion, got, id_line[:, None])
+    displacement, misfits = finish(tiles, motion, got, chooser)
     return displacement, misfits.reshape(3), outs[2]
 
 

time: 124 us -> 97.5 us (0.79)
  blocking collectives: 34.7 us -> 48.6 us
  Pallas kernels: 31.6 us -> 19.6 us
  starting transfers between devices: 27.9 us -> 16.6 us
  waiting for transfers between devices: 18 us -> 7.38 us
  local copies, waits for them, and re-layouts: 8.16 us -> 4.19 us
  other arithmetic: 2.2 us -> 0 us
    all_to_all x2 -> x3, blocking collectives: 34.7 us -> 48.6 us  [local(): received = lax.all_to_all(block, 'tile', 0, 0, tiled=True)]
    ppermute x5 -> x1, starting transfers between devices: 14.3 us -> 1.29 us  [from_behind(): lax.ppermute(block, axis, [(i - distance, i) for i in devices if i - dist...]
    ppermute x0 -> x4, starting transfers between devices: none -> 9.08 us  [swap(): return lax.ppermute(block, 'tile', pairs + [(j, i) for i, j in pairs])]
    all_to_all x1 -> x0, waiting for transfers between devices: 8.66 us -> none  [local(): received = lax.all_to_all(block, 'tile', 0, 0, tiled=True)]
    ppermute x7 -> x4, waiting for transfers between devices: 9.34 us -> 2.7 us  [ring(): lax.ppermute(block, 'depth', [((i + distance) % peers, i) for i in range(...]
    pallas_call x3, Pallas kernels: 19.5 us -> 13.7 us  [iteration(): pl.pallas_call(functools.partial(iteration_body, tiles, first, last), out...]
    pallas_call x3, Pallas kernels: 10.2 us -> 4.94 us  [the longest x1 4.38 us: corner_images(): pl.pallas_call(functools.partial(corner_body, tiles), out_shape=[jax.Shap...]
    all_to_all x1 -> x0, starting transfers between devices: 4.7 us -> none  [local(): received = lax.all_to_all(block, 'tile', 0, 0, tiled=True)]
  transfers between devices with their start and end apart: 13 -> 9, of which waited for: 6 -> 3; matrix products, arithmetic and copies ran while one was open for 4% -> 0% of each run, Pallas kernels for 6% -> 5%
where the time goes in v2:
time: 97.5 us; the launch traced here: 97.1 us
  blocking collectives  48.6 us (50%)
  Pallas kernels  19.6 us (20%)
  starting transfers between devices  16.6 us (17%)
  waiting for transfers between devices  7.38 us (8%)
  local copies, waits for them, and re-layouts  4.19 us (4%)
    all_to_all x3, blocking collectives, local(): received = lax.all_to_all(block, 'tile', 0, 0, tiled=True)  48.6 us
    pallas_call x3, Pallas kernels, iteration(): pl.pallas_call(functools.partial(iteration_body, tiles, first, last), out...  13.7 us
    ppermute x4, starting transfers between devices, swap(): return lax.ppermute(block, 'tile', pairs + [(j, i) for i, j in pairs])  9.08 us
    ppermute x4, starting transfers between devices, ring(): lax.ppermute(block, 'depth', [((i + distance) % peers, i) for i in range(...  6.19 us
    pallas_call x1, Pallas kernels, corner_images(): pl.pallas_call(functools.partial(corner_body, tiles), out_shape=[jax.Shap...  4.38 us
    unnamed x7, local copies, waits for them, and re-layouts  3.27 us
    ppermute x1, waiting for transfers between devices, from_behind(): lax.ppermute(block, axis, [(i - distance, i) for i in devices if i - dist...  3.23 us
    ppermute x4, waiting for transfers between devices, ring(): lax.ppermute(block, 'depth', [((i + distance) % peers, i) for i in range(...  2.7 us
  transfers between devices with their start and end apart: 9, of which 3 were waited for; matrix products, arithmetic and copies ran while one was open for 0% of the time, Pallas kernels for 5%

profile of v2, /device:TPU:1, one launch (start us, length us, event | category | flops | bytes accessed | tf_op | source)
XLA Modules:
  0.0 97.1 jit_solution(11109582266516808291)
XLA Ops:
  0.6 0.9 constant_dynamic-update-slice_fusion.1
  1.5 0.9 constant_dynamic-update-slice_fusion.refs_0_.own.refs_1_
  2.5 2.2 %collective-permute-start.2 = (f32[16,32,128]{2,1,0:T(8,128)S(1)}, f32[16,32,128]{2,1,0:T(8,128)S(1)}, u32[]{:S(2)}, u32[]{:S(2)}) collective-permute-start(f32[16,32,128]{2,1,0:T(8,128)S(1)} %constant_dynamic-update-slice_fusion.refs_0_.own.refs_1_), channel_id=1, source_target_pairs={{3,0},{0,1},{1,2},{2,3},{7,4},{4,5},{5,6},{6,7},{11,8},{8,9},{9,10... | collective-permute-start | bytes 786440 | tf_op jit(solution)/shard_map/ppermute | solution.py:554
  4.7 2.6 %collective-permute-start.1 = (f32[16,32,128]{2,1,0:T(8,128)S(1)}, f32[16,32,128]{2,1,0:T(8,128)S(1)}, u32[]{:S(2)}, u32[]{:S(2)}) collective-permute-start(f32[16,32,128]{2,1,0:T(8,128)S(1)} %constant_dynamic-update-slice_fusion.refs_0_.own.refs_1_), channel_id=1, source_target_pairs={{2,0},{3,1},{0,2},{1,3},{6,4},{7,5},{4,6},{5,7},{10,8},{11,9},{8,1... | collective-permute-start | bytes 786440 | tf_op jit(solution)/shard_map/ppermute | solution.py:554
  7.3 1.1 %collective-permute-start = (f32[16,32,128]{2,1,0:T(8,128)S(1)}, f32[16,32,128]{2,1,0:T(8,128)S(1)}, u32[]{:S(2)}, u32[]{:S(2)}) collective-permute-start(f32[16,32,128]{2,1,0:T(8,128)S(1)} %constant_dynamic-update-slice_fusion.refs_0_.own.refs_1_), channel_id=1, source_target_pairs={{1,0},{2,1},{3,2},{0,3},{5,4},{6,5},{7,6},{4,7},{9,8},{10,9},{11,1... | collective-permute-start | bytes 786440 | tf_op jit(solution)/shard_map/ppermute | solution.py:554
  8.4 0.0 copy-start
  8.4 1.0 %copy-done = s32[3,8,32,128]{3,2,1,0:T(8,128)S(1)} copy-done((s32[3,8,32,128]{3,2,1,0:T(8,128)S(1)}, s32[3,8,32,128]{3,2,1,0:T(8,128)}, u32[]{:S(2)}) %copy-start) | copy-done | bytes 393240
  9.4 0.0 copy-start.1
  9.4 0.7 copy-done.1
  10.0 0.0 copy-start.2
  10.0 0.7 copy-done.2
  10.7 0.5 prepare.1
  11.2 1.3 %collective-permute-start.4 = (f32[8,128]{1,0:T(8,128)S(1)}, f32[8,128]{1,0:T(8,128)S(1)}, u32[]{:S(2)}, u32[]{:S(2)}) collective-permute-start(f32[8,128]{1,0:T(8,128)S(1)} %get-tuple-element.26.refs_4_), channel_id=1, source_target_pairs={{8,0},{12,4},{16,8},{20,12},{24,16},{28,20},{32,24},{36,28},{40,32... | collective-permute-start | bytes 12296 | tf_op jit(solution)/shard_map/ppermute | solution.py:544
  12.5 0.3 collective-permute-start.3
  12.8 3.2 %collective-permute-done.4.refs_6_ = f32[8,128]{1,0:T(8,128)S(1)} collective-permute-done((f32[8,128]{1,0:T(8,128)S(1)}, f32[8,128]{1,0:T(8,128)S(1)}, u32[]{:S(2)}, u32[]{:S(2)}) %collective-permute-start.4) | collective-permute-done | bytes 4128 | tf_op jit(solution)/shard_map/ppermute | solution.py:544
  16.0 2.7 %collective-permute-done.3.refs_5_ = f32[8,128]{1,0:T(8,128)S(1)} collective-permute-done((f32[8,128]{1,0:T(8,128)S(1)}, f32[8,128]{1,0:T(8,128)S(1)}, u32[]{:S(2)}, u32[]{:S(2)}) %collective-permute-start.3) | collective-permute-done | bytes 4128 | tf_op jit(solution)/shard_map/ppermute | solution.py:554
  18.7 0.0 collective-permute-done.2.refs_3_.three.refs_4_
  18.7 0.0 collective-permute-done.1.refs_2_.two.refs_3_
  18.7 0.0 collective-permute-done.refs_1_.one.refs_2_
  18.7 0.1 pack.1
  18.8 5.0 %collective-permute-start.5 = (f32[33,24,128]{2,1,0:T(8,128)S(1)}, f32[33,24,128]{2,1,0:T(8,128)S(1)}, u32[]{:S(2)}, u32[]{:S(2)}) collective-permute-start(f32[33,24,128]{2,1,0:T(8,128)S(1)} %get-tuple-element.27), channel_id=1, source_target_pairs={{4,8},{12,16},{20,24},{28,32},{36,40},{44,48},{52,56},{60,64},{68,... | collective-permute-start | bytes 1216520 | tf_op jit(solution)/shard_map/ppermute | solution.py:549
  23.8 0.1 collective-permute-start.6
  23.9 3.9 %collective-permute-start.7 = (f32[32,16,128]{2,1,0:T(8,128)S(1)}, f32[32,16,128]{2,1,0:T(8,128)S(1)}, u32[]{:S(2)}, u32[]{:S(2)}) collective-permute-start(f32[32,16,128]{2,1,0:T(8,128)S(1)} %get-tuple-element.31), channel_id=1, source_target_pairs={{4,8},{12,16},{20,24},{28,32},{36,40},{44,48},{52,56},{60,64},{68,... | collective-permute-start | bytes 786440 | tf_op jit(solution)/shard_map/ppermute | solution.py:549
  27.8 0.1 collective-permute-start.8
  27.9 1.5 %collective-permute-done.5.far = f32[33,24,128]{2,1,0:T(8,128)S(1)} collective-permute-done((f32[33,24,128]{2,1,0:T(8,128)S(1)}, f32[33,24,128]{2,1,0:T(8,128)S(1)}, u32[]{:S(2)}, u32[]{:S(2)}) %collective-permute-start.5) | collective-permute-done | bytes 405536 | tf_op jit(solution)/shard_map/ppermute | solution.py:549
  29.4 0.0 collective-permute-done.6.near
  29.4 4.4 %corners.1 = (f32[10,2,17,4,8,128]{5,4,3,2,1,0:T(8,128)S(1)}, f32[8,128]{1,0:T(8,128)S(1)}) custom-call(f32[16,32,128]{2,1,0:T(8,128)S(1)} %constant_dynamic-update-slice_fusion.refs_0_.own.refs_1_, f32[16,32,128]{2,1,0:T(8,128)S(1)} %collective-permute-done.refs_1_.one.refs_2_, f32[16,32,128]{2,1,0:T(8,128)S(1)} %collective-permute-done.1.refs_2_.two.refs_3_, ...), custom_call_target="tpu_custom_call" | custom-call | flops 10000000 | bytes 9000000 | tf_op jit(solution)/shard_map/corners/pallas_call | solution.py:257
  33.8 0.0 collective-permute-done.7.refs_5_
  33.8 0.0 collective-permute-done.8.refs_6_
  33.8 4.3 %iteration.3 = (f32[64,128]{1,0:T(8,128)S(1)}, f32[8,128]{1,0:T(8,128)S(1)}, f32[32,64,128]{2,1,0:T(8,128)S(1)}) custom-call(f32[8,128]{1,0:T(8,128)S(1)} %get-tuple-element.30.refs_0_, f32[16,32,128]{2,1,0:T(8,128)S(1)} %constant_dynamic-update-slice_fusion.refs_0_.own.refs_1_, f32[16,32,128]{2,1,0:T(8,128)S(1)} %collective-permute-done.refs_1_.one.refs_2_, ...), custom_call_target="tpu_custom_call" | custom-call | flops 20000000 | bytes 9000000 | tf_op jit(solution)/shard_map/iteration/pallas_call | solution.py:502
  38.1 22.0 %all_to_all.33 = f32[64,1,128]{2,1,0:T(1,128)S(1)} all-to-all(f32[64,1,128]{2,1,0:T(1,128)S(1)} %bitcast.18), channel_id=1, replica_groups=mesh['tile'=64,'depth'=4] {'tile'}, dimensions={0} | all-to-all | bytes 65536 | tf_op jit(solution)/shard_map/all_to_all | solution.py:579
  60.1 4.4 %iteration.4 = (f32[64,128]{1,0:T(8,128)S(1)}, f32[8,128]{1,0:T(8,128)S(1)}) custom-call(f32[8,128]{1,0:T(8,128)S(1)} %get-tuple-element.38.refs_0_, f32[64,128]{1,0:T(8,128)S(1)} %bitcast.13, f32[32,64,128]{2,1,0:T(8,128)S(1)} %get-tuple-element.40.refs_2_, f32[10,2,17,4,8,128]{5,4,3,2,1,0:T(8,128)S(1)} %get-tuple-element.33.refs_7_.refs_3_, ...), custom_call_target="tpu_custom_call" | custom-call | flops 20000000 | bytes 9000000 | tf_op jit(solution)/shard_map/iteration/pallas_call | solution.py:502
  64.5 13.3 %all_to_all.34 = f32[64,1,128]{2,1,0:T(1,128)S(1)} all-to-all(f32[64,1,128]{2,1,0:T(1,128)S(1)} %bitcast.20), channel_id=1, replica_groups=mesh['tile'=64,'depth'=4] {'tile'}, dimensions={0} | all-to-all | bytes 65536 | tf_op jit(solution)/shard_map/all_to_all | solution.py:579
  77.8 5.0 %iteration.5 = (f32[64,128]{1,0:T(8,128)S(1)}, f32[8,128]{1,0:T(8,128)S(1)}, f32[8,32,128]{2,1,0:T(8,128)}) custom-call(f32[8,128]{1,0:T(8,128)S(1)} %get-tuple-element.41.refs_0_, f32[64,128]{1,0:T(8,128)S(1)} %bitcast.15, f32[32,64,128]{2,1,0:T(8,128)S(1)} %get-tuple-element.40.refs_2_, f32[10,2,17,4,8,128]{5,4,3,2,1,0:T(8,128)S(1)} %get-tuple-element.33.refs_7_.refs_3_, ...), custom_call_target="tpu_custom_call" | custom-call | flops 20000000 | bytes 9000000 | tf_op jit(solution)/shard_map/iteration/pallas_call | solution.py:502
  82.8 13.3 %all_to_all.35 = f32[64,1,128]{2,1,0:T(1,128)S(1)} all-to-all(f32[64,1,128]{2,1,0:T(1,128)S(1)} %bitcast.19), channel_id=1, replica_groups=mesh['tile'=64,'depth'=4] {'tile'}, dimensions={0} | all-to-all | bytes 65536 | tf_op jit(solution)/shard_map/all_to_all | solution.py:579
  96.1 1.0 %finish.1 = (f32[3,32]{1,0:T(4,128)}, f32[1,3]{1,0:T(1,128)}) custom-call(f32[8,128]{1,0:T(8,128)S(1)} %get-tuple-element.43.motion, f32[64,128]{1,0:T(8,128)S(1)} %bitcast.14, f32[64,128]{1,0:T(8,128)S(1)} %bitcast.16, f32[64,128]{1,0:T(8,128)S(1)} %bitcast.17, f32[32,128]{1,0:T(8,128)S(1)} %get-tuple-element.45.chooser), custom_call_target="tpu_custom_call" | custom-call | tf_op jit(solution)/shard_map/finish/pallas_call | solution.py:531
Async XLA Ops:
  2.5 16.2 %collective-permute-start.2 = (f32[16,32,128]{2,1,0:T(8,128)S(1)}, f32[16,32,128]{2,1,0:T(8,128)S(1)}, u32[]{:S(2)}, u32[]{:S(2)}) collective-permute-start(f32[16,32,128]{2,1,0:T(8,128)S(1)} %constant_dynamic-update-slice_fusion.refs_0_.own.refs_1_), channel_id=1, source_target_pairs={{3,0},{0,1},{1,2},{2,3},{7,4},{4,5},{5,6},{6,7},{11,8},{8,9},{9,10... | collective-permute-start | bytes 786440 | tf_op jit(solution)/shard_map/ppermute | solution.py:554
  4.7 14.0 %collective-permute-start.1 = (f32[16,32,128]{2,1,0:T(8,128)S(1)}, f32[16,32,128]{2,1,0:T(8,128)S(1)}, u32[]{:S(2)}, u32[]{:S(2)}) collective-permute-start(f32[16,32,128]{2,1,0:T(8,128)S(1)} %constant_dynamic-update-slice_fusion.refs_0_.own.refs_1_), channel_id=1, source_target_pairs={{2,0},{3,1},{0,2},{1,3},{6,4},{7,5},{4,6},{5,7},{10,8},{11,9},{8,1... | collective-permute-start | bytes 786440 | tf_op jit(solution)/shard_map/ppermute | solution.py:554
  7.3 11.4 %collective-permute-start = (f32[16,32,128]{2,1,0:T(8,128)S(1)}, f32[16,32,128]{2,1,0:T(8,128)S(1)}, u32[]{:S(2)}, u32[]{:S(2)}) collective-permute-start(f32[16,32,128]{2,1,0:T(8,128)S(1)} %constant_dynamic-update-slice_fusion.refs_0_.own.refs_1_), channel_id=1, source_target_pairs={{1,0},{2,1},{3,2},{0,3},{5,4},{6,5},{7,6},{4,7},{9,8},{10,9},{11,1... | collective-permute-start | bytes 786440 | tf_op jit(solution)/shard_map/ppermute | solution.py:554
  8.4 1.0 %copy-start = (s32[3,8,32,128]{3,2,1,0:T(8,128)S(1)}, s32[3,8,32,128]{3,2,1,0:T(8,128)}, u32[]{:S(2)}) copy-start(s32[3,8,32,128]{3,2,1,0:T(8,128)} %offsets.1) | copy-start | bytes 1179652
  9.4 0.7 copy-start.1
  10.0 0.7 copy-start.2
  11.2 4.8 %collective-permute-start.4 = (f32[8,128]{1,0:T(8,128)S(1)}, f32[8,128]{1,0:T(8,128)S(1)}, u32[]{:S(2)}, u32[]{:S(2)}) collective-permute-start(f32[8,128]{1,0:T(8,128)S(1)} %get-tuple-element.26.refs_4_), channel_id=1, source_target_pairs={{8,0},{12,4},{16,8},{20,12},{24,16},{28,20},{32,24},{36,28},{40,32... | collective-permute-start | bytes 12296 | tf_op jit(solution)/shard_map/ppermute | solution.py:544
  12.5 6.2 %collective-permute-start.3 = (f32[8,128]{1,0:T(8,128)S(1)}, f32[8,128]{1,0:T(8,128)S(1)}, u32[]{:S(2)}, u32[]{:S(2)}) collective-permute-start(f32[8,128]{1,0:T(8,128)S(1)} %get-tuple-element.26.refs_4_), channel_id=1, source_target_pairs={{2,0},{3,1},{0,2},{1,3},{6,4},{7,5},{4,6},{5,7},{10,8},{11,9},{8,1... | collective-permute-start | bytes 12296 | tf_op jit(solution)/shard_map/ppermute | solution.py:554
  18.8 10.6 %collective-permute-start.5 = (f32[33,24,128]{2,1,0:T(8,128)S(1)}, f32[33,24,128]{2,1,0:T(8,128)S(1)}, u32[]{:S(2)}, u32[]{:S(2)}) collective-permute-start(f32[33,24,128]{2,1,0:T(8,128)S(1)} %get-tuple-element.27), channel_id=1, source_target_pairs={{4,8},{12,16},{20,24},{28,32},{36,40},{44,48},{52,56},{60,64},{68,... | collective-permute-start | bytes 1216520 | tf_op jit(solution)/shard_map/ppermute | solution.py:549
  23.8 5.6 %collective-permute-start.6 = (f32[33,24,128]{2,1,0:T(8,128)S(1)}, f32[33,24,128]{2,1,0:T(8,128)S(1)}, u32[]{:S(2)}, u32[]{:S(2)}) collective-permute-start(f32[33,24,128]{2,1,0:T(8,128)S(1)} %get-tuple-element.28), channel_id=1, source_target_pairs={{0,4},{8,12},{16,20},{24,28},{32,36},{40,44},{48,52},{56,60},{64,6... | collective-permute-start | bytes 1216520 | tf_op jit(solution)/shard_map/ppermute | solution.py:549
  23.9 9.9 %collective-permute-start.7 = (f32[32,16,128]{2,1,0:T(8,128)S(1)}, f32[32,16,128]{2,1,0:T(8,128)S(1)}, u32[]{:S(2)}, u32[]{:S(2)}) collective-permute-start(f32[32,16,128]{2,1,0:T(8,128)S(1)} %get-tuple-element.31), channel_id=1, source_target_pairs={{4,8},{12,16},{20,24},{28,32},{36,40},{44,48},{52,56},{60,64},{68,... | collective-permute-start | bytes 786440 | tf_op jit(solution)/shard_map/ppermute | solution.py:549
  27.8 6.0 %collective-permute-start.8 = (f32[32,16,128]{2,1,0:T(8,128)S(1)}, f32[32,16,128]{2,1,0:T(8,128)S(1)}, u32[]{:S(2)}, u32[]{:S(2)}) collective-permute-start(f32[32,16,128]{2,1,0:T(8,128)S(1)} %get-tuple-element.32), channel_id=1, source_target_pairs={{0,4},{8,12},{16,20},{24,28},{32,36},{40,44},{48,52},{56,60},{64,6... | collective-permute-start | bytes 786440 | tf_op jit(solution)/shard_map/ppermute | solution.py:549

commit v3 on v2

--- a/solution.py
+++ b/solution.py
@@ -26,6 +26,21 @@
     return jnp.dot(left, right, precision=highest, preferred_element_type=F32)
 
 
+def split(value, parts):
+    pieces = []
+    for _ in range(parts):
+        piece = value.astype(jnp.bfloat16)
+        pieces.append(piece)
+        value = value - piece.astype(F32)
+    return pieces
+
+
+def exact_dot(left, tables):
+    left = jnp.concatenate(split(left, 3) * len(tables), axis=1)
+    right = jnp.concatenate([table for table in tables for _ in range(3)], axis=0)
+    return jnp.dot(left, right, preferred_element_type=F32)
+
+
 def lane_ids(shape):
     return lax.broadcasted_iota(jnp.int32, shape, 1)
 
@@ -40,18 +55,9 @@
     return jnp.maximum(1.0 - jnp.abs(y - places) * (1.0 / ELEM), 0.0)
 
 
-def along_x_table():
-    shape = (FRAME, 64)
-    row = row_ids(shape).astype(F32) + (0.5 - HALO)
-    column = lane_ids(shape)
-    node = 2 * (column // 16 - 1) + column % 16 // 6
-    hats = jnp.maximum(1.0 - jnp.abs(row - (node * ELEM).astype(F32)) * (1.0 / ELEM), 0.0)
-    return [jnp.where((column % 16 < 12) & (column % 16 % 6 == n), hats, 0.0) for n in range(6)]
-
-
 def prepare_body(offsets, far_ids, far_motion, *refs):
-    lines, chooser, along_x, along_y, over_y, over_y2 = refs[:6]
-    held, node_ids, start_motion, sem = refs[6:]
+    lines, chooser, along_y, over_y, over_y2 = refs[:5]
+    held, node_ids, start_motion, sem = refs[5:]
     nodes = [
         pltpu.make_async_copy(far_ids, node_ids, sem.at[6]),
         pltpu.make_async_copy(far_motion, start_motion, sem.at[7]),
@@ -86,12 +92,10 @@
         jnp.where(component == row_ids((3, LANES)), taken, 0.0), axis=0, keepdims=True
     )
     square = (LANES, LANES)
-    along_y[...] = along_y_table(square, 0)
+    along_y[...] = along_y_table(square, 0).astype(jnp.bfloat16)
     table = along_y_table(square, 1)
-    over_y[...] = table
-    over_y2[...] = table * table
-    for n, hats in enumerate(along_x_table()):
-        along_x[n * FRAME : (n + 1) * FRAME] = hats
+    over_y[...] = table.astype(jnp.bfloat16)
+    over_y2[0], over_y2[1] = split(table * table, 2)
     lines[...] = jnp.broadcast_to(line, shape)
     for n, copy in enumerate(picked):
         copy.wait()
@@ -101,10 +105,12 @@
 def prepare(offsets, node_ids, start_motion):
     vmem = pl.BlockSpec(memory_space=pltpu.VMEM)
     outside = pl.BlockSpec(memory_space=pltpu.HBM)
-    shapes = ((8, LANES), (32, LANES), (6 * FRAME, 64)) + ((LANES, LANES),) * 3
+    shapes = [jax.ShapeDtypeStruct((n, LANES), F32) for n in (8, 32)]
+    for size in ((LANES, LANES), (LANES, LANES), (2, LANES, LANES)):
+        shapes.append(jax.ShapeDtypeStruct(size, jnp.bfloat16))
     return pl.pallas_call(
         prepare_body,
-        out_shape=[jax.ShapeDtypeStruct(shape, F32) for shape in shapes],
+        out_shape=shapes,
         in_specs=[outside] * 3,
         out_specs=[vmem] * len(shapes),
         scratch_shapes=[
@@ -120,17 +126,17 @@
 
 def pack_body(*refs):
     both = refs[:4]
-    lines, other, beyond, far, far_target, near, near_target, extra = refs[4:]
+    lines, other, beyond, far, far_target, near, extra = refs[4:]
     depth = lax.axis_index("depth")
     odd = lax.rem(lax.axis_index("tile"), 2)
-    for step in range(4):
+    far_rows = pl.ds(pl.multiple_of(8 * odd, 8), HALO)
+    near_rows = pl.ds(pl.multiple_of(8 * (1 - odd), 8), HALO)
+    for step, piece in enumerate(both):
         planes = pl.ds(lax.rem(depth + step, 4) * 8, 8)
-        for part, odds in ((far, odd), (near, 1 - odd)):
-            rows = pl.ds(pl.multiple_of(8 * odds, 8), HALO)
-            part[planes] = both[step][0:8, rows]
-        for part, odds in ((far_target, odd), (near_target, 1 - odd)):
-            rows = pl.ds(pl.multiple_of(16 * odds, 8), ELEM)
-            part[planes] = both[step][8:16, rows]
+        far[planes] = piece[0:8, far_rows]
+        near[planes, :HALO] = piece[0:8, near_rows]
+        far_target[planes] = piece[8:16, pl.ds(pl.multiple_of(ELEM * odd, 8), ELEM)]
+        near[planes, HALO:] = piece[8:16, pl.ds(pl.multiple_of(ELEM * (1 - odd), 8), ELEM)]
     upper = depth >= 2
     mine, given = lines[0:6], other[0:6]
     extra[...] = jnp.zeros_like(extra)
@@ -139,13 +145,17 @@
     extra[12:13] = lines[6:7]
     extra[13:14] = beyond[6:7]
     far[SLAB] = extra[...]
-    near[SLAB] = extra[...]
+    near[SLAB, :HALO] = extra[...]
+    near[SLAB, HALO:] = jnp.zeros((ELEM, LANES), F32)
 
 
 def pack(*args):
-    sides = (SLAB + 1, HALO, LANES)
-    target_sides = (SLAB, ELEM, LANES)
-    shapes = (sides, target_sides, sides, target_sides, (HALO, LANES))
+    shapes = (
+        (SLAB + 1, HALO, LANES),
+        (SLAB, ELEM, LANES),
+        (SLAB + 1, HALO + ELEM, LANES),
+        (HALO, LANES),
+    )
     vmem = pl.BlockSpec(memory_space=pltpu.VMEM)
     return pl.pallas_call(
         pack_body,
@@ -158,41 +168,49 @@
     )(*args)
 
 
-def corner_body(tiles, own, one, two, three, far, near, extra, *refs):
-    chunk, motion, source, shifted, table = refs
+def near_base(odd):
+    return 4 * (1 - odd)
+
+
+def far_base(odd):
+    return 6 * odd
+
+
+def corner_body(tiles, is_far, own, one, two, three, part, *refs):
+    if is_far:
+        near, extra, chunk, motion, source, shifted, table = refs
+    else:
+        extra, chunk, source, shifted, table = refs
     tile = lax.axis_index("tile")
     depth = lax.axis_index("depth")
     odd = lax.rem(tile, 2)
-    motion[...] = jnp.zeros_like(motion)
-    motion[1:2] = extra[12:13]
-    motion[3:4] = extra[13:14]
-    motion[pl.ds(2 * odd, 1)] = far[SLAB, 12:13]
-    motion[pl.ds(2 - 2 * odd, 1)] = near[SLAB, 12:13]
-    zero = jnp.zeros((2, FRAME + 16, LANES), F32)
-    source[0:2] = zero
-    source[SLAB + 2 : SLAB + 4] = zero
-    edge = jnp.zeros((SLAB, 8, LANES), F32)
-    source[2 : SLAB + 2, 0:8] = edge
-    source[2 : SLAB + 2, 8 + FRAME : 16 + FRAME] = edge
-    for part, right in ((far, odd), (near, 1 - odd)):
-        rows = pl.ds(pl.multiple_of(8 + (HALO + ROWS) * right, 8), HALO)
-        source[2 : SLAB + 2, rows] = part[0:SLAB]
+    if is_far:
+        motion[...] = jnp.zeros_like(motion)
+        motion[1:2] = extra[12:13]
+        motion[3:4] = extra[13:14]
+        motion[pl.ds(2 * odd, 1)] = part[SLAB, 12:13]
+        motion[pl.ds(2 - 2 * odd, 1)] = near[SLAB, 12:13]
+    right = odd if is_far else 1 - odd
+    base = far_base(odd) if is_far else near_base(odd)
+    rows = pl.ds(pl.multiple_of(8 + (HALO + ROWS) * right, 8), HALO)
+    source[:, rows] = part[0:SLAB, :HALO]
     for step, piece in enumerate((own, one, two, three)):
         start = lax.rem(depth + step, 4) * 8
-        source[pl.ds(start + 2, 8), 8 + HALO : 8 + HALO + ROWS] = piece[0:8]
+        source[pl.ds(start, 8), 8 + HALO : 8 + HALO + ROWS] = piece[0:8]
     for e in range(2):
         for c in range(3):
             for which in range(2):
                 at = e * 6 + c * 2 + which
                 row = (e * 6 + which) * 3 + c
                 table[row + 6 : row + 7] = extra[at : at + 1]
-                table[pl.ds(row + 12 * odd, 1)] = far[SLAB, at : at + 1]
-                table[pl.ds(row + 12 - 12 * odd, 1)] = near[SLAB, at : at + 1]
+                table[pl.ds(row + 12 * right, 1)] = part[SLAB, at : at + 1]
 
     shape = (8, LANES)
     lanes = lane_ids(shape)
-
-    def group(v, carry):
+    zeros = jnp.zeros(shape, F32)
+
+    def group(number, carry):
+        v = base + number
         ex = (v + 1) // 2
         outside = ((tile == 0) & (v < 3)) | ((tile == tiles - 1) & (v >= 7))
         inside = jnp.where(outside, 0.0, 1.0).astype(F32)
@@ -200,76 +218,77 @@
             offs = [
                 jnp.broadcast_to(table[pl.ds((e * 6 + ex) * 3 + c, 1)], shape) for c in range(3)
             ]
-            base = lanes + offs[2].astype(jnp.int32)
+            reach = lanes + offs[2].astype(jnp.int32)
             picks = []
             for s in range(2):
-                at = base + s
+                at = reach + s
                 good = jnp.where((at >= 0) & (at < LANES), inside, 0.0)
                 picks.append((jnp.clip(at, 0, LANES - 1), good))
+            is_x = [offs[1] == float(o) for o in (-2, -1, 0)]
+            odd_z = (offs[0] == -1.0) | (offs[0] == 1.0)
+            high_z = offs[0] >= 0.0
+            planes = []
+            steps = []
             for p in range(20):
-                for half in range(2):
-                    block = source[16 * e + p, pl.ds(8 * v + 6 + 4 * half, 8)]
-                    for s in range(2):
-                        index, good = picks[s]
-                        taken = jnp.take_along_axis(block, index, axis=1, mode="promise_in_bounds")
-                        shifted[s, p, 4 * half : 4 * half + 8] = taken * good
-            is_x = [offs[1] == float(o) for o in (-2, -1, 0)]
-            is_z = [offs[0] == float(o) for o in (-2, -1, 0)]
-            window = []
-            for p in range(20):
-                corners = []
-                for sx in range(2):
-                    for sy in range(2):
-                        rows = [shifted[sy, p, sx + o : sx + o + 8] for o in range(4)]
-                        corners.append(
-                            jnp.where(
-                                is_x[0],
-                                rows[0],
-                                jnp.where(is_x[1], rows[1], jnp.where(is_x[2], rows[2], rows[3])),
+                z = 16 * e + p - 2
+                corners = [zeros] * 4
+                if 0 <= z < SLAB:
+                    for half in range(2):
+                        block = source[z, pl.ds(8 * v + 6 + 4 * half, 8)]
+                        for s in range(2):
+                            index, good = picks[s]
+                            taken = jnp.take_along_axis(
+                                block, index, axis=1, mode="promise_in_bounds"
                             )
-                        )
-                window.append(corners)
+                            shifted[e, s, p, 4 * half : 4 * half + 8] = taken * good
+                    corners = []
+                    for sx in range(2):
+                        for sy in range(2):
+                            rows = [shifted[e, sy, p, sx + o : sx + o + 8] for o in range(4)]
+                            corners.append(
+                                jnp.where(
+                                    is_x[0],
+                                    rows[0],
+                                    jnp.where(
+                                        is_x[1], rows[1], jnp.where(is_x[2], rows[2], rows[3])
+                                    ),
+                                )
+                            )
+                planes.append(corners)
+                if p >= 1:
+                    steps.append(
+                        [jnp.where(odd_z, planes[p][n], planes[p - 1][n]) for n in range(4)]
+                    )
                 if p >= 3:
                     c00, c01, c10, c11 = [
-                        jnp.where(
-                            is_z[0],
-                            window[p - 3][n],
-                            jnp.where(
-                                is_z[1],
-                                window[p - 2][n],
-                                jnp.where(is_z[2], window[p - 1][n], window[p][n]),
-                            ),
-                        )
-                        for n in range(4)
+                        jnp.where(high_z, steps[p - 1][n], steps[p - 3][n]) for n in range(4)
                     ]
-                    chunk[v, e, p - 3, 0] = c00
-                    chunk[v, e, p - 3, 1] = c01 - c00
-                    chunk[v, e, p - 3, 2] = c10 - c00
-                    chunk[v, e, p - 3, 3] = (c11 - c10) - (c01 - c00)
+                    along = c01 - c00
+                    chunk[number, e, p - 3, 0] = c00
+                    chunk[number, e, p - 3, 1] = along
+                    chunk[number, e, p - 3, 2] = c10 - c00
+                    chunk[number, e, p - 3, 3] = (c11 - c10) - along
         return carry
 
-    lax.fori_loop(0, GROUPS, group, 0)
-
-
-def corner_images(tiles, *args):
+    lax.fori_loop(0, chunk.shape[0], group, 0)
+
+
+def corner_images(tiles, is_far, *args):
     vmem = pl.BlockSpec(memory_space=pltpu.VMEM)
-    shape = (GROUPS, 2, 17, 4, 8, LANES)
+    shapes = [(4 if is_far else 6, 2, 17, 4, 8, LANES)] + ([(8, LANES)] if is_far else [])
     return pl.pallas_call(
-        functools.partial(corner_body, tiles),
-        out_shape=[
-            jax.ShapeDtypeStruct(size, F32)
-            for size in (shape, (8, LANES))
-        ],
+        functools.partial(corner_body, tiles, is_far),
+        out_shape=[jax.ShapeDtypeStruct(shape, F32) for shape in shapes],
         in_specs=[vmem] * len(args),
-        out_specs=[vmem] * 2,
+        out_specs=[vmem] * len(shapes),
         scratch_shapes=[
-            pltpu.VMEM((SLAB + 4, FRAME + 16, LANES), F32),
-            pltpu.VMEM((2, 20, 16, LANES), F32),
+            pltpu.VMEM((SLAB, FRAME + 16, LANES), F32),
+            pltpu.VMEM((2, 2, 20, 16, LANES), F32),
             pltpu.VMEM((40, LANES), F32),
         ],
-        cost_estimate=pl.CostEstimate(flops=10000000, bytes_accessed=9000000, transcendentals=0),
-        name="corners",
-        compiler_params=pltpu.CompilerParams(vmem_limit_bytes=12 * 2**20),
+        cost_estimate=pl.CostEstimate(flops=5000000, bytes_accessed=4000000, transcendentals=0),
+        name="corners_far" if is_far else "corners_near",
+        compiler_params=pltpu.CompilerParams(vmem_limit_bytes=8 * 2**20),
     )(*args)
 
 
@@ -293,23 +312,25 @@
         pieces, refs = refs[:6], refs[6:]
     else:
         target = refs.pop(0)
-    cors, along_x, along_y, over_y, over_y2, block_out, motion_out = refs[:7]
+    near_cors, far_cors, along_y, over_y, over_y2, block_out, motion_out = refs[:7]
     refs = refs[7:]
     if first:
         target = refs.pop(0)
     residual_out = refs.pop(0) if last else None
-    wide, warped, slopes, layers, rows_f, rows_s, padded = refs[:7]
-    residuals = refs[7] if last else None
+    wide, ends, warped, slopes, layers, rows_f, rows_s, padded = refs[:8]
+    residuals = refs[8] if last else None
 
     tile = lax.axis_index("tile")
+    odd = lax.rem(tile, 2)
     if first:
         depth = lax.axis_index("depth")
-        odd = lax.rem(tile, 2)
         for step, piece in enumerate(pieces[:4]):
             start = lax.rem(depth + step, 4) * 8
             target[pl.ds(start, 8), ELEM : ELEM + ROWS] = piece[8:16]
-        for part, right in ((pieces[4], odd), (pieces[5], 1 - odd)):
-            target[:, pl.ds(pl.multiple_of((ELEM + ROWS) * right, 8), ELEM)] = part[...]
+        far = pl.ds(pl.multiple_of((ELEM + ROWS) * odd, 8), ELEM)
+        near = pl.ds(pl.multiple_of((ELEM + ROWS) * (1 - odd), 8), ELEM)
+        target[:, far] = pieces[4][...]
+        target[:, near] = pieces[5][0:SLAB, HALO:]
     low_flag = jnp.where(tile > 0, 1.0, 0.0).astype(F32)
     high_flag = jnp.where(tile < tiles - 1, 1.0, 0.0).astype(F32)
     now = motion[...] if first else updated_motion(motion, received, tile, tiles, padded)
@@ -319,16 +340,27 @@
     spread = jnp.concatenate(
         [jnp.where(pick, jnp.broadcast_to(now[n : n + 1], shape16), 0.0) for n in range(4)], axis=0
     )
-    wide[...] = dot(along_x[...], dot(spread, along_y[...]))
+    wide[...] = exact_dot(spread, [along_y[...]])
 
     zero = jnp.zeros((2, FRAME, LANES), F32)
     warped[0:2] = zero
     warped[SLAB + 2 : SLAB + 4] = zero
 
-    def warp(v, carry):
+    shares = (row_ids((8, LANES)).astype(F32) + 0.5) * (1.0 / ELEM)
+    for v in range(GROUPS):
+        node = (v + 1) // 2
+        lower = 16 * (node // 2) + 6 * (node % 2)
+        upper = 16 * ((node + 1) // 2) + 6 * ((node + 1) % 2)
+        share = shares + 0.5 * ((v + 1) % 2)
+        for n in range(6):
+            begin = wide[lower + n : lower + n + 1]
+            ends[v, n] = begin + share * (wide[upper + n : upper + n + 1] - begin)
+
+    def warp(cors, base, number, carry):
+        v = base + number
         at = pl.ds(pl.multiple_of(8 * v, 8), 8)
-        near = [wide[pl.ds(pl.multiple_of(2 * c * FRAME + 8 * v, 8), 8)] for c in range(3)]
-        far = [wide[pl.ds(pl.multiple_of((2 * c + 1) * FRAME + 8 * v, 8), 8)] for c in range(3)]
+        near = [ends[v, 2 * c] for c in range(3)]
+        far = [ends[v, 2 * c + 1] for c in range(3)]
         for e in range(2):
             if e == 0:
                 move = [n + (f - n) * (1.0 / 32) for n, f in zip(near, far)]
@@ -336,9 +368,9 @@
             else:
                 move = [f * (31.0 / 32) for f in far]
                 gain = [f * (-1.0 / 16) for f in far]
-            plane = [cors[v, e, 0, n] for n in range(4)]
+            plane = [cors[number, e, 0, n] for n in range(4)]
             for j in range(16):
-                above = [cors[v, e, j + 1, n] for n in range(4)]
+                above = [cors[number, e, j + 1, n] for n in range(4)]
                 mz, mx, my = move
                 here = (plane[0] + my * plane[1]) + mx * (plane[2] + my * plane[3])
                 there = (above[0] + my * above[1]) + mx * (above[2] + my * above[3])
@@ -348,7 +380,8 @@
                     move = [m + g for m, g in zip(move, gain)]
         return carry
 
-    lax.fori_loop(0, GROUPS, warp, 0)
+    lax.fori_loop(0, 6, functools.partial(warp, near_cors, near_base(odd)), 0)
+    lax.fori_loop(0, 4, functools.partial(warp, far_cors, far_base(odd)), 0)
 
     shape = (8, LANES)
     lanes = lane_ids(shape)
@@ -368,6 +401,7 @@
             second_sum = [zeros] * 3
             squares_0 = [zeros] * 3
             squares_1 = [zeros] * 3
+            squares_2 = [zeros] * 3
             for j in range(16):
                 z = 16 * e + j
                 planes.append(warped[z + 4, at])
@@ -395,16 +429,21 @@
                     first_sum[c] = first_sum[c] + three[c] * residual
                     second_sum[c] = second_sum[c] + first_sum[c]
                     square = three[c] * three[c]
-                    squares_0[c] = squares_0[c] + (weight * weight) * square
                     if e == 0:
-                        squares_1[c] = squares_1[c] + ((1.0 - weight) ** 2) * square
+                        squares_0[c] = squares_0[c] + square
+                        squares_1[c] = squares_1[c] + squares_0[c]
+                        squares_2[c] = squares_2[c] + squares_1[c]
+                    else:
+                        squares_0[c] = squares_0[c] + (weight * weight) * square
             for c in range(3):
                 falling = (second_sum[c] - 0.5 * first_sum[c]) * (1.0 / 16)
                 if e == 0:
                     layers[v - 1, 2 * c] = falling
                     layers[v - 1, 2 * c + 1] = first_sum[c] - falling
-                    layers[v - 1, 6 + 2 * c] = squares_0[c]
-                    layers[v - 1, 6 + 2 * c + 1] = squares_1[c]
+                    line = (squares_1[c] - 0.5 * squares_0[c]) * (1.0 / 16)
+                    both = (squares_2[c] - squares_1[c]) * (1.0 / 128) + squares_0[c] * (1.0 / 1024)
+                    layers[v - 1, 6 + 2 * c] = both
+                    layers[v - 1, 6 + 2 * c + 1] = (squares_0[c] - 2.0 * line) + both
                 else:
                     layers[v - 1, 2 * c + 1] += falling
                     layers[v - 1, 6 + 2 * c + 1] += squares_0[c]
@@ -414,6 +453,11 @@
     misfit = lax.fori_loop(3, 7, lambda v, m: slope_group(v, True, m), zeros)
     lax.fori_loop(7, 9, lambda v, m: slope_group(v, False, m), zeros)
 
+    if last:
+        leaving = pltpu.make_async_copy(
+            residuals.at[pl.ds(lax.axis_index("depth") * 8, 8)], residual_out, refs[9].at[0]
+        )
+        leaving.start()
     rows_f[...] = jnp.zeros_like(rows_f)
     rows_s[...] = jnp.zeros_like(rows_s)
     rows8 = row_ids((8, 1)).astype(F32)
@@ -432,8 +476,8 @@
             at = k * 6 + n
             rows_f[at : at + 1] = jnp.sum(sums[n], axis=0, keepdims=True)
             rows_s[at : at + 1] = jnp.sum(sums[6 + n], axis=0, keepdims=True)
-    force = dot(rows_f[...], over_y[...]) * (1.0 / 12)
-    stiffness = dot(rows_s[...], over_y2[...]) * (1.0 / 144)
+    force = exact_dot(rows_f[...], [over_y[...]]) * (1.0 / 12)
+    stiffness = exact_dot(rows_s[...], [over_y2[0], over_y2[1]]) * (1.0 / 144)
     shape24 = (24, LANES)
     rows24 = row_ids(shape24)
     lanes24 = lane_ids(shape24)
@@ -443,7 +487,7 @@
     owned = jnp.where(rows24 < 12, held, 0.0)
     descent = jnp.sum(force * owned)
     length = jnp.sum(owned * owned)
-    rows_f[...] = dot(held, along_y[...])
+    rows_f[...] = exact_dot(held, [along_y[...]])
     curved = zeros
     for v in range(3, 7):
         k = (v - 3) // 2
@@ -459,13 +503,15 @@
                 move = [field[2 * c] + (field[2 * c + 1] - field[2 * c]) * (1.0 / 32) for c in range(3)]
                 gain = [(field[2 * c + 1] - field[2 * c]) * (1.0 / 16) for c in range(3)]
             else:
-                move = [field[2 * c + 1] * (31.0 / 32) for c in range(3)]
-                gain = [field[2 * c + 1] * (-1.0 / 16) for c in range(3)]
+                move = [field[2 * c + 1] for c in range(3)]
             for j in range(16):
                 three = [slopes[c, 16 * e + j, row : row + 8] for c in range(3)]
                 projected = (three[0] * move[0] + three[1] * move[1]) + three[2] * move[2]
-                curved = curved + projected * projected
-                if j < 15:
+                projected = projected * projected
+                if e == 1:
+                    projected = projected * (1.0 - (j + 0.5) / 16.0) ** 2
+                curved = curved + projected
+                if e == 0 and j < 15:
                     move = [m + g for m, g in zip(move, gain)]
     curvature = jnp.sum(curved) * (1.0 / 144)
     misfit = jnp.sum(misfit)
@@ -475,18 +521,19 @@
         line = jnp.where(line_lanes == at, value, line)
     block_out[...] = jnp.broadcast_to(line, (tiles, LANES))
     if last:
-        residual_out[...] = residuals[pl.ds(lax.axis_index("depth") * 8, 8)]
-
-
-def iteration(tiles, first, last, motion, received, target, cor, tables):
+        leaving.wait()
+
+
+def iteration(tiles, first, last, motion, received, target, cors, tables):
     vmem = pl.BlockSpec(memory_space=pltpu.VMEM)
-    args = [motion] + ([] if first else [received]) + [*target, cor, *tables]
+    args = [motion] + ([] if first else [received]) + [*target, *cors, *tables]
     shapes = [
         jax.ShapeDtypeStruct((tiles, LANES), F32),
         jax.ShapeDtypeStruct((8, LANES), F32),
     ]
     scratch = [
-        pltpu.VMEM((6 * FRAME, LANES), F32),
+        pltpu.VMEM((64, LANES), F32),
+        pltpu.VMEM((GROUPS, 6, 8, LANES), F32),
         pltpu.VMEM((SLAB + 4, FRAME, LANES), F32),
         pltpu.VMEM((3, SLAB, ROWS, LANES), F32),
         pltpu.VMEM((8, 12, 8, LANES), F32),
@@ -499,11 +546,15 @@
     if last:
         shapes.append(jax.ShapeDtypeStruct((8, ROWS, LANES), F32))
         scratch.append(pltpu.VMEM((SLAB, ROWS, LANES), F32))
+        scratch.append(pltpu.SemaphoreType.DMA((1,)))
+    out_specs = [vmem] * len(shapes)
+    if last:
+        out_specs[-1] = pl.BlockSpec(memory_space=pltpu.HBM)
     return pl.pallas_call(
         functools.partial(iteration_body, tiles, first, last),
         out_shape=shapes,
         in_specs=[vmem] * len(args),
-        out_specs=[vmem] * len(shapes),
+        out_specs=out_specs,
         scratch_shapes=scratch,
         cost_estimate=pl.CostEstimate(flops=20000000, bytes_accessed=9000000, transcendentals=0),
         name="iteration",
@@ -556,23 +607,26 @@
 
 def local(reference_image, deformed_image, offsets, node_ids, start_motion):
     tiles = lax.axis_size("tile")
-    both = jnp.concatenate([deformed_image, reference_image], axis=0)
+    zero = jnp.zeros((), F32)
+    both = lax.pad(deformed_image, zero, ((0, 8, 0), (0, 0, 0), (0, 0, 0)))
+    both = both + lax.pad(reference_image, zero, ((8, 0, 0), (0, 0, 0), (0, 0, 0)))
     both = [both] + [ring(both, n) for n in (1, 2, 3)]
     lines, chooser, *tables = prepare(offsets, node_ids, start_motion)
     other = ring(lines, 2)
     beyond = from_behind(lines, "tile", -2)
-    far, far_target, near, near_target, extra = pack(*both, lines, other, beyond)
+    far, far_target, near, extra = pack(*both, lines, other, beyond)
     far = swap(far, 1)
     near = swap(near, 0)
     far_target = swap(far_target, 1)
-    near_target = swap(near_target, 0)
-    cor, motion = corner_images(tiles, *both, far, near, extra)
-    target = (*both, far_target, near_target)
+    (near_cors,) = corner_images(tiles, False, *both, near, extra)
+    far_cors, motion = corner_images(tiles, True, *both, far, near, extra)
+    cors = (near_cors, far_cors)
+    target = (*both, far_target, near)
     received = None
     got = []
     for number in range(ITERS):
         first, last = number == 0, number == ITERS - 1
-        outs = iteration(tiles, first, last, motion, received, target, cor, tables)
+        outs = iteration(tiles, first, last, motion, received, target, cors, tables)
         block, motion = outs[:2]
         if first:
             target = (outs[2],)

time: 97.5 us -> 93.2 us (0.956)
  Pallas kernels: 19.6 us -> 16.8 us
  starting transfers between devices: 16.6 us -> 14.7 us
  local copies, waits for them, and re-layouts: 4.19 us -> 2.36 us
  other arithmetic: 0 us -> 0.99 us
    pallas_call x3, Pallas kernels: 13.7 us -> 11.2 us  [iteration(): pl.pallas_call(functools.partial(iteration_body, tiles, first, last), out...]
    ppermute x4 -> x3, starting transfers between devices: 9.08 us -> 7.18 us  [swap(): return lax.ppermute(block, 'tile', pairs + [(j, i) for i, j in pairs])]
    add x0 -> x1, other arithmetic: none -> 0.99 us  [local(): both + lax.pad(reference_image, zero, ((8, 0, 0), (0, 0, 0), (0, 0, 0)))]
    ppermute x4 -> x3, waiting for transfers between devices: 1.46 us -> 2.45 us  [swap(): return lax.ppermute(block, 'tile', pairs + [(j, i) for i, j in pairs])]
    unnamed x7 -> x6, local copies, waits for them, and re-layouts: 3.27 us -> 2.36 us
    pallas_call x2 -> x3, Pallas kernels: 4.83 us -> 4.46 us  [the longest x2 3.99 us: corner_images(): pl.pallas_call(functools.partial(corner_body, tiles, is_far), out_shape=[...]
  transfers between devices with their start and end apart: 9 -> 8, of which waited for: 3 -> 4; matrix products, arithmetic and copies ran while one was open for 0% -> 0% of each run, Pallas kernels for 5% -> 5%
where the time goes in v3:
time: 93.2 us; the launch traced here: 92.9 us
  blocking collectives  49 us (53%)
  Pallas kernels  16.8 us (18%)
  starting transfers between devices  14.7 us (16%)
  waiting for transfers between devices  8.35 us (9%)
  local copies, waits for them, and re-layouts  2.36 us (3%)
  other arithmetic  0.99 us (1%)
    all_to_all x3, blocking collectives, local(): received = lax.all_to_all(block, 'tile', 0, 0, tiled=True)  49 us
    pallas_call x3, Pallas kernels, iteration(): pl.pallas_call(functools.partial(iteration_body, tiles, first, last), out...  11.2 us
    ppermute x3, starting transfers between devices, swap(): return lax.ppermute(block, 'tile', pairs + [(j, i) for i, j in pairs])  7.18 us
    ppermute x4, starting transfers between devices, ring(): lax.ppermute(block, 'depth', [((i + distance) % peers, i) for i in range(...  6.19 us
    pallas_call x2, Pallas kernels, corner_images(): pl.pallas_call(functools.partial(corner_body, tiles, is_far), out_shape=[...  3.99 us
    ppermute x1, waiting for transfers between devices, from_behind(): lax.ppermute(block, axis, [(i - distance, i) for i in devices if i - dist...  3.23 us
    ppermute x4, waiting for transfers between devices, ring(): lax.ppermute(block, 'depth', [((i + distance) % peers, i) for i in range(...  2.68 us
    ppermute x3, waiting for transfers between devices, swap(): return lax.ppermute(block, 'tile', pairs + [(j, i) for i, j in pairs])  2.45 us
  transfers between devices with their start and end apart: 8, of which 4 were waited for; matrix products, arithmetic and copies ran while one was open for 0% of the time, Pallas kernels for 5%

profile of v3, /device:TPU:1, one launch (start us, length us, event | category | flops | bytes accessed | tf_op | source)
XLA Modules:
  0.0 92.9 jit_solution(9073904071545647603)
XLA Ops:
  0.6 1.0 %pad_add_fusion.refs_0_.own.refs_1_ = f32[16,32,128]{2,1,0:T(8,128)S(1)} fusion(f32[8,32,128]{2,1,0:T(8,128)} %param.5, f32[8,32,128]{2,1,0:T(8,128)} %param.6), kind=kLoop, calls=%fused_computation | loop fusion | flops 65536 | bytes 524288 | tf_op jit(solution)/shard_map/add | solution.py:612
  1.6 2.2 %collective-permute-start.2 = (f32[16,32,128]{2,1,0:T(8,128)S(1)}, f32[16,32,128]{2,1,0:T(8,128)S(1)}, u32[]{:S(2)}, u32[]{:S(2)}) collective-permute-start(f32[16,32,128]{2,1,0:T(8,128)S(1)} %pad_add_fusion.refs_0_.own.refs_1_), channel_id=1, source_target_pairs={{3,0},{0,1},{1,2},{2,3},{7,4},{4,5},{5,6},{6,7},{11,8},{8,9},{9,10... | collective-permute-start | bytes 786440 | tf_op jit(solution)/shard_map/ppermute | solution.py:605
  3.8 2.6 %collective-permute-start.1 = (f32[16,32,128]{2,1,0:T(8,128)S(1)}, f32[16,32,128]{2,1,0:T(8,128)S(1)}, u32[]{:S(2)}, u32[]{:S(2)}) collective-permute-start(f32[16,32,128]{2,1,0:T(8,128)S(1)} %pad_add_fusion.refs_0_.own.refs_1_), channel_id=1, source_target_pairs={{2,0},{3,1},{0,2},{1,3},{6,4},{7,5},{4,6},{5,7},{10,8},{11,9},{8,1... | collective-permute-start | bytes 786440 | tf_op jit(solution)/shard_map/ppermute | solution.py:605
  6.4 1.1 %collective-permute-start = (f32[16,32,128]{2,1,0:T(8,128)S(1)}, f32[16,32,128]{2,1,0:T(8,128)S(1)}, u32[]{:S(2)}, u32[]{:S(2)}) collective-permute-start(f32[16,32,128]{2,1,0:T(8,128)S(1)} %pad_add_fusion.refs_0_.own.refs_1_), channel_id=1, source_target_pairs={{1,0},{2,1},{3,2},{0,3},{5,4},{6,5},{7,6},{4,7},{9,8},{10,9},{11,1... | collective-permute-start | bytes 786440 | tf_op jit(solution)/shard_map/ppermute | solution.py:605
  7.5 0.0 copy-start
  7.5 1.0 %copy-done = s32[3,8,32,128]{3,2,1,0:T(8,128)S(1)} copy-done((s32[3,8,32,128]{3,2,1,0:T(8,128)S(1)}, s32[3,8,32,128]{3,2,1,0:T(8,128)}, u32[]{:S(2)}) %copy-start) | copy-done | bytes 393240
  8.5 0.0 copy-start.1
  8.5 0.7 copy-done.1
  9.2 0.0 copy-start.2
  9.2 0.7 copy-done.2
  9.9 0.5 prepare.1
  10.4 1.3 %collective-permute-start.4 = (f32[8,128]{1,0:T(8,128)S(1)}, f32[8,128]{1,0:T(8,128)S(1)}, u32[]{:S(2)}, u32[]{:S(2)}) collective-permute-start(f32[8,128]{1,0:T(8,128)S(1)} %get-tuple-element.24.refs_4_), channel_id=1, source_target_pairs={{8,0},{12,4},{16,8},{20,12},{24,16},{28,20},{32,24},{36,28},{40,32... | collective-permute-start | bytes 12296 | tf_op jit(solution)/shard_map/ppermute | solution.py:595
  11.7 0.3 collective-permute-start.3
  12.0 3.2 %collective-permute-done.4.refs_6_ = f32[8,128]{1,0:T(8,128)S(1)} collective-permute-done((f32[8,128]{1,0:T(8,128)S(1)}, f32[8,128]{1,0:T(8,128)S(1)}, u32[]{:S(2)}, u32[]{:S(2)}) %collective-permute-start.4) | collective-permute-done | bytes 4128 | tf_op jit(solution)/shard_map/ppermute | solution.py:595
  15.2 2.7 %collective-permute-done.3.refs_5_ = f32[8,128]{1,0:T(8,128)S(1)} collective-permute-done((f32[8,128]{1,0:T(8,128)S(1)}, f32[8,128]{1,0:T(8,128)S(1)}, u32[]{:S(2)}, u32[]{:S(2)}) %collective-permute-start.3) | collective-permute-done | bytes 4128 | tf_op jit(solution)/shard_map/ppermute | solution.py:605
  17.9 0.0 collective-permute-done.2.refs_3_.three.refs_4_
  17.9 0.0 collective-permute-done.1.refs_2_.two.refs_3_
  17.9 0.0 collective-permute-done.refs_1_.one.refs_2_
  17.9 0.1 pack.1
  18.0 1.6 %collective-permute-start.6 = (f32[33,40,128]{2,1,0:T(8,128)S(1)}, f32[33,40,128]{2,1,0:T(8,128)S(1)}, u32[]{:S(2)}, u32[]{:S(2)}) collective-permute-start(f32[33,40,128]{2,1,0:T(8,128)S(1)} %get-tuple-element.26), channel_id=1, source_target_pairs={{0,4},{8,12},{16,20},{24,28},{32,36},{40,44},{48,52},{56,60},{64,6... | collective-permute-start | bytes 2027528 | tf_op jit(solution)/shard_map/ppermute | solution.py:600
  19.6 3.4 %collective-permute-start.5 = (f32[33,24,128]{2,1,0:T(8,128)S(1)}, f32[33,24,128]{2,1,0:T(8,128)S(1)}, u32[]{:S(2)}, u32[]{:S(2)}) collective-permute-start(f32[33,24,128]{2,1,0:T(8,128)S(1)} %get-tuple-element.25), channel_id=1, source_target_pairs={{4,8},{12,16},{20,24},{28,32},{36,40},{44,48},{52,56},{60,64},{68,... | collective-permute-start | bytes 1216520 | tf_op jit(solution)/shard_map/ppermute | solution.py:600
  23.1 2.1 %collective-permute-start.7 = (f32[32,16,128]{2,1,0:T(8,128)S(1)}, f32[32,16,128]{2,1,0:T(8,128)S(1)}, u32[]{:S(2)}, u32[]{:S(2)}) collective-permute-start(f32[32,16,128]{2,1,0:T(8,128)S(1)} %get-tuple-element.29), channel_id=1, source_target_pairs={{4,8},{12,16},{20,24},{28,32},{36,40},{44,48},{52,56},{60,64},{68,... | collective-permute-start | bytes 786440 | tf_op jit(solution)/shard_map/ppermute | solution.py:600
  25.2 0.0 collective-permute-done.6.refs_0_.part.refs_6_
  25.2 2.4 %corners_near.1.refs_7_.refs_3_ = f32[6,2,17,4,8,128]{5,4,3,2,1,0:T(8,128)S(1)} custom-call(f32[16,32,128]{2,1,0:T(8,128)S(1)} %pad_add_fusion.refs_0_.own.refs_1_, f32[16,32,128]{2,1,0:T(8,128)S(1)} %collective-permute-done.refs_1_.one.refs_2_, f32[16,32,128]{2,1,0:T(8,128)S(1)} %collective-permute-done.1.refs_2_.two.refs_3_, ...), custom_call_target="tpu_custom_call" | custom-call | flops 5000000 | bytes 4000000 | tf_op jit(solution)/shard_map/corners_near/pallas_call | solution.py:279
  27.6 1.3 %collective-permute-done.5.part = f32[33,24,128]{2,1,0:T(8,128)S(1)} collective-permute-done((f32[33,24,128]{2,1,0:T(8,128)S(1)}, f32[33,24,128]{2,1,0:T(8,128)S(1)}, u32[]{:S(2)}, u32[]{:S(2)}) %collective-permute-start.5) | collective-permute-done | bytes 405536 | tf_op jit(solution)/shard_map/ppermute | solution.py:600
  28.8 1.6 %corners_far.1 = (f32[4,2,17,4,8,128]{5,4,3,2,1,0:T(8,128)S(1)}, f32[8,128]{1,0:T(8,128)S(1)}) custom-call(f32[16,32,128]{2,1,0:T(8,128)S(1)} %pad_add_fusion.refs_0_.own.refs_1_, f32[16,32,128]{2,1,0:T(8,128)S(1)} %collective-permute-done.refs_1_.one.refs_2_, f32[16,32,128]{2,1,0:T(8,128)S(1)} %collective-permute-done.1.refs_2_.two.refs_3_, ...), custom_call_target="tpu_custom_call" | custom-call | flops 5000000 | bytes 4000000 | tf_op jit(solution)/shard_map/corners_far/pallas_call | solution.py:279
  30.5 1.2 %collective-permute-done.7.refs_5_ = f32[32,16,128]{2,1,0:T(8,128)S(1)} collective-permute-done((f32[32,16,128]{2,1,0:T(8,128)S(1)}, f32[32,16,128]{2,1,0:T(8,128)S(1)}, u32[]{:S(2)}, u32[]{:S(2)}) %collective-permute-start.7) | collective-permute-done | bytes 262176 | tf_op jit(solution)/shard_map/ppermute | solution.py:600
  31.6 3.6 %iteration.3 = (f32[64,128]{1,0:T(8,128)S(1)}, f32[8,128]{1,0:T(8,128)S(1)}, f32[32,64,128]{2,1,0:T(8,128)S(1)}) custom-call(f32[8,128]{1,0:T(8,128)S(1)} %get-tuple-element.28.refs_0_, f32[16,32,128]{2,1,0:T(8,128)S(1)} %pad_add_fusion.refs_0_.own.refs_1_, f32[16,32,128]{2,1,0:T(8,128)S(1)} %collective-permute-done.refs_1_.one.refs_2_, ...), custom_call_target="tpu_custom_call" | custom-call | flops 20000000 | bytes 9000000 | tf_op jit(solution)/shard_map/iteration/pallas_call | solution.py:553
  35.2 22.4 %all_to_all.33 = f32[64,1,128]{2,1,0:T(1,128)S(1)} all-to-all(f32[64,1,128]{2,1,0:T(1,128)S(1)} %bitcast.18), channel_id=1, replica_groups=mesh['tile'=64,'depth'=4] {'tile'}, dimensions={0} | all-to-all | bytes 65536 | tf_op jit(solution)/shard_map/all_to_all | solution.py:633
  57.6 3.8 %iteration.4 = (f32[64,128]{1,0:T(8,128)S(1)}, f32[8,128]{1,0:T(8,128)S(1)}) custom-call(f32[8,128]{1,0:T(8,128)S(1)} %get-tuple-element.34.refs_0_, f32[64,128]{1,0:T(8,128)S(1)} %bitcast.13, f32[32,64,128]{2,1,0:T(8,128)S(1)} %get-tuple-element.36.refs_2_, f32[6,2,17,4,8,128]{5,4,3,2,1,0:T(8,128)S(1)} %corners_near.1.refs_7_.refs_3_, ...), custom_call_target="tpu_custom_call" | custom-call | flops 20000000 | bytes 9000000 | tf_op jit(solution)/shard_map/iteration/pallas_call | solution.py:553
  61.4 13.3 %all_to_all.34 = f32[64,1,128]{2,1,0:T(1,128)S(1)} all-to-all(f32[64,1,128]{2,1,0:T(1,128)S(1)} %bitcast.20), channel_id=1, replica_groups=mesh['tile'=64,'depth'=4] {'tile'}, dimensions={0} | all-to-all | bytes 65536 | tf_op jit(solution)/shard_map/all_to_all | solution.py:633
  74.7 3.9 %iteration.5 = (f32[64,128]{1,0:T(8,128)S(1)}, f32[8,128]{1,0:T(8,128)S(1)}, f32[8,32,128]{2,1,0:T(8,128)}) custom-call(f32[8,128]{1,0:T(8,128)S(1)} %get-tuple-element.37.refs_0_, f32[64,128]{1,0:T(8,128)S(1)} %bitcast.15, f32[32,64,128]{2,1,0:T(8,128)S(1)} %get-tuple-element.36.refs_2_, f32[6,2,17,4,8,128]{5,4,3,2,1,0:T(8,128)S(1)} %corners_near.1.refs_7_.refs_3_, ...), custom_call_target="tpu_custom_call" | custom-call | flops 20000000 | bytes 9000000 | tf_op jit(solution)/shard_map/iteration/pallas_call | solution.py:553
  78.6 13.3 %all_to_all.35 = f32[64,1,128]{2,1,0:T(1,128)S(1)} all-to-all(f32[64,1,128]{2,1,0:T(1,128)S(1)} %bitcast.19), channel_id=1, replica_groups=mesh['tile'=64,'depth'=4] {'tile'}, dimensions={0} | all-to-all | bytes 65536 | tf_op jit(solution)/shard_map/all_to_all | solution.py:633
  91.9 1.0 %finish.1 = (f32[3,32]{1,0:T(4,128)}, f32[1,3]{1,0:T(1,128)}) custom-call(f32[8,128]{1,0:T(8,128)S(1)} %get-tuple-element.39.motion, f32[64,128]{1,0:T(8,128)S(1)} %bitcast.14, f32[64,128]{1,0:T(8,128)S(1)} %bitcast.16, f32[64,128]{1,0:T(8,128)S(1)} %bitcast.17, f32[32,128]{1,0:T(8,128)S(1)} %get-tuple-element.41.chooser), custom_call_target="tpu_custom_call" | custom-call | tf_op jit(solution)/shard_map/finish/pallas_call | solution.py:582
Async XLA Ops:
  1.6 16.2 %collective-permute-start.2 = (f32[16,32,128]{2,1,0:T(8,128)S(1)}, f32[16,32,128]{2,1,0:T(8,128)S(1)}, u32[]{:S(2)}, u32[]{:S(2)}) collective-permute-start(f32[16,32,128]{2,1,0:T(8,128)S(1)} %pad_add_fusion.refs_0_.own.refs_1_), channel_id=1, source_target_pairs={{3,0},{0,1},{1,2},{2,3},{7,4},{4,5},{5,6},{6,7},{11,8},{8,9},{9,10... | collective-permute-start | bytes 786440 | tf_op jit(solution)/shard_map/ppermute | solution.py:605
  3.8 14.0 %collective-permute-start.1 = (f32[16,32,128]{2,1,0:T(8,128)S(1)}, f32[16,32,128]{2,1,0:T(8,128)S(1)}, u32[]{:S(2)}, u32[]{:S(2)}) collective-permute-start(f32[16,32,128]{2,1,0:T(8,128)S(1)} %pad_add_fusion.refs_0_.own.refs_1_), channel_id=1, source_target_pairs={{2,0},{3,1},{0,2},{1,3},{6,4},{7,5},{4,6},{5,7},{10,8},{11,9},{8,1... | collective-permute-start | bytes 786440 | tf_op jit(solution)/shard_map/ppermute | solution.py:605
  6.4 11.4 %collective-permute-start = (f32[16,32,128]{2,1,0:T(8,128)S(1)}, f32[16,32,128]{2,1,0:T(8,128)S(1)}, u32[]{:S(2)}, u32[]{:S(2)}) collective-permute-start(f32[16,32,128]{2,1,0:T(8,128)S(1)} %pad_add_fusion.refs_0_.own.refs_1_), channel_id=1, source_target_pairs={{1,0},{2,1},{3,2},{0,3},{5,4},{6,5},{7,6},{4,7},{9,8},{10,9},{11,1... | collective-permute-start | bytes 786440 | tf_op jit(solution)/shard_map/ppermute | solution.py:605
  7.5 1.0 %copy-start = (s32[3,8,32,128]{3,2,1,0:T(8,128)S(1)}, s32[3,8,32,128]{3,2,1,0:T(8,128)}, u32[]{:S(2)}) copy-start(s32[3,8,32,128]{3,2,1,0:T(8,128)} %offsets.1) | copy-start | bytes 1179652
  8.5 0.7 copy-start.1
  9.2 0.7 copy-start.2
  10.4 4.8 %collective-permute-start.4 = (f32[8,128]{1,0:T(8,128)S(1)}, f32[8,128]{1,0:T(8,128)S(1)}, u32[]{:S(2)}, u32[]{:S(2)}) collective-permute-start(f32[8,128]{1,0:T(8,128)S(1)} %get-tuple-element.24.refs_4_), channel_id=1, source_target_pairs={{8,0},{12,4},{16,8},{20,12},{24,16},{28,20},{32,24},{36,28},{40,32... | collective-permute-start | bytes 12296 | tf_op jit(solution)/shard_map/ppermute | solution.py:595
  11.7 6.2 %collective-permute-start.3 = (f32[8,128]{1,0:T(8,128)S(1)}, f32[8,128]{1,0:T(8,128)S(1)}, u32[]{:S(2)}, u32[]{:S(2)}) collective-permute-start(f32[8,128]{1,0:T(8,128)S(1)} %get-tuple-element.24.refs_4_), channel_id=1, source_target_pairs={{2,0},{3,1},{0,2},{1,3},{6,4},{7,5},{4,6},{5,7},{10,8},{11,9},{8,1... | collective-permute-start | bytes 12296 | tf_op jit(solution)/shard_map/ppermute | solution.py:605
  18.0 7.2 %collective-permute-start.6 = (f32[33,40,128]{2,1,0:T(8,128)S(1)}, f32[33,40,128]{2,1,0:T(8,128)S(1)}, u32[]{:S(2)}, u32[]{:S(2)}) collective-permute-start(f32[33,40,128]{2,1,0:T(8,128)S(1)} %get-tuple-element.26), channel_id=1, source_target_pairs={{0,4},{8,12},{16,20},{24,28},{32,36},{40,44},{48,52},{56,60},{64,6... | collective-permute-start | bytes 2027528 | tf_op jit(solution)/shard_map/ppermute | solution.py:600
  19.6 9.2 %collective-permute-start.5 = (f32[33,24,128]{2,1,0:T(8,128)S(1)}, f32[33,24,128]{2,1,0:T(8,128)S(1)}, u32[]{:S(2)}, u32[]{:S(2)}) collective-permute-start(f32[33,24,128]{2,1,0:T(8,128)S(1)} %get-tuple-element.25), channel_id=1, source_target_pairs={{4,8},{12,16},{20,24},{28,32},{36,40},{44,48},{52,56},{60,64},{68,... | collective-permute-start | bytes 1216520 | tf_op jit(solution)/shard_map/ppermute | solution.py:600
  23.1 8.6 %collective-permute-start.7 = (f32[32,16,128]{2,1,0:T(8,128)S(1)}, f32[32,16,128]{2,1,0:T(8,128)S(1)}, u32[]{:S(2)}, u32[]{:S(2)}) collective-permute-start(f32[32,16,128]{2,1,0:T(8,128)S(1)} %get-tuple-element.29), channel_id=1, source_target_pairs={{4,8},{12,16},{20,24},{28,32},{36,40},{44,48},{52,56},{60,64},{68,... | collective-permute-start | bytes 786440 | tf_op jit(solution)/shard_map/ppermute | solution.py:600

commit v4 on v3

--- a/solution.py
+++ b/solution.py
@@ -13,6 +13,7 @@
 ROWS = 32
 LANES = 128
 HALO = 24
+REACH = 20
 FRAME = ROWS + 2 * HALO
 GROUPS = FRAME // 8
 LEVENBERG = 0.1 * ELEM**3
@@ -39,6 +40,10 @@
     left = jnp.concatenate(split(left, 3) * len(tables), axis=1)
     right = jnp.concatenate([table for table in tables for _ in range(3)], axis=0)
     return jnp.dot(left, right, preferred_element_type=F32)
+
+
+def aligned(row):
+    return row if isinstance(row, int) else pl.multiple_of(row, 8)
 
 
 def lane_ids(shape):
@@ -129,11 +134,13 @@
     lines, other, beyond, far, far_target, near, extra = refs[4:]
     depth = lax.axis_index("depth")
     odd = lax.rem(lax.axis_index("tile"), 2)
-    far_rows = pl.ds(pl.multiple_of(8 * odd, 8), HALO)
+    far_rows = pl.ds((ROWS - REACH) * odd, REACH)
     near_rows = pl.ds(pl.multiple_of(8 * (1 - odd), 8), HALO)
     for step, piece in enumerate(both):
         planes = pl.ds(lax.rem(depth + step, 4) * 8, 8)
-        far[planes] = piece[0:8, far_rows]
+        for n in range(8):
+            to = pl.ds((lax.rem(depth + step, 4) * 8 + n) * REACH, REACH)
+            far[to] = piece[n, far_rows]
         near[planes, :HALO] = piece[0:8, near_rows]
         far_target[planes] = piece[8:16, pl.ds(pl.multiple_of(ELEM * odd, 8), ELEM)]
         near[planes, HALO:] = piece[8:16, pl.ds(pl.multiple_of(ELEM * (1 - odd), 8), ELEM)]
@@ -144,14 +151,14 @@
     extra[6:12] = jnp.where(upper, mine, given)
     extra[12:13] = lines[6:7]
     extra[13:14] = beyond[6:7]
-    far[SLAB] = extra[...]
+    far[SLAB * REACH :] = extra[0:16]
     near[SLAB, :HALO] = extra[...]
     near[SLAB, HALO:] = jnp.zeros((ELEM, LANES), F32)
 
 
 def pack(*args):
     shapes = (
-        (SLAB + 1, HALO, LANES),
+        (SLAB * REACH + 16, LANES),
         (SLAB, ELEM, LANES),
         (SLAB + 1, HALO + ELEM, LANES),
         (HALO, LANES),
@@ -188,12 +195,17 @@
         motion[...] = jnp.zeros_like(motion)
         motion[1:2] = extra[12:13]
         motion[3:4] = extra[13:14]
-        motion[pl.ds(2 * odd, 1)] = part[SLAB, 12:13]
+        motion[pl.ds(2 * odd, 1)] = part[SLAB * REACH + 12 : SLAB * REACH + 13]
         motion[pl.ds(2 - 2 * odd, 1)] = near[SLAB, 12:13]
     right = odd if is_far else 1 - odd
     base = far_base(odd) if is_far else near_base(odd)
-    rows = pl.ds(pl.multiple_of(8 + (HALO + ROWS) * right, 8), HALO)
-    source[:, rows] = part[0:SLAB, :HALO]
+    if is_far:
+        rows = pl.ds(8 + HALO - REACH + (ROWS + REACH) * right, REACH)
+        for z in range(SLAB):
+            source[z, rows] = part[z * REACH : (z + 1) * REACH]
+    else:
+        rows = pl.ds(pl.multiple_of(8 + (HALO + ROWS) * right, 8), HALO)
+        source[:, rows] = part[0:SLAB, :HALO]
     for step, piece in enumerate((own, one, two, three)):
         start = lax.rem(depth + step, 4) * 8
         source[pl.ds(start, 8), 8 + HALO : 8 + HALO + ROWS] = piece[0:8]
@@ -203,7 +215,11 @@
                 at = e * 6 + c * 2 + which
                 row = (e * 6 + which) * 3 + c
                 table[row + 6 : row + 7] = extra[at : at + 1]
-                table[pl.ds(row + 12 * right, 1)] = part[SLAB, at : at + 1]
+                if is_far:
+                    line = part[SLAB * REACH + at : SLAB * REACH + at + 1]
+                else:
+                    line = part[SLAB, at : at + 1]
+                table[pl.ds(row + 12 * right, 1)] = line
 
     shape = (8, LANES)
     lanes = lane_ids(shape)
@@ -304,39 +320,14 @@
     return motion[...] - step * near
 
 
-def iteration_body(tiles, first, last, *refs):
-    refs = list(refs)
-    motion = refs.pop(0)
-    received = None if first else refs.pop(0)
-    if first:
-        pieces, refs = refs[:6], refs[6:]
-    else:
-        target = refs.pop(0)
-    near_cors, far_cors, along_y, over_y, over_y2, block_out, motion_out = refs[:7]
-    refs = refs[7:]
-    if first:
-        target = refs.pop(0)
-    residual_out = refs.pop(0) if last else None
-    wide, ends, warped, slopes, layers, rows_f, rows_s, padded = refs[:8]
-    residuals = refs[8] if last else None
-
-    tile = lax.axis_index("tile")
-    odd = lax.rem(tile, 2)
-    if first:
-        depth = lax.axis_index("depth")
-        for step, piece in enumerate(pieces[:4]):
-            start = lax.rem(depth + step, 4) * 8
-            target[pl.ds(start, 8), ELEM : ELEM + ROWS] = piece[8:16]
-        far = pl.ds(pl.multiple_of((ELEM + ROWS) * odd, 8), ELEM)
-        near = pl.ds(pl.multiple_of((ELEM + ROWS) * (1 - odd), 8), ELEM)
-        target[:, far] = pieces[4][...]
-        target[:, near] = pieces[5][0:SLAB, HALO:]
-    low_flag = jnp.where(tile > 0, 1.0, 0.0).astype(F32)
-    high_flag = jnp.where(tile < tiles - 1, 1.0, 0.0).astype(F32)
-    now = motion[...] if first else updated_motion(motion, received, tile, tiles, padded)
-    motion_out[...] = now
+def own_lanes():
+    shape = (16, LANES)
+    return (lane_ids(shape) // 8 == row_ids(shape)) & (row_ids(shape) < 12)
+
+
+def warp_image(now, odd, near_cors, far_cors, along_y, wide, ends, warped):
     shape16 = (16, LANES)
-    pick = (lane_ids(shape16) // 8 == row_ids(shape16)) & (row_ids(shape16) < 12)
+    pick = own_lanes()
     spread = jnp.concatenate(
         [jnp.where(pick, jnp.broadcast_to(now[n : n + 1], shape16), 0.0) for n in range(4)], axis=0
     )
@@ -383,6 +374,69 @@
     lax.fori_loop(0, 6, functools.partial(warp, near_cors, near_base(odd)), 0)
     lax.fori_loop(0, 4, functools.partial(warp, far_cors, far_base(odd)), 0)
 
+
+def warp_body(motion, near_cors, far_cors, along_y, warped, wide, ends):
+    odd = lax.rem(lax.axis_index("tile"), 2)
+    warp_image(motion[...], odd, near_cors, far_cors, along_y, wide, ends, warped)
+
+
+def first_warp(motion, cors, along_y):
+    vmem = pl.BlockSpec(memory_space=pltpu.VMEM)
+    return pl.pallas_call(
+        warp_body,
+        out_shape=jax.ShapeDtypeStruct((SLAB + 4, FRAME, LANES), F32),
+        in_specs=[vmem] * 4,
+        out_specs=vmem,
+        scratch_shapes=[
+            pltpu.VMEM((64, LANES), F32),
+            pltpu.VMEM((GROUPS, 6, 8, LANES), F32),
+        ],
+        cost_estimate=pl.CostEstimate(flops=4000000, bytes_accessed=7000000, transcendentals=0),
+        name="warp",
+        compiler_params=pltpu.CompilerParams(vmem_limit_bytes=4 * 2**20),
+    )(motion, *cors, along_y)
+
+
+def iteration_body(tiles, first, last, *refs):
+    refs = list(refs)
+    motion = refs.pop(0)
+    received = None if first else refs.pop(0)
+    if first:
+        pieces, refs = refs[:6], refs[6:]
+    else:
+        target = refs.pop(0)
+    if first:
+        warped = refs.pop(0)
+    else:
+        near_cors, far_cors, refs = refs[0], refs[1], refs[2:]
+    along_y, over_y, over_y2, block_out, motion_out = refs[:5]
+    refs = refs[5:]
+    if first:
+        target = refs.pop(0)
+    residual_out = refs.pop(0) if last else None
+    slopes, layers, rows_f, rows_s, padded = refs[:5]
+    if not first:
+        wide, ends, warped = refs[5:8]
+    residuals = refs[8] if last else None
+
+    tile = lax.axis_index("tile")
+    odd = lax.rem(tile, 2)
+    if first:
+        depth = lax.axis_index("depth")
+        for step, piece in enumerate(pieces[:4]):
+            start = lax.rem(depth + step, 4) * 8
+            target[pl.ds(start, 8), ELEM : ELEM + ROWS] = piece[8:16]
+        far = pl.ds(pl.multiple_of((ELEM + ROWS) * odd, 8), ELEM)
+        near = pl.ds(pl.multiple_of((ELEM + ROWS) * (1 - odd), 8), ELEM)
+        target[:, far] = pieces[4][...]
+        target[:, near] = pieces[5][0:SLAB, HALO:]
+    low_flag = jnp.where(tile > 0, 1.0, 0.0).astype(F32)
+    high_flag = jnp.where(tile < tiles - 1, 1.0, 0.0).astype(F32)
+    now = motion[...] if first else updated_motion(motion, received, tile, tiles, padded)
+    motion_out[...] = now
+    if not first:
+        warp_image(now, odd, near_cors, far_cors, along_y, wide, ends, warped)
+
     shape = (8, LANES)
     lanes = lane_ids(shape)
     ahead_1 = jnp.where(lanes < LANES - 1, 8.0, 0.0)
@@ -392,9 +446,9 @@
     zeros = jnp.zeros(shape, F32)
 
     def slope_group(v, own, misfit):
-        at = pl.ds(pl.multiple_of(8 * v, 8), 8)
-        row = pl.multiple_of(8 * (v - 3), 8)
-        goal = pl.ds(pl.multiple_of(8 * (v - 1), 8), 8)
+        at = pl.ds(aligned(8 * v), 8)
+        row = aligned(8 * (v - 3))
+        goal = pl.ds(aligned(8 * (v - 1)), 8)
         planes = [warped[n, at] for n in range(4)]
         for e in range(2):
             first_sum = [zeros] * 3
@@ -449,9 +503,15 @@
                     layers[v - 1, 6 + 2 * c + 1] += squares_0[c]
         return misfit
 
-    lax.fori_loop(1, 3, lambda v, m: slope_group(v, False, m), zeros)
-    misfit = lax.fori_loop(3, 7, lambda v, m: slope_group(v, True, m), zeros)
-    lax.fori_loop(7, 9, lambda v, m: slope_group(v, False, m), zeros)
+    def two_groups(number, misfit):
+        misfit = slope_group(3 + 2 * number, True, misfit)
+        return slope_group(4 + 2 * number, True, misfit)
+
+    slope_group(1, False, zeros)
+    slope_group(2, False, zeros)
+    misfit = lax.fori_loop(0, 2, two_groups, zeros)
+    slope_group(7, False, zeros)
+    slope_group(8, False, zeros)
 
     if last:
         leaving = pltpu.make_async_copy(
@@ -515,7 +575,7 @@
                     move = [m + g for m, g in zip(move, gain)]
     curvature = jnp.sum(curved) * (1.0 / 144)
     misfit = jnp.sum(misfit)
-    line = jnp.sum(jnp.where(pick, direction[0:16], 0.0), axis=0, keepdims=True)
+    line = jnp.sum(jnp.where(own_lanes(), direction[0:16], 0.0), axis=0, keepdims=True)
     line_lanes = lane_ids((1, LANES))
     for at, value in ((96, descent), (97, length), (98, curvature), (99, misfit)):
         line = jnp.where(line_lanes == at, value, line)
@@ -532,15 +592,18 @@
         jax.ShapeDtypeStruct((8, LANES), F32),
     ]
     scratch = [
-        pltpu.VMEM((64, LANES), F32),
-        pltpu.VMEM((GROUPS, 6, 8, LANES), F32),
-        pltpu.VMEM((SLAB + 4, FRAME, LANES), F32),
         pltpu.VMEM((3, SLAB, ROWS, LANES), F32),
         pltpu.VMEM((8, 12, 8, LANES), F32),
         pltpu.VMEM((24, LANES), F32),
         pltpu.VMEM((24, LANES), F32),
         pltpu.VMEM((tiles + 24, LANES), F32),
     ]
+    if not first:
+        scratch += [
+            pltpu.VMEM((64, LANES), F32),
+            pltpu.VMEM((GROUPS, 6, 8, LANES), F32),
+            pltpu.VMEM((SLAB + 4, FRAME, LANES), F32),
+        ]
     if first:
         shapes.append(jax.ShapeDtypeStruct((SLAB, ROWS + 2 * ELEM, LANES), F32))
     if last:
@@ -621,12 +684,14 @@
     (near_cors,) = corner_images(tiles, False, *both, near, extra)
     far_cors, motion = corner_images(tiles, True, *both, far, near, extra)
     cors = (near_cors, far_cors)
+    warped = first_warp(motion, cors, tables[0])
     target = (*both, far_target, near)
     received = None
     got = []
     for number in range(ITERS):
         first, last = number == 0, number == ITERS - 1
-        outs = iteration(tiles, first, last, motion, received, target, cors, tables)
+        sources = (warped,) if first else cors
+        outs = iteration(tiles, first, last, motion, received, target, sources, tables)
         block, motion = outs[:2]
         if first:
             target = (outs[2],)

time: 93.2 us -> 91.3 us (0.980)
  waiting for transfers between devices: 8.35 us -> 6.55 us
    pallas_call x3, Pallas kernels: 11.2 us -> 9.31 us  [iteration(): pl.pallas_call(functools.partial(iteration_body, tiles, first, last), out...]
    ppermute x3, waiting for transfers between devices: 2.45 us -> 0.64 us  [swap(): return lax.ppermute(block, 'tile', pairs + [(j, i) for i, j in pairs])]
    pallas_call x0 -> x1, Pallas kernels: none -> 1.05 us  [first_warp(): pl.pallas_call(warp_body, out_shape=jax.ShapeDtypeStruct((SLAB + 4, FRAME...]
  transfers between devices with their start and end apart: 8 -> 8, of which waited for: 4 -> 4; matrix products, arithmetic and copies ran while one was open for 0% -> 0% of each run, Pallas kernels for 5% -> 6%
where the time goes in v4:
time: 91.3 us; the launch traced here: 90.9 us
  blocking collectives  49.7 us (54%)
  Pallas kernels  15.9 us (17%)
  starting transfers between devices  14.7 us (16%)
  waiting for transfers between devices  6.55 us (7%)
  local copies, waits for them, and re-layouts  2.36 us (3%)
  other arithmetic  0.99 us (1%)
    all_to_all x3, blocking collectives, local(): received = lax.all_to_all(block, 'tile', 0, 0, tiled=True)  49.7 us
    pallas_call x3, Pallas kernels, iteration(): pl.pallas_call(functools.partial(iteration_body, tiles, first, last), out...  9.31 us
    ppermute x3, starting transfers between devices, swap(): return lax.ppermute(block, 'tile', pairs + [(j, i) for i, j in pairs])  7.18 us
    ppermute x4, starting transfers between devices, ring(): lax.ppermute(block, 'depth', [((i + distance) % peers, i) for i in range(...  6.19 us
    pallas_call x2, Pallas kernels, corner_images(): pl.pallas_call(functools.partial(corner_body, tiles, is_far), out_shape=[...  3.99 us
    ppermute x1, waiting for transfers between devices, from_behind(): lax.ppermute(block, axis, [(i - distance, i) for i in devices if i - dist...  3.23 us
    ppermute x4, waiting for transfers between devices, ring(): lax.ppermute(block, 'depth', [((i + distance) % peers, i) for i in range(...  2.68 us
    unnamed x6, local copies, waits for them, and re-layouts  2.36 us
  transfers between devices with their start and end apart: 8, of which 4 were waited for; matrix products, arithmetic and copies ran while one was open for 0% of the time, Pallas kernels for 6%

profile of v4, /device:TPU:1, one launch (start us, length us, event | category | flops | bytes accessed | tf_op | source)
XLA Modules:
  0.0 90.9 jit_solution(2126581033900872504)
XLA Ops:
  0.6 1.0 %pad_add_fusion.refs_0_.own.refs_1_ = f32[16,32,128]{2,1,0:T(8,128)S(1)} fusion(f32[8,32,128]{2,1,0:T(8,128)} %param.5, f32[8,32,128]{2,1,0:T(8,128)} %param.6), kind=kLoop, calls=%fused_computation | loop fusion | flops 65536 | bytes 524288 | tf_op jit(solution)/shard_map/add | solution.py:675
  1.6 2.2 %collective-permute-start.2 = (f32[16,32,128]{2,1,0:T(8,128)S(1)}, f32[16,32,128]{2,1,0:T(8,128)S(1)}, u32[]{:S(2)}, u32[]{:S(2)}) collective-permute-start(f32[16,32,128]{2,1,0:T(8,128)S(1)} %pad_add_fusion.refs_0_.own.refs_1_), channel_id=1, source_target_pairs={{3,0},{0,1},{1,2},{2,3},{7,4},{4,5},{5,6},{6,7},{11,8},{8,9},{9,10... | collective-permute-start | bytes 786440 | tf_op jit(solution)/shard_map/ppermute | solution.py:668
  3.8 2.6 %collective-permute-start.1 = (f32[16,32,128]{2,1,0:T(8,128)S(1)}, f32[16,32,128]{2,1,0:T(8,128)S(1)}, u32[]{:S(2)}, u32[]{:S(2)}) collective-permute-start(f32[16,32,128]{2,1,0:T(8,128)S(1)} %pad_add_fusion.refs_0_.own.refs_1_), channel_id=1, source_target_pairs={{2,0},{3,1},{0,2},{1,3},{6,4},{7,5},{4,6},{5,7},{10,8},{11,9},{8,1... | collective-permute-start | bytes 786440 | tf_op jit(solution)/shard_map/ppermute | solution.py:668
  6.4 1.1 %collective-permute-start = (f32[16,32,128]{2,1,0:T(8,128)S(1)}, f32[16,32,128]{2,1,0:T(8,128)S(1)}, u32[]{:S(2)}, u32[]{:S(2)}) collective-permute-start(f32[16,32,128]{2,1,0:T(8,128)S(1)} %pad_add_fusion.refs_0_.own.refs_1_), channel_id=1, source_target_pairs={{1,0},{2,1},{3,2},{0,3},{5,4},{6,5},{7,6},{4,7},{9,8},{10,9},{11,1... | collective-permute-start | bytes 786440 | tf_op jit(solution)/shard_map/ppermute | solution.py:668
  7.5 0.0 copy-start
  7.5 1.0 %copy-done = s32[3,8,32,128]{3,2,1,0:T(8,128)S(1)} copy-done((s32[3,8,32,128]{3,2,1,0:T(8,128)S(1)}, s32[3,8,32,128]{3,2,1,0:T(8,128)}, u32[]{:S(2)}) %copy-start) | copy-done | bytes 393240
  8.5 0.0 copy-start.1
  8.5 0.7 copy-done.1
  9.2 0.0 copy-start.2
  9.2 0.7 copy-done.2
  9.9 0.5 prepare.1
  10.4 1.3 %collective-permute-start.4 = (f32[8,128]{1,0:T(8,128)S(1)}, f32[8,128]{1,0:T(8,128)S(1)}, u32[]{:S(2)}, u32[]{:S(2)}) collective-permute-start(f32[8,128]{1,0:T(8,128)S(1)} %get-tuple-element.24.refs_4_), channel_id=1, source_target_pairs={{8,0},{12,4},{16,8},{20,12},{24,16},{28,20},{32,24},{36,28},{40,32... | collective-permute-start | bytes 12296 | tf_op jit(solution)/shard_map/ppermute | solution.py:658
  11.7 0.3 collective-permute-start.3
  12.0 3.2 %collective-permute-done.4.refs_6_ = f32[8,128]{1,0:T(8,128)S(1)} collective-permute-done((f32[8,128]{1,0:T(8,128)S(1)}, f32[8,128]{1,0:T(8,128)S(1)}, u32[]{:S(2)}, u32[]{:S(2)}) %collective-permute-start.4) | collective-permute-done | bytes 4128 | tf_op jit(solution)/shard_map/ppermute | solution.py:658
  15.2 2.7 %collective-permute-done.3.refs_5_ = f32[8,128]{1,0:T(8,128)S(1)} collective-permute-done((f32[8,128]{1,0:T(8,128)S(1)}, f32[8,128]{1,0:T(8,128)S(1)}, u32[]{:S(2)}, u32[]{:S(2)}) %collective-permute-start.3) | collective-permute-done | bytes 4128 | tf_op jit(solution)/shard_map/ppermute | solution.py:668
  17.9 0.0 collective-permute-done.2.refs_3_.three.refs_4_
  17.9 0.0 collective-permute-done.1.refs_2_.two.refs_3_
  17.9 0.0 collective-permute-done.refs_1_.one.refs_2_
  17.9 0.1 pack.1
  18.0 1.6 %collective-permute-start.6 = (f32[33,40,128]{2,1,0:T(8,128)S(1)}, f32[33,40,128]{2,1,0:T(8,128)S(1)}, u32[]{:S(2)}, u32[]{:S(2)}) collective-permute-start(f32[33,40,128]{2,1,0:T(8,128)S(1)} %get-tuple-element.26), channel_id=1, source_target_pairs={{0,4},{8,12},{16,20},{24,28},{32,36},{40,44},{48,52},{56,60},{64,6... | collective-permute-start | bytes 2027528 | tf_op jit(solution)/shard_map/ppermute | solution.py:663
  19.6 3.4 %collective-permute-start.5 = (f32[656,128]{1,0:T(8,128)S(1)}, f32[656,128]{1,0:T(8,128)S(1)}, u32[]{:S(2)}, u32[]{:S(2)}) collective-permute-start(f32[656,128]{1,0:T(8,128)S(1)} %get-tuple-element.25), channel_id=1, source_target_pairs={{4,8},{12,16},{20,24},{28,32},{36,40},{44,48},{52,56},{60,64},{68,... | collective-permute-start | bytes 1007624 | tf_op jit(solution)/shard_map/ppermute | solution.py:663
  23.1 2.1 %collective-permute-start.7 = (f32[32,16,128]{2,1,0:T(8,128)S(1)}, f32[32,16,128]{2,1,0:T(8,128)S(1)}, u32[]{:S(2)}, u32[]{:S(2)}) collective-permute-start(f32[32,16,128]{2,1,0:T(8,128)S(1)} %get-tuple-element.29), channel_id=1, source_target_pairs={{4,8},{12,16},{20,24},{28,32},{36,40},{44,48},{52,56},{60,64},{68,... | collective-permute-start | bytes 786440 | tf_op jit(solution)/shard_map/ppermute | solution.py:663
  25.2 0.0 collective-permute-done.6.refs_0_.part.refs_6_
  25.2 2.4 %corners_near.1.near_cors.refs_3_ = f32[6,2,17,4,8,128]{5,4,3,2,1,0:T(8,128)S(1)} custom-call(f32[16,32,128]{2,1,0:T(8,128)S(1)} %pad_add_fusion.refs_0_.own.refs_1_, f32[16,32,128]{2,1,0:T(8,128)S(1)} %collective-permute-done.refs_1_.one.refs_2_, f32[16,32,128]{2,1,0:T(8,128)S(1)} %collective-permute-done.1.refs_2_.two.refs_3_, ...), custom_call_target="tpu_custom_call" | custom-call | flops 5000000 | bytes 4000000 | tf_op jit(solution)/shard_map/corners_near/pallas_call | solution.py:295
  27.6 0.5 collective-permute-done.5.part
  28.1 1.6 %corners_far.1 = (f32[4,2,17,4,8,128]{5,4,3,2,1,0:T(8,128)S(1)}, f32[8,128]{1,0:T(8,128)S(1)}) custom-call(f32[16,32,128]{2,1,0:T(8,128)S(1)} %pad_add_fusion.refs_0_.own.refs_1_, f32[16,32,128]{2,1,0:T(8,128)S(1)} %collective-permute-done.refs_1_.one.refs_2_, f32[16,32,128]{2,1,0:T(8,128)S(1)} %collective-permute-done.1.refs_2_.two.refs_3_, ...), custom_call_target="tpu_custom_call" | custom-call | flops 5000000 | bytes 4000000 | tf_op jit(solution)/shard_map/corners_far/pallas_call | solution.py:295
  29.7 1.1 %warp.1.refs_7_ = f32[36,80,128]{2,1,0:T(8,128)S(1)} custom-call(f32[8,128]{1,0:T(8,128)S(1)} %get-tuple-element.28.motion.refs_0_, f32[6,2,17,4,8,128]{5,4,3,2,1,0:T(8,128)S(1)} %corners_near.1.near_cors.refs_3_, f32[4,2,17,4,8,128]{5,4,3,2,1,0:T(8,128)S(1)} %get-tuple-element.30.far_cors.refs_4_, bf16[128,128]{1,0:T(8,128)(2,1)S(1)} %get-tuple-element.31.along_y.refs_8_.refs_5_), custom_call_target="tpu_custom_call" | custom-call | flops 4000000 | bytes 7000000 | tf_op jit(solution)/shard_map/warp/pallas_call | solution.py:385
  30.8 0.1 collective-permute-done.7.refs_5_
  30.9 2.2 %iteration.3 = (f32[64,128]{1,0:T(8,128)S(1)}, f32[8,128]{1,0:T(8,128)S(1)}, f32[32,64,128]{2,1,0:T(8,128)S(1)}) custom-call(f32[8,128]{1,0:T(8,128)S(1)} %get-tuple-element.28.motion.refs_0_, f32[16,32,128]{2,1,0:T(8,128)S(1)} %pad_add_fusion.refs_0_.own.refs_1_, f32[16,32,128]{2,1,0:T(8,128)S(1)} %collective-permute-done.refs_1_.one.refs_2_, ...), custom_call_target="tpu_custom_call" | custom-call | flops 20000000 | bytes 9000000 | tf_op jit(solution)/shard_map/iteration/pallas_call | solution.py:616
  33.1 23.1 %all_to_all.33 = f32[64,1,128]{2,1,0:T(1,128)S(1)} all-to-all(f32[64,1,128]{2,1,0:T(1,128)S(1)} %bitcast.18), channel_id=1, replica_groups=mesh['tile'=64,'depth'=4] {'tile'}, dimensions={0} | all-to-all | bytes 65536 | tf_op jit(solution)/shard_map/all_to_all | solution.py:698
  56.3 3.5 %iteration.4 = (f32[64,128]{1,0:T(8,128)S(1)}, f32[8,128]{1,0:T(8,128)S(1)}) custom-call(f32[8,128]{1,0:T(8,128)S(1)} %get-tuple-element.34.refs_0_, f32[64,128]{1,0:T(8,128)S(1)} %bitcast.13, f32[32,64,128]{2,1,0:T(8,128)S(1)} %get-tuple-element.36.refs_2_, f32[6,2,17,4,8,128]{5,4,3,2,1,0:T(8,128)S(1)} %corners_near.1.near_cors.refs_3_, ...), custom_call_target="tpu_custom_call" | custom-call | flops 20000000 | bytes 9000000 | tf_op jit(solution)/shard_map/iteration/pallas_call | solution.py:616
  59.8 13.3 %all_to_all.34 = f32[64,1,128]{2,1,0:T(1,128)S(1)} all-to-all(f32[64,1,128]{2,1,0:T(1,128)S(1)} %bitcast.20), channel_id=1, replica_groups=mesh['tile'=64,'depth'=4] {'tile'}, dimensions={0} | all-to-all | bytes 65536 | tf_op jit(solution)/shard_map/all_to_all | solution.py:698
  73.1 3.6 %iteration.5 = (f32[64,128]{1,0:T(8,128)S(1)}, f32[8,128]{1,0:T(8,128)S(1)}, f32[8,32,128]{2,1,0:T(8,128)}) custom-call(f32[8,128]{1,0:T(8,128)S(1)} %get-tuple-element.37.refs_0_, f32[64,128]{1,0:T(8,128)S(1)} %bitcast.15, f32[32,64,128]{2,1,0:T(8,128)S(1)} %get-tuple-element.36.refs_2_, f32[6,2,17,4,8,128]{5,4,3,2,1,0:T(8,128)S(1)} %corners_near.1.near_cors.refs_3_, ...), custom_call_target="tpu_custom_call" | custom-call | flops 20000000 | bytes 9000000 | tf_op jit(solution)/shard_map/iteration/pallas_call | solution.py:616
  76.7 13.3 %all_to_all.35 = f32[64,1,128]{2,1,0:T(1,128)S(1)} all-to-all(f32[64,1,128]{2,1,0:T(1,128)S(1)} %bitcast.19), channel_id=1, replica_groups=mesh['tile'=64,'depth'=4] {'tile'}, dimensions={0} | all-to-all | bytes 65536 | tf_op jit(solution)/shard_map/all_to_all | solution.py:698
  90.0 1.0 %finish.1 = (f32[3,32]{1,0:T(4,128)}, f32[1,3]{1,0:T(1,128)}) custom-call(f32[8,128]{1,0:T(8,128)S(1)} %get-tuple-element.39.motion, f32[64,128]{1,0:T(8,128)S(1)} %bitcast.14, f32[64,128]{1,0:T(8,128)S(1)} %bitcast.16, f32[64,128]{1,0:T(8,128)S(1)} %bitcast.17, f32[32,128]{1,0:T(8,128)S(1)} %get-tuple-element.41.chooser), custom_call_target="tpu_custom_call" | custom-call | tf_op jit(solution)/shard_map/finish/pallas_call | solution.py:645
Async XLA Ops:
  1.6 16.2 %collective-permute-start.2 = (f32[16,32,128]{2,1,0:T(8,128)S(1)}, f32[16,32,128]{2,1,0:T(8,128)S(1)}, u32[]{:S(2)}, u32[]{:S(2)}) collective-permute-start(f32[16,32,128]{2,1,0:T(8,128)S(1)} %pad_add_fusion.refs_0_.own.refs_1_), channel_id=1, source_target_pairs={{3,0},{0,1},{1,2},{2,3},{7,4},{4,5},{5,6},{6,7},{11,8},{8,9},{9,10... | collective-permute-start | bytes 786440 | tf_op jit(solution)/shard_map/ppermute | solution.py:668
  3.8 14.0 %collective-permute-start.1 = (f32[16,32,128]{2,1,0:T(8,128)S(1)}, f32[16,32,128]{2,1,0:T(8,128)S(1)}, u32[]{:S(2)}, u32[]{:S(2)}) collective-permute-start(f32[16,32,128]{2,1,0:T(8,128)S(1)} %pad_add_fusion.refs_0_.own.refs_1_), channel_id=1, source_target_pairs={{2,0},{3,1},{0,2},{1,3},{6,4},{7,5},{4,6},{5,7},{10,8},{11,9},{8,1... | collective-permute-start | bytes 786440 | tf_op jit(solution)/shard_map/ppermute | solution.py:668
  6.4 11.4 %collective-permute-start = (f32[16,32,128]{2,1,0:T(8,128)S(1)}, f32[16,32,128]{2,1,0:T(8,128)S(1)}, u32[]{:S(2)}, u32[]{:S(2)}) collective-permute-start(f32[16,32,128]{2,1,0:T(8,128)S(1)} %pad_add_fusion.refs_0_.own.refs_1_), channel_id=1, source_target_pairs={{1,0},{2,1},{3,2},{0,3},{5,4},{6,5},{7,6},{4,7},{9,8},{10,9},{11,1... | collective-permute-start | bytes 786440 | tf_op jit(solution)/shard_map/ppermute | solution.py:668
  7.5 1.0 %copy-start = (s32[3,8,32,128]{3,2,1,0:T(8,128)S(1)}, s32[3,8,32,128]{3,2,1,0:T(8,128)}, u32[]{:S(2)}) copy-start(s32[3,8,32,128]{3,2,1,0:T(8,128)} %offsets.1) | copy-start | bytes 1179652
  8.5 0.7 copy-start.1
  9.2 0.7 copy-start.2
  10.4 4.8 %collective-permute-start.4 = (f32[8,128]{1,0:T(8,128)S(1)}, f32[8,128]{1,0:T(8,128)S(1)}, u32[]{:S(2)}, u32[]{:S(2)}) collective-permute-start(f32[8,128]{1,0:T(8,128)S(1)} %get-tuple-element.24.refs_4_), channel_id=1, source_target_pairs={{8,0},{12,4},{16,8},{20,12},{24,16},{28,20},{32,24},{36,28},{40,32... | collective-permute-start | bytes 12296 | tf_op jit(solution)/shard_map/ppermute | solution.py:658
  11.7 6.2 %collective-permute-start.3 = (f32[8,128]{1,0:T(8,128)S(1)}, f32[8,128]{1,0:T(8,128)S(1)}, u32[]{:S(2)}, u32[]{:S(2)}) collective-permute-start(f32[8,128]{1,0:T(8,128)S(1)} %get-tuple-element.24.refs_4_), channel_id=1, source_target_pairs={{2,0},{3,1},{0,2},{1,3},{6,4},{7,5},{4,6},{5,7},{10,8},{11,9},{8,1... | collective-permute-start | bytes 12296 | tf_op jit(solution)/shard_map/ppermute | solution.py:668
  18.0 7.2 %collective-permute-start.6 = (f32[33,40,128]{2,1,0:T(8,128)S(1)}, f32[33,40,128]{2,1,0:T(8,128)S(1)}, u32[]{:S(2)}, u32[]{:S(2)}) collective-permute-start(f32[33,40,128]{2,1,0:T(8,128)S(1)} %get-tuple-element.26), channel_id=1, source_target_pairs={{0,4},{8,12},{16,20},{24,28},{32,36},{40,44},{48,52},{56,60},{64,6... | collective-permute-start | bytes 2027528 | tf_op jit(solution)/shard_map/ppermute | solution.py:663
  19.6 8.5 %collective-permute-start.5 = (f32[656,128]{1,0:T(8,128)S(1)}, f32[656,128]{1,0:T(8,128)S(1)}, u32[]{:S(2)}, u32[]{:S(2)}) collective-permute-start(f32[656,128]{1,0:T(8,128)S(1)} %get-tuple-element.25), channel_id=1, source_target_pairs={{4,8},{12,16},{20,24},{28,32},{36,40},{44,48},{52,56},{60,64},{68,... | collective-permute-start | bytes 1007624 | tf_op jit(solution)/shard_map/ppermute | solution.py:663
  23.1 7.8 %collective-permute-start.7 = (f32[32,16,128]{2,1,0:T(8,128)S(1)}, f32[32,16,128]{2,1,0:T(8,128)S(1)}, u32[]{:S(2)}, u32[]{:S(2)}) collective-permute-start(f32[32,16,128]{2,1,0:T(8,128)S(1)} %get-tuple-element.29), channel_id=1, source_target_pairs={{4,8},{12,16},{20,24},{28,32},{36,40},{44,48},{52,56},{60,64},{68,... | collective-permute-start | bytes 786440 | tf_op jit(solution)/shard_map/ppermute | solution.py:663

commit v5 on v4

--- a/solution.py
+++ b/solution.py
@@ -90,7 +90,8 @@
             ids = jnp.where((group // 6 == k) & (group % 2 == a), wide, ids)
     ids = jnp.where(lanes1 < 96, ids, -1.0)
     chosen = jnp.where(row_ids((32, LANES)).astype(F32) == ids, 1.0, 0.0)
-    chooser[...] = chosen
+    wide = jnp.where(row_ids((LANES, LANES)).astype(F32) == ids, 1.0, 0.0)
+    chooser[...] = wide.T.astype(jnp.bfloat16)
     taken = dot(start_motion[...], chosen)
     component = (lane_ids((3, LANES)) // 16) % 3
     line = jnp.sum(
@@ -110,8 +111,8 @@
 def prepare(offsets, node_ids, start_motion):
     vmem = pl.BlockSpec(memory_space=pltpu.VMEM)
     outside = pl.BlockSpec(memory_space=pltpu.HBM)
-    shapes = [jax.ShapeDtypeStruct((n, LANES), F32) for n in (8, 32)]
-    for size in ((LANES, LANES), (LANES, LANES), (2, LANES, LANES)):
+    shapes = [jax.ShapeDtypeStruct((8, LANES), F32)]
+    for size in ((LANES, LANES),) * 3 + ((2, LANES, LANES),):
         shapes.append(jax.ShapeDtypeStruct(size, jnp.bfloat16))
     return pl.pallas_call(
         prepare_body,
@@ -135,15 +136,14 @@
     depth = lax.axis_index("depth")
     odd = lax.rem(lax.axis_index("tile"), 2)
     far_rows = pl.ds((ROWS - REACH) * odd, REACH)
-    near_rows = pl.ds(pl.multiple_of(8 * (1 - odd), 8), HALO)
+    near_rows = pl.ds((ROWS - REACH) * (1 - odd), REACH)
     for step, piece in enumerate(both):
         planes = pl.ds(lax.rem(depth + step, 4) * 8, 8)
         for n in range(8):
             to = pl.ds((lax.rem(depth + step, 4) * 8 + n) * REACH, REACH)
             far[to] = piece[n, far_rows]
-        near[planes, :HALO] = piece[0:8, near_rows]
+            near[to] = piece[n, near_rows]
         far_target[planes] = piece[8:16, pl.ds(pl.multiple_of(ELEM * odd, 8), ELEM)]
-        near[planes, HALO:] = piece[8:16, pl.ds(pl.multiple_of(ELEM * (1 - odd), 8), ELEM)]
     upper = depth >= 2
     mine, given = lines[0:6], other[0:6]
     extra[...] = jnp.zeros_like(extra)
@@ -152,15 +152,14 @@
     extra[12:13] = lines[6:7]
     extra[13:14] = beyond[6:7]
     far[SLAB * REACH :] = extra[0:16]
-    near[SLAB, :HALO] = extra[...]
-    near[SLAB, HALO:] = jnp.zeros((ELEM, LANES), F32)
+    near[SLAB * REACH :] = extra[0:16]
 
 
 def pack(*args):
     shapes = (
         (SLAB * REACH + 16, LANES),
         (SLAB, ELEM, LANES),
-        (SLAB + 1, HALO + ELEM, LANES),
+        (SLAB * REACH + 16, LANES),
         (HALO, LANES),
     )
     vmem = pl.BlockSpec(memory_space=pltpu.VMEM)
@@ -187,7 +186,7 @@
     if is_far:
         near, extra, chunk, motion, source, shifted, table = refs
     else:
-        extra, chunk, source, shifted, table = refs
+        extra, chunk, near_target, source, shifted, table = refs
     tile = lax.axis_index("tile")
     depth = lax.axis_index("depth")
     odd = lax.rem(tile, 2)
@@ -196,29 +195,25 @@
         motion[1:2] = extra[12:13]
         motion[3:4] = extra[13:14]
         motion[pl.ds(2 * odd, 1)] = part[SLAB * REACH + 12 : SLAB * REACH + 13]
-        motion[pl.ds(2 - 2 * odd, 1)] = near[SLAB, 12:13]
+        motion[pl.ds(2 - 2 * odd, 1)] = near[SLAB * REACH + 12 : SLAB * REACH + 13]
     right = odd if is_far else 1 - odd
     base = far_base(odd) if is_far else near_base(odd)
-    if is_far:
-        rows = pl.ds(8 + HALO - REACH + (ROWS + REACH) * right, REACH)
-        for z in range(SLAB):
-            source[z, rows] = part[z * REACH : (z + 1) * REACH]
-    else:
-        rows = pl.ds(pl.multiple_of(8 + (HALO + ROWS) * right, 8), HALO)
-        source[:, rows] = part[0:SLAB, :HALO]
+    rows = pl.ds(8 + HALO - REACH + (ROWS + REACH) * right, REACH)
+    for z in range(SLAB):
+        source[z, rows] = part[z * REACH : (z + 1) * REACH]
     for step, piece in enumerate((own, one, two, three)):
         start = lax.rem(depth + step, 4) * 8
         source[pl.ds(start, 8), 8 + HALO : 8 + HALO + ROWS] = piece[0:8]
+        if not is_far:
+            edge = pl.ds(pl.multiple_of(ELEM * (1 - odd), 8), ELEM)
+            near_target[pl.ds(start, 8)] = piece[8:16, edge]
     for e in range(2):
         for c in range(3):
             for which in range(2):
                 at = e * 6 + c * 2 + which
                 row = (e * 6 + which) * 3 + c
                 table[row + 6 : row + 7] = extra[at : at + 1]
-                if is_far:
-                    line = part[SLAB * REACH + at : SLAB * REACH + at + 1]
-                else:
-                    line = part[SLAB, at : at + 1]
+                line = part[SLAB * REACH + at : SLAB * REACH + at + 1]
                 table[pl.ds(row + 12 * right, 1)] = line
 
     shape = (8, LANES)
@@ -291,7 +286,8 @@
 
 def corner_images(tiles, is_far, *args):
     vmem = pl.BlockSpec(memory_space=pltpu.VMEM)
-    shapes = [(4 if is_far else 6, 2, 17, 4, 8, LANES)] + ([(8, LANES)] if is_far else [])
+    shapes = [(4 if is_far else 6, 2, 17, 4, 8, LANES)]
+    shapes.append((8, LANES) if is_far else (SLAB, ELEM, LANES))
     return pl.pallas_call(
         functools.partial(corner_body, tiles, is_far),
         out_shape=[jax.ShapeDtypeStruct(shape, F32) for shape in shapes],
@@ -429,7 +425,7 @@
         far = pl.ds(pl.multiple_of((ELEM + ROWS) * odd, 8), ELEM)
         near = pl.ds(pl.multiple_of((ELEM + ROWS) * (1 - odd), 8), ELEM)
         target[:, far] = pieces[4][...]
-        target[:, near] = pieces[5][0:SLAB, HALO:]
+        target[:, near] = pieces[5][...]
     low_flag = jnp.where(tile > 0, 1.0, 0.0).astype(F32)
     high_flag = jnp.where(tile < tiles - 1, 1.0, 0.0).astype(F32)
     now = motion[...] if first else updated_motion(motion, received, tile, tiles, padded)
@@ -631,10 +627,8 @@
     component = (lane_ids(shape) // 16) % 3
     mine = jnp.where(component == row_ids(shape), jnp.broadcast_to(now[1:2], shape), 0.0)
     mine = jnp.where(lane_ids(shape) < 96, mine, 0.0)
-    placed = lax.dot_general(
-        mine, chooser[...], (((1,), (1,)), ((), ())), precision=highest, preferred_element_type=F32
-    )
-    displacement[...] = placed[0:3]
+    placed = exact_dot(mine, [chooser[...]])
+    displacement[...] = placed[0:3, 0:32]
     for n, got in enumerate((got_1, got_2, got_3)):
         total = jnp.sum(got[...], axis=0, keepdims=True)
         misfits[:, n : n + 1] = total[:, 99:100] * (1.0 / VOXELS)
@@ -681,11 +675,12 @@
     far = swap(far, 1)
     near = swap(near, 0)
     far_target = swap(far_target, 1)
-    (near_cors,) = corner_images(tiles, False, *both, near, extra)
+    near_cors, near_target = corner_images(tiles, False, *both, near, extra)
+    near_target = swap(near_target, 0)
     far_cors, motion = corner_images(tiles, True, *both, far, near, extra)
     cors = (near_cors, far_cors)
     warped = first_warp(motion, cors, tables[0])
-    target = (*both, far_target, near)
+    target = (*both, far_target, near_target)
     received = None
     got = []
     for number in range(ITERS):

time: 91.3 us -> 91.3 us (level)
    ppermute x3 -> x4, starting transfers between devices: 7.18 us -> 7.28 us  [swap(): return lax.ppermute(block, 'tile', pairs + [(j, i) for i, j in pairs])]
  transfers between devices with their start and end apart: 8 -> 9, of which waited for: 4 -> 4; matrix products, arithmetic and copies ran while one was open for 0% -> 0% of each run, Pallas kernels for 6% -> 6%
where the time goes in v5:
time: 91.3 us; the launch traced here: 90.9 us
  blocking collectives  49.7 us (54%)
  Pallas kernels  15.9 us (17%)
  starting transfers between devices  14.8 us (16%)
  waiting for transfers between devices  6.47 us (7%)
  local copies, waits for them, and re-layouts  2.36 us (3%)
  other arithmetic  0.99 us (1%)
    all_to_all x3, blocking collectives, local(): received = lax.all_to_all(block, 'tile', 0, 0, tiled=True)  49.7 us
    pallas_call x3, Pallas kernels, iteration(): pl.pallas_call(functools.partial(iteration_body, tiles, first, last), out...  9.31 us
    ppermute x4, starting transfers between devices, swap(): return lax.ppermute(block, 'tile', pairs + [(j, i) for i, j in pairs])  7.28 us
    ppermute x4, starting transfers between devices, ring(): lax.ppermute(block, 'depth', [((i + distance) % peers, i) for i in range(...  6.19 us
    pallas_call x2, Pallas kernels, corner_images(): pl.pallas_call(functools.partial(corner_body, tiles, is_far), out_shape=[...  4 us
    ppermute x1, waiting for transfers between devices, from_behind(): lax.ppermute(block, axis, [(i - distance, i) for i in devices if i - dist...  3.23 us
    ppermute x4, waiting for transfers between devices, ring(): lax.ppermute(block, 'depth', [((i + distance) % peers, i) for i in range(...  2.72 us
    unnamed x6, local copies, waits for them, and re-layouts  2.36 us
  transfers between devices with their start and end apart: 9, of which 4 were waited for; matrix products, arithmetic and copies ran while one was open for 0% of the time, Pallas kernels for 6%

profile of v5, /device:TPU:1, one launch (start us, length us, event | category | flops | bytes accessed | tf_op | source)
XLA Modules:
  0.0 90.9 jit_solution(9568735523661980682)
XLA Ops:
  0.6 1.0 %pad_add_fusion.refs_0_.own.refs_1_ = f32[16,32,128]{2,1,0:T(8,128)S(1)} fusion(f32[8,32,128]{2,1,0:T(8,128)} %param.5, f32[8,32,128]{2,1,0:T(8,128)} %param.6), kind=kLoop, calls=%fused_computation | loop fusion | flops 65536 | bytes 524288 | tf_op jit(solution)/shard_map/add | solution.py:669
  1.6 2.2 %collective-permute-start.2 = (f32[16,32,128]{2,1,0:T(8,128)S(1)}, f32[16,32,128]{2,1,0:T(8,128)S(1)}, u32[]{:S(2)}, u32[]{:S(2)}) collective-permute-start(f32[16,32,128]{2,1,0:T(8,128)S(1)} %pad_add_fusion.refs_0_.own.refs_1_), channel_id=1, source_target_pairs={{3,0},{0,1},{1,2},{2,3},{7,4},{4,5},{5,6},{6,7},{11,8},{8,9},{9,10... | collective-permute-start | bytes 786440 | tf_op jit(solution)/shard_map/ppermute | solution.py:662
  3.8 2.6 %collective-permute-start.1 = (f32[16,32,128]{2,1,0:T(8,128)S(1)}, f32[16,32,128]{2,1,0:T(8,128)S(1)}, u32[]{:S(2)}, u32[]{:S(2)}) collective-permute-start(f32[16,32,128]{2,1,0:T(8,128)S(1)} %pad_add_fusion.refs_0_.own.refs_1_), channel_id=1, source_target_pairs={{2,0},{3,1},{0,2},{1,3},{6,4},{7,5},{4,6},{5,7},{10,8},{11,9},{8,1... | collective-permute-start | bytes 786440 | tf_op jit(solution)/shard_map/ppermute | solution.py:662
  6.4 1.1 %collective-permute-start = (f32[16,32,128]{2,1,0:T(8,128)S(1)}, f32[16,32,128]{2,1,0:T(8,128)S(1)}, u32[]{:S(2)}, u32[]{:S(2)}) collective-permute-start(f32[16,32,128]{2,1,0:T(8,128)S(1)} %pad_add_fusion.refs_0_.own.refs_1_), channel_id=1, source_target_pairs={{1,0},{2,1},{3,2},{0,3},{5,4},{6,5},{7,6},{4,7},{9,8},{10,9},{11,1... | collective-permute-start | bytes 786440 | tf_op jit(solution)/shard_map/ppermute | solution.py:662
  7.5 0.0 copy-start
  7.5 1.0 %copy-done = s32[3,8,32,128]{3,2,1,0:T(8,128)S(1)} copy-done((s32[3,8,32,128]{3,2,1,0:T(8,128)S(1)}, s32[3,8,32,128]{3,2,1,0:T(8,128)}, u32[]{:S(2)}) %copy-start) | copy-done | bytes 393240
  8.5 0.0 copy-start.1
  8.5 0.7 copy-done.1
  9.2 0.0 copy-start.2
  9.2 0.7 copy-done.2
  9.9 0.4 prepare.1
  10.3 1.3 %collective-permute-start.4 = (f32[8,128]{1,0:T(8,128)S(1)}, f32[8,128]{1,0:T(8,128)S(1)}, u32[]{:S(2)}, u32[]{:S(2)}) collective-permute-start(f32[8,128]{1,0:T(8,128)S(1)} %get-tuple-element.26.refs_4_), channel_id=1, source_target_pairs={{8,0},{12,4},{16,8},{20,12},{24,16},{28,20},{32,24},{36,28},{40,32... | collective-permute-start | bytes 12296 | tf_op jit(solution)/shard_map/ppermute | solution.py:652
  11.6 0.3 collective-permute-start.3
  11.9 3.2 %collective-permute-done.4.refs_6_ = f32[8,128]{1,0:T(8,128)S(1)} collective-permute-done((f32[8,128]{1,0:T(8,128)S(1)}, f32[8,128]{1,0:T(8,128)S(1)}, u32[]{:S(2)}, u32[]{:S(2)}) %collective-permute-start.4) | collective-permute-done | bytes 4128 | tf_op jit(solution)/shard_map/ppermute | solution.py:652
  15.1 2.7 %collective-permute-done.3.refs_5_ = f32[8,128]{1,0:T(8,128)S(1)} collective-permute-done((f32[8,128]{1,0:T(8,128)S(1)}, f32[8,128]{1,0:T(8,128)S(1)}, u32[]{:S(2)}, u32[]{:S(2)}) %collective-permute-start.3) | collective-permute-done | bytes 4128 | tf_op jit(solution)/shard_map/ppermute | solution.py:662
  17.9 0.0 collective-permute-done.2.refs_3_.three.refs_4_
  17.9 0.0 collective-permute-done.1.refs_2_.two.refs_3_
  17.9 0.0 collective-permute-done.refs_1_.one.refs_2_
  17.9 0.1 pack.1
  18.0 1.6 %collective-permute-start.6 = (f32[656,128]{1,0:T(8,128)S(1)}, f32[656,128]{1,0:T(8,128)S(1)}, u32[]{:S(2)}, u32[]{:S(2)}) collective-permute-start(f32[656,128]{1,0:T(8,128)S(1)} %get-tuple-element.28), channel_id=1, source_target_pairs={{0,4},{8,12},{16,20},{24,28},{32,36},{40,44},{48,52},{56,60},{64,6... | collective-permute-start | bytes 1007624 | tf_op jit(solution)/shard_map/ppermute | solution.py:657
  19.6 3.4 %collective-permute-start.5 = (f32[656,128]{1,0:T(8,128)S(1)}, f32[656,128]{1,0:T(8,128)S(1)}, u32[]{:S(2)}, u32[]{:S(2)}) collective-permute-start(f32[656,128]{1,0:T(8,128)S(1)} %get-tuple-element.27), channel_id=1, source_target_pairs={{4,8},{12,16},{20,24},{28,32},{36,40},{44,48},{52,56},{60,64},{68,... | collective-permute-start | bytes 1007624 | tf_op jit(solution)/shard_map/ppermute | solution.py:657
  23.1 2.1 %collective-permute-start.7 = (f32[32,16,128]{2,1,0:T(8,128)S(1)}, f32[32,16,128]{2,1,0:T(8,128)S(1)}, u32[]{:S(2)}, u32[]{:S(2)}) collective-permute-start(f32[32,16,128]{2,1,0:T(8,128)S(1)} %get-tuple-element.31), channel_id=1, source_target_pairs={{4,8},{12,16},{20,24},{28,32},{36,40},{44,48},{52,56},{60,64},{68,... | collective-permute-start | bytes 786440 | tf_op jit(solution)/shard_map/ppermute | solution.py:657
  25.2 0.0 collective-permute-done.6.refs_0_.part
  25.2 2.4 %corners_near.1 = (f32[6,2,17,4,8,128]{5,4,3,2,1,0:T(8,128)S(1)}, f32[32,16,128]{2,1,0:T(8,128)S(1)}) custom-call(f32[16,32,128]{2,1,0:T(8,128)S(1)} %pad_add_fusion.refs_0_.own.refs_1_, f32[16,32,128]{2,1,0:T(8,128)S(1)} %collective-permute-done.refs_1_.one.refs_2_, f32[16,32,128]{2,1,0:T(8,128)S(1)} %collective-permute-done.1.refs_2_.two.refs_3_, ...), custom_call_target="tpu_custom_call" | custom-call | flops 5000000 | bytes 4000000 | tf_op jit(solution)/shard_map/corners_near/pallas_call | solution.py:291
  27.6 0.1 collective-permute-start.8
  27.7 0.4 collective-permute-done.5.part
  28.1 1.6 %corners_far.1 = (f32[4,2,17,4,8,128]{5,4,3,2,1,0:T(8,128)S(1)}, f32[8,128]{1,0:T(8,128)S(1)}) custom-call(f32[16,32,128]{2,1,0:T(8,128)S(1)} %pad_add_fusion.refs_0_.own.refs_1_, f32[16,32,128]{2,1,0:T(8,128)S(1)} %collective-permute-done.refs_1_.one.refs_2_, f32[16,32,128]{2,1,0:T(8,128)S(1)} %collective-permute-done.1.refs_2_.two.refs_3_, ...), custom_call_target="tpu_custom_call" | custom-call | flops 5000000 | bytes 4000000 | tf_op jit(solution)/shard_map/corners_far/pallas_call | solution.py:291
  29.7 1.1 %warp.1.refs_7_ = f32[36,80,128]{2,1,0:T(8,128)S(1)} custom-call(f32[8,128]{1,0:T(8,128)S(1)} %get-tuple-element.30.motion.refs_0_, f32[6,2,17,4,8,128]{5,4,3,2,1,0:T(8,128)S(1)} %get-tuple-element.33.near_cors.refs_3_, f32[4,2,17,4,8,128]{5,4,3,2,1,0:T(8,128)S(1)} %get-tuple-element.34.far_cors.refs_4_, ...), custom_call_target="tpu_custom_call" | custom-call | flops 4000000 | bytes 7000000 | tf_op jit(solution)/shard_map/warp/pallas_call | solution.py:381
  30.8 0.1 collective-permute-done.7.refs_5_
  30.9 0.0 collective-permute-done.8.refs_6_
  30.9 2.2 %iteration.3 = (f32[64,128]{1,0:T(8,128)S(1)}, f32[8,128]{1,0:T(8,128)S(1)}, f32[32,64,128]{2,1,0:T(8,128)S(1)}) custom-call(f32[8,128]{1,0:T(8,128)S(1)} %get-tuple-element.30.motion.refs_0_, f32[16,32,128]{2,1,0:T(8,128)S(1)} %pad_add_fusion.refs_0_.own.refs_1_, f32[16,32,128]{2,1,0:T(8,128)S(1)} %collective-permute-done.refs_1_.one.refs_2_, ...), custom_call_target="tpu_custom_call" | custom-call | flops 20000000 | bytes 9000000 | tf_op jit(solution)/shard_map/iteration/pallas_call | solution.py:612
  33.1 23.1 %all_to_all.33 = f32[64,1,128]{2,1,0:T(1,128)S(1)} all-to-all(f32[64,1,128]{2,1,0:T(1,128)S(1)} %bitcast.18), channel_id=1, replica_groups=mesh['tile'=64,'depth'=4] {'tile'}, dimensions={0} | all-to-all | bytes 65536 | tf_op jit(solution)/shard_map/all_to_all | solution.py:693
  56.2 3.5 %iteration.4 = (f32[64,128]{1,0:T(8,128)S(1)}, f32[8,128]{1,0:T(8,128)S(1)}) custom-call(f32[8,128]{1,0:T(8,128)S(1)} %get-tuple-element.38.refs_0_, f32[64,128]{1,0:T(8,128)S(1)} %bitcast.13, f32[32,64,128]{2,1,0:T(8,128)S(1)} %get-tuple-element.40.refs_2_, f32[6,2,17,4,8,128]{5,4,3,2,1,0:T(8,128)S(1)} %get-tuple-element.33.near_cors.refs_3_, ...), custom_call_target="tpu_custom_call" | custom-call | flops 20000000 | bytes 9000000 | tf_op jit(solution)/shard_map/iteration/pallas_call | solution.py:612
  59.7 13.3 %all_to_all.34 = f32[64,1,128]{2,1,0:T(1,128)S(1)} all-to-all(f32[64,1,128]{2,1,0:T(1,128)S(1)} %bitcast.20), channel_id=1, replica_groups=mesh['tile'=64,'depth'=4] {'tile'}, dimensions={0} | all-to-all | bytes 65536 | tf_op jit(solution)/shard_map/all_to_all | solution.py:693
  73.0 3.6 %iteration.5 = (f32[64,128]{1,0:T(8,128)S(1)}, f32[8,128]{1,0:T(8,128)S(1)}, f32[8,32,128]{2,1,0:T(8,128)}) custom-call(f32[8,128]{1,0:T(8,128)S(1)} %get-tuple-element.41.refs_0_, f32[64,128]{1,0:T(8,128)S(1)} %bitcast.15, f32[32,64,128]{2,1,0:T(8,128)S(1)} %get-tuple-element.40.refs_2_, f32[6,2,17,4,8,128]{5,4,3,2,1,0:T(8,128)S(1)} %get-tuple-element.33.near_cors.refs_3_, ...), custom_call_target="tpu_custom_call" | custom-call | flops 20000000 | bytes 9000000 | tf_op jit(solution)/shard_map/iteration/pallas_call | solution.py:612
  76.6 13.3 %all_to_all.35 = f32[64,1,128]{2,1,0:T(1,128)S(1)} all-to-all(f32[64,1,128]{2,1,0:T(1,128)S(1)} %bitcast.19), channel_id=1, replica_groups=mesh['tile'=64,'depth'=4] {'tile'}, dimensions={0} | all-to-all | bytes 65536 | tf_op jit(solution)/shard_map/all_to_all | solution.py:693
  89.9 1.0 %finish.1 = (f32[3,32]{1,0:T(4,128)}, f32[1,3]{1,0:T(1,128)}) custom-call(f32[8,128]{1,0:T(8,128)S(1)} %get-tuple-element.43.motion, f32[64,128]{1,0:T(8,128)S(1)} %bitcast.14, f32[64,128]{1,0:T(8,128)S(1)} %bitcast.16, f32[64,128]{1,0:T(8,128)S(1)} %bitcast.17, bf16[128,128]{1,0:T(8,128)(2,1)S(1)} %get-tuple-element.45.chooser), custom_call_target="tpu_custom_call" | custom-call | tf_op jit(solution)/shard_map/finish/pallas_call | solution.py:639
Async XLA Ops:
  1.6 16.2 %collective-permute-start.2 = (f32[16,32,128]{2,1,0:T(8,128)S(1)}, f32[16,32,128]{2,1,0:T(8,128)S(1)}, u32[]{:S(2)}, u32[]{:S(2)}) collective-permute-start(f32[16,32,128]{2,1,0:T(8,128)S(1)} %pad_add_fusion.refs_0_.own.refs_1_), channel_id=1, source_target_pairs={{3,0},{0,1},{1,2},{2,3},{7,4},{4,5},{5,6},{6,7},{11,8},{8,9},{9,10... | collective-permute-start | bytes 786440 | tf_op jit(solution)/shard_map/ppermute | solution.py:662
  3.8 14.0 %collective-permute-start.1 = (f32[16,32,128]{2,1,0:T(8,128)S(1)}, f32[16,32,128]{2,1,0:T(8,128)S(1)}, u32[]{:S(2)}, u32[]{:S(2)}) collective-permute-start(f32[16,32,128]{2,1,0:T(8,128)S(1)} %pad_add_fusion.refs_0_.own.refs_1_), channel_id=1, source_target_pairs={{2,0},{3,1},{0,2},{1,3},{6,4},{7,5},{4,6},{5,7},{10,8},{11,9},{8,1... | collective-permute-start | bytes 786440 | tf_op jit(solution)/shard_map/ppermute | solution.py:662
  6.4 11.4 %collective-permute-start = (f32[16,32,128]{2,1,0:T(8,128)S(1)}, f32[16,32,128]{2,1,0:T(8,128)S(1)}, u32[]{:S(2)}, u32[]{:S(2)}) collective-permute-start(f32[16,32,128]{2,1,0:T(8,128)S(1)} %pad_add_fusion.refs_0_.own.refs_1_), channel_id=1, source_target_pairs={{1,0},{2,1},{3,2},{0,3},{5,4},{6,5},{7,6},{4,7},{9,8},{10,9},{11,1... | collective-permute-start | bytes 786440 | tf_op jit(solution)/shard_map/ppermute | solution.py:662
  7.5 1.0 %copy-start = (s32[3,8,32,128]{3,2,1,0:T(8,128)S(1)}, s32[3,8,32,128]{3,2,1,0:T(8,128)}, u32[]{:S(2)}) copy-start(s32[3,8,32,128]{3,2,1,0:T(8,128)} %offsets.1) | copy-start | bytes 1179652
  8.5 0.7 copy-start.1
  9.2 0.7 copy-start.2
  10.3 4.8 %collective-permute-start.4 = (f32[8,128]{1,0:T(8,128)S(1)}, f32[8,128]{1,0:T(8,128)S(1)}, u32[]{:S(2)}, u32[]{:S(2)}) collective-permute-start(f32[8,128]{1,0:T(8,128)S(1)} %get-tuple-element.26.refs_4_), channel_id=1, source_target_pairs={{8,0},{12,4},{16,8},{20,12},{24,16},{28,20},{32,24},{36,28},{40,32... | collective-permute-start | bytes 12296 | tf_op jit(solution)/shard_map/ppermute | solution.py:652
  11.6 6.2 %collective-permute-start.3 = (f32[8,128]{1,0:T(8,128)S(1)}, f32[8,128]{1,0:T(8,128)S(1)}, u32[]{:S(2)}, u32[]{:S(2)}) collective-permute-start(f32[8,128]{1,0:T(8,128)S(1)} %get-tuple-element.26.refs_4_), channel_id=1, source_target_pairs={{2,0},{3,1},{0,2},{1,3},{6,4},{7,5},{4,6},{5,7},{10,8},{11,9},{8,1... | collective-permute-start | bytes 12296 | tf_op jit(solution)/shard_map/ppermute | solution.py:662
  18.0 7.2 %collective-permute-start.6 = (f32[656,128]{1,0:T(8,128)S(1)}, f32[656,128]{1,0:T(8,128)S(1)}, u32[]{:S(2)}, u32[]{:S(2)}) collective-permute-start(f32[656,128]{1,0:T(8,128)S(1)} %get-tuple-element.28), channel_id=1, source_target_pairs={{0,4},{8,12},{16,20},{24,28},{32,36},{40,44},{48,52},{56,60},{64,6... | collective-permute-start | bytes 1007624 | tf_op jit(solution)/shard_map/ppermute | solution.py:657
  19.6 8.5 %collective-permute-start.5 = (f32[656,128]{1,0:T(8,128)S(1)}, f32[656,128]{1,0:T(8,128)S(1)}, u32[]{:S(2)}, u32[]{:S(2)}) collective-permute-start(f32[656,128]{1,0:T(8,128)S(1)} %get-tuple-element.27), channel_id=1, source_target_pairs={{4,8},{12,16},{20,24},{28,32},{36,40},{44,48},{52,56},{60,64},{68,... | collective-permute-start | bytes 1007624 | tf_op jit(solution)/shard_map/ppermute | solution.py:657
  23.1 7.8 %collective-permute-start.7 = (f32[32,16,128]{2,1,0:T(8,128)S(1)}, f32[32,16,128]{2,1,0:T(8,128)S(1)}, u32[]{:S(2)}, u32[]{:S(2)}) collective-permute-start(f32[32,16,128]{2,1,0:T(8,128)S(1)} %get-tuple-element.31), channel_id=1, source_target_pairs={{4,8},{12,16},{20,24},{28,32},{36,40},{44,48},{52,56},{60,64},{68,... | collective-permute-start | bytes 786440 | tf_op jit(solution)/shard_map/ppermute | solution.py:657
  27.6 3.3 %collective-permute-start.8 = (f32[32,16,128]{2,1,0:T(8,128)S(1)}, f32[32,16,128]{2,1,0:T(8,128)S(1)}, u32[]{:S(2)}, u32[]{:S(2)}) collective-permute-start(f32[32,16,128]{2,1,0:T(8,128)S(1)} %get-tuple-element.32), channel_id=1, source_target_pairs={{0,4},{8,12},{16,20},{24,28},{32,36},{40,44},{48,52},{56,60},{64,6... | collective-permute-start | bytes 786440 | tf_op jit(solution)/shard_map/ppermute | solution.py:657
